TPU v7x, 32 devices: a whole 2x2x4 slice. The times are simulated.
32 devices in a mesh: group: 2 (over y), tile: 4 (over z), chan: 4 (over x, core).
Axes of the slice: x: 2, y: 2, z: 4, core: 2. Of those that a mesh axis runs over, the one named last changes fastest.
Arguments:
- source: bfloat16 [128, 16384], P('chan', ('group', 'tile')), parts along dimension 1, may hold values from -6 to 6
- send_list: int32 [4, 4, 8], P('tile'), may hold values from 0 to 15, as said below
- block_slot: int32 [512, 6], P('tile'), may hold values from 0 to 31, as said below
- weight_index: int32 [512, 6], P('tile'), may hold values from 0 to 31
- remap_table: bfloat16 [32, 128, 128], replicated, may hold values from -0.21875 to 0.21875
- neighbour_tile: int32 [4, 4], P('tile'), may hold values from 0 to 3, as said below
- neighbour_edge: int32 [4, 4], P('tile'), may hold values from 0 to 7, as said below
- conv_weight: bfloat16 [3, 3, 128, 256], P(None, None, None, 'chan'), may hold values from -0.1875 to 0.1875
Outputs:
- convolved: bfloat16 [256, 1024, 128], P('chan', ('group', 'tile')), parts along dimension 1
There are 2 independent parts, one for each index of `group`. A program takes and returns all parts, laid end to end along the dimension named above; an argument that names none is the same for every part. Nothing has to cross between parts.
Inputs may be any that keep to these rules, and one draw needn't show every extreme that they name: `send_list`: within one band and tile the 8 entries are distinct local block numbers of that band. `block_slot`: A tile reads from a band only the first slots of that band's list to it, at least one; every such slot is read by some row of the tile; every band has some tile, a different one for each band, that reads all 8 slots of that band's list to it. `neighbour_tile`: sides pair up: if side s of tile u borders edge e of tile v, then side e of tile v borders edge s of tile u with the same reversal. `neighbour_edge`: an edge number 0 to 3, plus 4 where the order is reversed; consistent with neighbour_tile as stated there.
All inputs are finite; a program needn't handle non-finite values.
Results may differ from a plain program's by a relative error of at most 0.0049.
Values may be sent and summed in bfloat16 or wider, within the bound.
No kernel may reach another device: no remote copies, remote signals or barrier semaphores. Data moves between devices by JAX's collectives and lax.ppermute only.
A program may use at most 128 MiB of HBM per device.

v0:
```python
import jax
import jax.numpy as jnp
from jax import lax
from jax.sharding import PartitionSpec as P


def convolve(padded, filters):
    result = lax.conv_general_dilated(
        padded[None],
        filters,
        (1, 1),
        "VALID",
        dimension_numbers=("NCHW", "HWIO", "NCHW"),
        preferred_element_type=jnp.float32,
    )
    return result[0]


def body(
    source,
    send_list,
    block_slot,
    weight_index,
    remap_table,
    neighbour_tile,
    neighbour_edge,
    conv_weight,
):
    tile_side = remap_table.shape[1]
    chan_count = source.shape[0]
    tile_count = send_list.shape[1]
    slot_cap = send_list.shape[2]
    band_blocks = source.reshape(chan_count, -1, tile_side)
    every_band = lax.all_gather(band_blocks, "tile", axis=1, tiled=True)
    all_lists = lax.all_gather(send_list, "tile", axis=0, tiled=True)
    my_lists = lax.dynamic_index_in_dim(all_lists, lax.axis_index("tile"), 1, keepdims=False)
    arrived = jnp.take_along_axis(
        every_band.reshape(chan_count, tile_count, -1, tile_side),
        my_lists[None, :, :, None],
        axis=2,
    )
    buffer_rows = arrived.reshape(chan_count, tile_count * slot_cap, tile_side)
    summed = jnp.zeros((chan_count, tile_side, tile_side), jnp.float32)
    for block_k in range(block_slot.shape[1]):
        chosen = jnp.take(buffer_rows, block_slot[:, block_k], axis=1)
        matrices = jnp.take(remap_table, weight_index[:, block_k], axis=0)
        summed = summed + jnp.einsum(
            "crq,rqp->crp", chosen, matrices, preferred_element_type=jnp.float32
        )
    remapped = summed.astype(jnp.bfloat16)
    borders = jnp.stack(
        [remapped[:, 0, :], remapped[:, -1, :], remapped[:, :, 0], remapped[:, :, -1]]
    )[None]
    targets = neighbour_tile[0]
    edge_codes = neighbour_edge[0]
    piece = lax.all_gather(borders, "tile", axis=0, tiled=True)
    owners = jnp.arange(piece.shape[0], dtype=jnp.int32)
    match_tile = owners[None, :] == targets[:, None]
    match_edge = jnp.arange(4, dtype=jnp.int32)[None, :] == (edge_codes % 4)[:, None]
    select = (match_tile[:, :, None] & match_edge[:, None, :]).astype(jnp.bfloat16)
    incoming = jnp.einsum(
        "sme,mecp->scp", select, piece, preferred_element_type=jnp.float32
    ).astype(jnp.bfloat16)
    incoming = jnp.where((edge_codes >= 4)[:, None, None], incoming[:, :, ::-1], incoming)
    padded = jnp.pad(remapped, ((0, 0), (1, 1), (1, 1)))
    padded = padded.at[:, 0, 1:-1].set(incoming[0]).at[:, -1, 1:-1].set(incoming[1])
    padded = padded.at[:, 1:-1, 0].set(incoming[2]).at[:, 1:-1, -1].set(incoming[3])
    parts_count = lax.axis_size("chan")
    strip_rows = tile_side // parts_count
    strips = jnp.stack(
        [
            padded[:, strip_idx * strip_rows : strip_idx * strip_rows + strip_rows + 2, :]
            for strip_idx in range(parts_count)
        ]
    )
    all_channels = lax.all_to_all(strips, "chan", split_axis=0, concat_axis=1, tiled=True)
    all_filters = lax.all_gather(conv_weight, "chan", axis=3, tiled=True)
    strip_out = convolve(all_channels[0], all_filters).astype(jnp.bfloat16)
    return lax.all_to_all(strip_out, "chan", split_axis=0, concat_axis=1, tiled=True)


def solution(mesh):
    in_specs = (
        P("chan", ("group", "tile")),
        P("tile", None, None),
        P("tile", None),
        P("tile", None),
        P(),
        P("tile", None),
        P("tile", None),
        P(None, None, None, "chan"),
    )
    out_specs = P("chan", ("group", "tile"), None)
    return jax.shard_map(body, mesh=mesh, in_specs=in_specs, out_specs=out_specs, check_vma=False)
```

profile of v0, /device:TPU:0, one launch (start us, length us, event | category | flops | bytes accessed | tf_op | source)
XLA Modules:
  0.0 202.9 jit_solution(15934715427704498456)
XLA Ops:
  0.0 0.9 compare_and_fusion.10
  0.9 13.7 %all_gather.12 = s32[4,4,8]{2,1,0:T(4,128)S(1)} all-gather(s32[1,4,8]{2,1,0:T(4,128)} %param.21), channel_id=1, replica_groups=mesh['group'=2,'tile'=4,'chan'=4] {'tile'}, dimensions={0}, use_global_device_ids=true | all-gather | bytes 640 | tf_op jit(solution)/shard_map/all_gather | solution.py:35
  14.6 0.5 broadcast.320
  15.1 0.7 fusion.79
  15.9 0.9 copy_bitcast_fusion
  16.8 15.9 %all_gather.13 = bf16[32,64,128]{2,0,1:T(8,128)(2,1)S(1)} all-gather(bf16[32,16,128]{2,0,1:T(8,128)(2,1)S(1)} %copy_bitcast_fusion), channel_id=1, replica_groups=mesh['group'=2,'tile'=4,'chan'=4] {'tile'}, dimensions={1}, use_global_device_ids=true | all-gather | bytes 655360 | tf_op jit(solution)/shard_map/all_gather | solution.py:34
  32.8 0.9 compare_and_fusion.11
  33.8 0.7 gather_fusion
  34.4 0.1 bitcast_select_fusion
  34.5 1.7 gather_fusion.12
  36.2 0.8 gather_fusion.10
  37.0 3.0 %gather_fusion.11 = bf16[128,128,128]{2,1,0:T(8,128)(2,1)} fusion(bf16[32,128,128]{2,1,0:T(8,128)(2,1)S(1)} %copy-done, s32[1024]{0:T(1024)S(1)} %get-tuple-element.115), kind=kCustom, calls=%fused_computation.6.clone | custom fusion | bytes 8389120 | tf_op jit(solution)/shard_map/jit(_take)/gather | solution.py:46
  40.0 3.1 %gather_fusion.9 = bf16[128,128,128]{2,1,0:T(8,128)(2,1)} fusion(bf16[32,128,128]{2,1,0:T(8,128)(2,1)S(1)} %copy-done, s32[1024]{0:T(1024)S(1)} %get-tuple-element.116), kind=kCustom, calls=%fused_computation.5.clone | custom fusion | bytes 8389120 | tf_op jit(solution)/shard_map/jit(_take)/gather | solution.py:46
  43.1 1.8 gather_fusion.8
  44.9 3.0 %gather_fusion.7 = bf16[128,128,128]{2,1,0:T(8,128)(2,1)} fusion(bf16[32,128,128]{2,1,0:T(8,128)(2,1)S(1)} %copy-done, s32[1024]{0:T(1024)S(1)} %get-tuple-element.117), kind=kCustom, calls=%fused_computation.4.clone | custom fusion | bytes 8389120 | tf_op jit(solution)/shard_map/jit(_take)/gather | solution.py:46
  47.9 1.7 gather_fusion.6
  49.6 3.0 %gather_fusion.5 = bf16[128,128,128]{2,1,0:T(8,128)(2,1)} fusion(bf16[32,128,128]{2,1,0:T(8,128)(2,1)S(1)} %copy-done, s32[1024]{0:T(1024)S(1)} %get-tuple-element.118), kind=kCustom, calls=%fused_computation.3.clone | custom fusion | bytes 8389120 | tf_op jit(solution)/shard_map/jit(_take)/gather | solution.py:46
  52.6 1.7 gather_fusion.4
  54.3 3.1 %gather_fusion.3 = bf16[128,128,128]{2,1,0:T(8,128)(2,1)} fusion(bf16[32,128,128]{2,1,0:T(8,128)(2,1)S(1)} %copy-done, s32[1024]{0:T(1024)S(1)} %get-tuple-element.119), kind=kCustom, calls=%fused_computation.2.clone | custom fusion | bytes 8389120 | tf_op jit(solution)/shard_map/jit(_take)/gather | solution.py:46
  57.4 0.8 gather_fusion.2
  58.2 3.1 %gather_fusion.1 = bf16[128,128,128]{2,1,0:T(8,128)(2,1)} fusion(bf16[32,128,128]{2,1,0:T(8,128)(2,1)S(1)} %copy-done, s32[1024]{0:T(1024)S(1)} %get-tuple-element.120), kind=kCustom, calls=%fused_computation.clone | custom fusion | bytes 8389120 | tf_op jit(solution)/shard_map/jit(_take)/gather | solution.py:46
  61.2 3.9 %fusion = f32[128,128,32]{1,2,0:T(8,128)S(1)} fusion(bf16[128,128,128]{2,1,0:T(8,128)(2,1)} %gather_fusion.11, pred[128]{0:T(512)(128)(4,1)S(1)} %get-tuple-element.109, bf16[128,32,128]{2,1,0:T(8,128)(2,1)} %gather_fusion.12, pred[128]{0:T(512)(128)(4,1)S(1)} %get-tuple-element.99), kind=kOutput, calls=%fused_computation.14 | convolution fusion | flops 136839168 | bytes 7340288 | tf_op jit(solution)/shard_map/crq,rqp->crp/dot_general | solution.py:47
  65.2 1.3 fusion.2
  66.5 0.9 copy-done.4
  67.4 0.3 copy-done.7
  67.7 1.3 fusion.4
  69.0 0.9 copy-done.5
  69.9 0.3 copy-done.8
  70.2 1.3 fusion.6
  71.4 0.9 copy-done.6
  72.3 0.3 copy-done.9
  72.6 1.3 fusion.8
  73.9 0.9 copy-done.2
  74.8 1.8 fusion.27
  76.6 0.4 fusion.80
  77.1 0.2 copy-done.11
  77.3 1.1 copy.77
  78.4 1.1 copy.78
  79.6 13.3 %all-gather = bf16[16,32,128]{2,1,0:T(8,128)(2,1)S(1)} all-gather(bf16[4,32,128]{2,1,0:T(8,128)(2,1)S(1)} %pad_maximum_fusion.1), channel_id=2, replica_groups=mesh['group'=2,'tile'=4,'chan'=4] {'tile'}, dimensions={0}, use_global_device_ids=true | all-gather | bytes 163840 | tf_op jit(solution)/shard_map/all_gather | solution.py:56
  93.0 0.3 convolution_bitcast_fusion
  93.3 0.1 rev.3
  93.5 0.8 pad.20
  94.3 0.6 fusion.81
  95.0 2.4 %copy.81 = bf16[32,128,1]{2,0,1:T(8,128)(2,1)} copy(bf16[32,128,1]{1,0,2:T(8,128)(2,1)S(1)} %get-tuple-element.90) | data formatting | bytes 16384 | tf_op jit(solution)/shard_map/reshape.98
  97.4 1.6 copy.82
  98.9 1.7 scatter.14
  100.6 0.3 scatter.15
  101.0 5.5 %scatter.16 = bf16[32,130,130]{2,0,1:T(8,128)(2,1)S(1)} dynamic-update-slice(bf16[32,130,130]{2,0,1:T(8,128)(2,1)S(1)} %scatter.15, bf16[32,128,1]{2,0,1:T(8,128)(2,1)} %copy.81, s32[]{:T(128)} %constant.174.clone.1, s32[]{:T(128)} %constant.184.clone.1, s32[]{:T(128)} %constant.174.clone.1) | dynamic-update-slice | bytes 16388 | tf_op jit(solution)/shard_map/scatter | solution.py:67
  106.5 12.3 %scatter.19 = bf16[32,130,130]{2,0,1:T(8,128)(2,1)S(1)} dynamic-update-slice(bf16[32,130,130]{2,0,1:T(8,128)(2,1)S(1)} %scatter.16, bf16[32,128,1]{2,0,1:T(8,128)(2,1)S(1)} %copy.82, s32[]{:T(128)} %constant.174.clone.1, s32[]{:T(128)} %constant.184.clone.1, s32[]{:T(128)} %constant.183.clone.1) | dynamic-update-slice | bytes 16388 | tf_op jit(solution)/shard_map/scatter | solution.py:67
  118.9 0.2 slice_bitcast_fusion.4
  119.1 2.0 pad_maximum_fusion
  121.1 3.8 %all-to-all-start = ((bf16[4,32,34,130]{3,1,2,0:T(8,128)(2,1)}), bf16[4,32,34,130]{3,1,2,0:T(8,128)(2,1)S(1)}, u32[]{:S(2)}, u32[]{:S(2)}) async-start(bf16[4,32,34,130]{3,1,2,0:T(8,128)(2,1)} %pad_maximum_fusion), calls=%async_computation | async-start | bytes 4456448 | tf_op jit(solution)/shard_map/all_to_all | solution.py:76
  124.8 31.1 %all_gather.15 = bf16[3,3,128,256]{2,3,1,0:T(8,128)(2,1)S(1)} all-gather(bf16[3,3,128,64]{2,3,1,0:T(8,128)(2,1)S(1)} %copy-done.10), channel_id=1, replica_groups=mesh['group'=2,'tile'=4,'chan'=4] {'chan'}, dimensions={3}, use_global_device_ids=true | all-gather | bytes 737280 | tf_op jit(solution)/shard_map/all_gather | solution.py:77
  155.9 1.7 copy.83
  157.6 5.2 %copy.91 = bf16[128,34,1,130]{0,1,3,2:T(8,128)(2,1)S(1)} copy(bf16[128,34,1,130]{3,0,1,2:T(8,128)(2,1)} %bitcast.121) | data formatting | bytes 2263040
  162.8 0.2 pad.21.clone
  163.1 0.2 copy.86
  163.3 0.2 copy-done.13
  163.5 3.3 %select_convert_fusion = bf16[32,8,17,256]{3,1,2,0:T(8,128)(2,1)S(1)} fusion(pred[8,17]{0,1:T(8,128)(4,1)S(1)} %copy-done.13, bf16[3,3,128,256]{2,3,1,0:T(8,128)(2,1)S(1)} %all_gather.15, bf16[128,34,1,7,2]{0,3,4,1,2:T(8,128)(2,1)S(1)} %slice.246, bf16[128,34,1,8,17]{0,3,4,1,2:T(8,128)(2,1)S(1)} %copy.86), kind=kOutput, calls=%fused_computation.13 | convolution fusion | flops 2573111296 | bytes 4123784 | tf_op jit(solution)/shard_map/conv_general_dilated | solution.py:8
  166.8 0.5 copy.87
  167.4 0.2 slice_bitcast_fusion
  167.5 3.9 %copy.88 = bf16[256,32,128]{2,1,0:T(8,128)(2,1)} copy(bf16[256,32,128]{0,1,2:T(8,128)(2,1)S(1)} %slice_bitcast_fusion) | data formatting | bytes 4194304 | tf_op jit(solution)/shard_map/convert_element_type | solution.py:78
  171.5 29.4 %all_to_all.30 = bf16[256,32,128]{2,1,0:T(8,128)(2,1)S(1)} all-to-all(bf16[256,32,128]{2,1,0:T(8,128)(2,1)} %copy.88), channel_id=1, replica_groups=mesh['group'=2,'tile'=4,'chan'=4] {'chan'}, dimensions={0} | all-to-all | bytes 4194304 | tf_op jit(solution)/shard_map/all_to_all | solution.py:79
  200.9 2.0 copy.89
  (41 shorter events, 0.5 us)
Async XLA Ops:
  0.0 37.0 %copy-start = (bf16[32,128,128]{2,1,0:T(8,128)(2,1)S(1)}, bf16[32,128,128]{2,1,0:T(8,128)(2,1)}, u32[]{:S(2)}) copy-start(bf16[32,128,128]{2,1,0:T(8,128)(2,1)} %param.24) | copy-start | bytes 3145732
  61.2 3.9 %copy-start.3 = (bf16[128,128,128]{2,1,0:T(8,128)(2,1)S(1)}, bf16[128,128,128]{2,1,0:T(8,128)(2,1)}, u32[]{:S(2)}) copy-start(bf16[128,128,128]{2,1,0:T(8,128)(2,1)} %gather_fusion.9) | copy-start | bytes 12582916
  65.2 2.2 %copy-start.4 = (bf16[128,128,128]{2,1,0:T(8,128)(2,1)S(1)}, bf16[128,128,128]{2,1,0:T(8,128)(2,1)}, u32[]{:S(2)}) copy-start(bf16[128,128,128]{2,1,0:T(8,128)(2,1)} %gather_fusion.7) | copy-start | bytes 12582916
  65.2 2.5 %copy-start.7 = (bf16[128,32,128]{2,1,0:T(8,128)(2,1)S(1)}, bf16[128,32,128]{2,1,0:T(8,128)(2,1)}, u32[]{:S(2)}) copy-start(bf16[128,32,128]{2,1,0:T(8,128)(2,1)} %gather_fusion.8) | copy-start | bytes 3145732
  67.7 2.2 %copy-start.5 = (bf16[128,128,128]{2,1,0:T(8,128)(2,1)S(1)}, bf16[128,128,128]{2,1,0:T(8,128)(2,1)}, u32[]{:S(2)}) copy-start(bf16[128,128,128]{2,1,0:T(8,128)(2,1)} %gather_fusion.5) | copy-start | bytes 12582916
  67.7 2.5 %copy-start.8 = (bf16[128,32,128]{2,1,0:T(8,128)(2,1)S(1)}, bf16[128,32,128]{2,1,0:T(8,128)(2,1)}, u32[]{:S(2)}) copy-start(bf16[128,32,128]{2,1,0:T(8,128)(2,1)} %gather_fusion.6) | copy-start | bytes 3145732
  70.2 2.2 %copy-start.6 = (bf16[128,128,128]{2,1,0:T(8,128)(2,1)S(1)}, bf16[128,128,128]{2,1,0:T(8,128)(2,1)}, u32[]{:S(2)}) copy-start(bf16[128,128,128]{2,1,0:T(8,128)(2,1)} %gather_fusion.3) | copy-start | bytes 12582916
  70.2 2.5 %copy-start.9 = (bf16[128,32,128]{2,1,0:T(8,128)(2,1)S(1)}, bf16[128,32,128]{2,1,0:T(8,128)(2,1)}, u32[]{:S(2)}) copy-start(bf16[128,32,128]{2,1,0:T(8,128)(2,1)} %gather_fusion.4) | copy-start | bytes 3145732
  72.6 2.2 %copy-start.2 = (bf16[128,128,128]{2,1,0:T(8,128)(2,1)S(1)}, bf16[128,128,128]{2,1,0:T(8,128)(2,1)}, u32[]{:S(2)}) copy-start(bf16[128,128,128]{2,1,0:T(8,128)(2,1)} %gather_fusion.1) | copy-start | bytes 12582916
  76.6 0.7 copy-start.11
  77.0 15.9 %copy-start.12 = (s32[1,4]{1,0:T(1,128)S(1)}, s32[1,4]{1,0:T(1,128)}, u32[]{:S(2)}) copy-start(s32[1,4]{1,0:T(1,128)} %param.25) | copy-start | bytes 52
  121.1 3.8 %copy-start.10 = (bf16[3,3,128,64]{2,3,1,0:T(8,128)(2,1)S(1)}, bf16[3,3,128,64]{2,3,1,0:T(8,128)(2,1)}, u32[]{:S(2)}) copy-start(bf16[3,3,128,64]{2,3,1,0:T(8,128)(2,1)} %param.27) | copy-start | bytes 442372
  121.1 34.9 %all-to-all-start = ((bf16[4,32,34,130]{3,1,2,0:T(8,128)(2,1)}), bf16[4,32,34,130]{3,1,2,0:T(8,128)(2,1)S(1)}, u32[]{:S(2)}, u32[]{:S(2)}) async-start(bf16[4,32,34,130]{3,1,2,0:T(8,128)(2,1)} %pad_maximum_fusion), calls=%async_computation | async-start | bytes 4456448 | tf_op jit(solution)/shard_map/all_to_all | solution.py:76
  162.8 0.7 copy-start.13
  171.5 31.4 %copy-start.1 = (bf16[32,128,128]{2,1,0:T(8,128)(2,1)S(1)}, bf16[32,128,128]{2,1,0:T(8,128)(2,1)}, u32[]{:S(2)}) copy-start(bf16[32,128,128]{2,1,0:T(8,128)(2,1)} %param.24) | copy-start | bytes 3145732
where the time goes:
time: 204 us; the launch traced here: 203 us
  blocking collectives  103 us (50%)
  local copies, waits for them, and re-layouts  76.7 us (38%)
  matrix products  14.5 us (7%)
  other arithmetic  4.13 us (2%)
  starting transfers between devices  3.75 us (2%)
    all_gather x1, blocking collectives, body(): all_filters = lax.all_gather(conv_weight, 'chan', axis=3, tiled=True)  31.1 us
    all_to_all x1, blocking collectives, body(): lax.all_to_all(strip_out, 'chan', split_axis=0, concat_axis=1, tiled=True)  29.4 us
    gather x6, local copies, waits for them, and re-layouts, body(): matrices = jnp.take(remap_table, weight_index[:, block_k], axis=0)  18.4 us
    scatter x2, local copies, waits for them, and re-layouts, body(): padded.at[:, 1:-1, 0].set(incoming[2]).at[:, 1:-1, -1].set(incoming[3])  17.9 us
    all_gather x1, blocking collectives, body(): every_band = lax.all_gather(band_blocks, 'tile', axis=1, tiled=True)  15.9 us
    all_gather x1, blocking collectives, body(): all_lists = lax.all_gather(send_list, 'tile', axis=0, tiled=True)  13.7 us
    all_gather x1, blocking collectives, body(): piece = lax.all_gather(borders, 'tile', axis=0, tiled=True)  13.3 us
    dot_general x6, matrix products, body(): jnp.einsum('crq,rqp->crp', chosen, matrices, preferred_element_type=jnp.f...  10.9 us
  transfers between devices with their start and end apart: 1, of which 0 were waited for; matrix products, arithmetic and copies ran while one was open for 0% of the time, Pallas kernels for 0%

commit v1 on v0

v1 whole, which is shorter than its diff:
```python
import functools

import jax
import jax.numpy as jnp
from jax import lax
from jax.experimental import pallas as pl
from jax.experimental.pallas import tpu as pltpu
from jax.sharding import PartitionSpec as P

F32 = jnp.float32
BF16 = jnp.bfloat16
VMEM = pl.BlockSpec(memory_space=pltpu.VMEM)
SMEM = pl.BlockSpec(memory_space=pltpu.SMEM)
ANY = pl.BlockSpec(memory_space=pl.ANY)
LIMIT = 48 * 2**20


def round_up(value, step):
    return -(-value // step) * step


def dot(a, b):
    return jnp.dot(a, b, preferred_element_type=F32)


def pack_kernel(side, slots_ref, weights_ref, lists_ref, source_ref, out_ref):
    chans = source_ref.shape[0]
    blocks = source_ref.shape[1] // side
    for block in range(blocks):
        out_ref[block * chans : (block + 1) * chans, :] = source_ref[:, block * side : (block + 1) * side]
    base = blocks * chans
    taps = slots_ref.shape[1]
    tiles, cap = lists_ref.shape[1], lists_ref.shape[2]
    rows = out_ref.shape[0] - base
    wide = jnp.concatenate(
        [slots_ref[...], weights_ref[...], jnp.zeros((side, side - 2 * taps), jnp.int32)], axis=1
    ).astype(F32)
    tables = wide.T[: 2 * taps]
    lists = jnp.concatenate(
        [lists_ref[0].astype(F32), jnp.zeros((tiles, side - cap), F32)], axis=1
    )
    parts = [tables, lists]
    if rows > 2 * taps + tiles:
        parts.append(jnp.zeros((rows - 2 * taps - tiles, side), F32))
    out_ref[base:, :] = jnp.concatenate(parts, axis=0).astype(BF16)


def edge_kernel(
    dims, neigh_ref, codes_ref, gathered_ref, table_ref, out_ref, ints, few_v, few_s, picked, columns, sem
):
    side, chans, blocks, tiles, cap, taps, rows = dims
    count = tiles * cap
    base = blocks * chans
    kinds = table_ref.shape[0]
    me = lax.axis_index("tile")
    for band in range(tiles):
        ints[band * rows : (band + 1) * rows, :] = gathered_ref[band, base:, :].astype(F32).astype(jnp.int32)
    owners = [me] + [neigh_ref[0, s] for s in range(4)]
    for which, owner in enumerate(owners):
        for band in range(tiles):
            few_v[pl.ds(which * tiles + band, 1), :] = ints[pl.ds(band * rows + 2 * taps + owner, 1), :]
    lists_end = 5 * tiles
    for s in range(4):
        for k in range(2 * taps):
            few_v[pl.ds(lists_end + s * 2 * taps + k, 1), :] = ints[pl.ds(owners[s + 1] * rows + k, 1), :]
    copy = pltpu.make_async_copy(few_v, few_s, sem)
    copy.start()
    column_of = lax.broadcasted_iota(jnp.int32, (side, side), 0)
    lane = lax.broadcasted_iota(jnp.int32, (side, side), 1)
    total = jnp.zeros((side, side), F32)
    for kind in range(kinds):
        pick = ((column_of == 0) & (lane == kind)) | ((column_of == side - 1) & (lane == kinds + kind))
        total = total + dot(table_ref[kind], pick.astype(BF16))
    columns[...] = total
    copy.wait()

    def block_of(which, slot):
        band = slot // cap
        local = few_s[which * tiles + band, slot % cap]
        return gathered_ref[band, pl.ds(pl.multiple_of(local * chans, chans), chans), :]

    for slot in range(count):
        out_ref[slot * chans : (slot + 1) * chans, :] = block_of(0, slot)
    per_group = side // kinds
    flip = (lane + column_of == side - 1).astype(BF16)
    for s in range(4):
        code = codes_ref[0, s]
        edge = code % 4
        dest = pl.ds((count + s) * chans, chans)

        @pl.when(edge < 2)
        def _():
            at = jnp.where(edge == 0, 0, side - 1)
            acc = jnp.zeros((chans, side), F32)
            for k in range(taps):
                slot = few_s[lists_end + s * 2 * taps + k, at]
                kind = few_s[lists_end + s * 2 * taps + taps + k, at]
                acc = acc + dot(block_of(1 + s, slot), table_ref[kind])
            out_ref[dest, :] = acc.astype(BF16)

        @pl.when(edge >= 2)
        def _():
            for slot in range(count):
                group, member = slot // per_group, slot % per_group
                picked[group * chans : (group + 1) * chans, member * side : (member + 1) * side] = block_of(1 + s, slot)
            col = columns[...]
            col = jnp.where(edge == 2, col, pltpu.roll(col, side - kinds, 1))
            col = jnp.where(lane < kinds, col, 0.0)
            spread = jnp.concatenate(
                [col if m == 0 else pltpu.roll(col, m * kinds, 1) for m in range(per_group)], axis=0
            ).astype(BF16)
            z = dot(picked[...], spread)
            z_hi = z.astype(BF16)
            z_lo = (z - z_hi.astype(F32)).astype(BF16)
            keys = [
                few_v[pl.ds(lists_end + s * 2 * taps + k, 1), :] * kinds
                + few_v[pl.ds(lists_end + s * 2 * taps + taps + k, 1), :]
                for k in range(taps)
            ]
            acc = jnp.zeros((2 * chans, side), F32)
            for group in range(count // per_group):
                seat = lax.broadcasted_iota(jnp.int32, (side, side), 0) + group * side
                hits = jnp.zeros((side, side), F32)
                for key in keys:
                    hits = hits + jnp.where(seat == key, 1.0, 0.0)
                at = slice(group * chans, (group + 1) * chans)
                acc = acc + dot(jnp.concatenate([z_hi[at], z_lo[at]], axis=0), hits.astype(BF16))
            out_ref[dest, :] = (acc[:chans] + acc[chans:]).astype(BF16)

        @pl.when(code >= 4)
        def _():
            out_ref[dest, :] = dot(out_ref[dest, :], flip).astype(BF16)


def tile_kernel(dims, order, *refs):
    side, chans, tiles, cap, taps, unroll_a, unroll_b = dims
    parts = refs[: len(order)]
    slots_ref, weights_ref, table_ref, filters_ref, out_ref, blocks, image, acc, sems = refs[len(order) :]
    count = tiles * cap
    all_chans = chans * len(order)
    outs = out_ref.shape[0]
    me = lax.axis_index("chan")
    copies = []
    for n, (flip, part) in enumerate(zip(order, parts)):
        off = pl.multiple_of((me ^ flip) * chans, chans)
        copies.append(pltpu.make_async_copy(part, blocks.at[:, pl.ds(off, chans), :], sems.at[n]))
    for copy in copies:
        copy.start()
    for copy in copies:
        copy.wait()

    def remap_row(r):
        lhs = jnp.concatenate([blocks[slots_ref[r, k]] for k in range(taps)], axis=1)
        rhs = jnp.concatenate([table_ref[weights_ref[r, k]] for k in range(taps)], axis=0)
        image[pl.ds(pl.multiple_of((r + 1) * all_chans, all_chans), all_chans), :] = dot(lhs, rhs).astype(BF16)

    def remap_step(t, carry):
        for u in range(unroll_a):
            remap_row(t * unroll_a + u)
        return carry

    lax.fori_loop(0, side // unroll_a, remap_step, 0)
    image[0:all_chans, :] = blocks[count]
    image[(side + 1) * all_chans :, :] = blocks[count + 1]

    lane = lax.broadcasted_iota(jnp.int32, (outs, side), 1)
    wide = lax.broadcasted_iota(jnp.int32, (all_chans, side), 1)

    def shifted(edge):
        value = blocks[count + edge].astype(F32)
        before = jnp.where(wide == 0, 0.0, pltpu.roll(value, 1, 1))
        after = jnp.where(wide == side - 1, 0.0, pltpu.roll(value, side - 1, 1))
        return jnp.concatenate([before, value, after], axis=0).astype(BF16)

    left = dot(filters_ref[0:outs, :], shifted(2))
    right = dot(filters_ref[2 * outs : 3 * outs, :], shifted(3))

    def conv_pair(i):
        x0 = image[pl.ds(pl.multiple_of(i * all_chans, all_chans), 3 * all_chans), :]
        x1 = image[pl.ds(pl.multiple_of((i + 1) * all_chans, all_chans), 3 * all_chans), :]
        y = dot(filters_ref[...], jnp.concatenate([x0, x1], axis=1))
        for h in range(2):
            yy = y[:, h * side : (h + 1) * side]
            from_left = jnp.where(lane == 0, pltpu.roll(left, lax.rem(side - (i + h), side), 1), pltpu.roll(yy[0:outs], 1, 1))
            from_right = jnp.where(
                lane == side - 1, pltpu.roll(right, side - 1 - (i + h), 1), pltpu.roll(yy[2 * outs :], side - 1, 1)
            )
            acc[:, i + h, :] = yy[outs : 2 * outs] + from_left + from_right

    def conv_step(t, carry):
        for u in range(unroll_b):
            conv_pair((t * unroll_b + u) * 2)
        return carry

    lax.fori_loop(0, side // (2 * unroll_b), conv_step, 0)

    def finish(t, carry):
        out_ref[pl.ds(t * 4, 4)] = acc[pl.ds(t * 4, 4)].astype(BF16)
        return carry

    lax.fori_loop(0, outs // 4, finish, 0)


def body(source, send_list, block_slot, weight_index, remap_table, neighbour_tile, neighbour_edge, conv_weight):
    kinds, side = remap_table.shape[:2]
    chans = source.shape[0]
    tiles, cap = send_list.shape[1:]
    taps = block_slot.shape[1]
    blocks = source.shape[1] // side
    count = tiles * cap
    outs = conv_weight.shape[3]
    parts = lax.axis_size("chan")
    rows = round_up(2 * taps + tiles, 16)
    params = pltpu.CompilerParams(vmem_limit_bytes=LIMIT)
    packed = pl.pallas_call(
        functools.partial(pack_kernel, side),
        out_shape=jax.ShapeDtypeStruct((blocks * chans + rows, side), BF16),
        in_specs=[VMEM] * 4,
        out_specs=VMEM,
        compiler_params=params,
        name="pack",
    )(block_slot, weight_index, send_list, source)
    gathered = lax.all_gather(packed, "tile")
    few = 5 * tiles + 4 * 2 * taps
    mine = pl.pallas_call(
        functools.partial(edge_kernel, (side, chans, blocks, tiles, cap, taps, rows)),
        out_shape=jax.ShapeDtypeStruct(((count + 4) * chans, side), BF16),
        in_specs=[SMEM, SMEM, VMEM, VMEM],
        out_specs=VMEM,
        scratch_shapes=[
            pltpu.VMEM((tiles * rows, side), jnp.int32),
            pltpu.VMEM((few, side), jnp.int32),
            pltpu.SMEM((few, side), jnp.int32),
            pltpu.VMEM((count * kinds // side * chans, side * side // kinds), BF16),
            pltpu.VMEM((side, side), F32),
            pltpu.SemaphoreType.DMA,
        ],
        compiler_params=params,
        name="edges",
    )(neighbour_tile, neighbour_edge, gathered, remap_table)

    def swap(value, flip):
        return lax.ppermute(value, "chan", [(i, i ^ flip) for i in range(parts)])

    held = {0: mine}
    bit = parts // 2
    while bit:
        for flip in list(held):
            held[flip ^ bit] = swap(held[flip], bit)
        bit //= 2
    order = tuple(sorted(held))
    filters = conv_weight.transpose(1, 3, 0, 2).reshape(3 * outs, 3 * conv_weight.shape[2])
    all_chans = chans * parts
    return pl.pallas_call(
        functools.partial(tile_kernel, (side, chans, tiles, cap, taps, 16, 8), order),
        out_shape=jax.ShapeDtypeStruct((outs, side, side), BF16),
        in_specs=[ANY] * len(order) + [SMEM, SMEM, VMEM, VMEM],
        out_specs=VMEM,
        scratch_shapes=[
            pltpu.VMEM((count + 4, all_chans, side), BF16),
            pltpu.VMEM(((side + 2) * all_chans, side), BF16),
            pltpu.VMEM((outs, side, side), F32),
            pltpu.SemaphoreType.DMA((len(order),)),
        ],
        compiler_params=params,
        name="tile",
    )(*[held[f].reshape(count + 4, chans, side) for f in order], block_slot, weight_index, remap_table, filters)


def solution(mesh):
    in_specs = (
        P("chan", ("group", "tile")),
        P("tile", None, None),
        P("tile", None),
        P("tile", None),
        P(),
        P("tile", None),
        P("tile", None),
        P(None, None, None, "chan"),
    )
    out_specs = P("chan", ("group", "tile"), None)
    return jax.shard_map(body, mesh=mesh, in_specs=in_specs, out_specs=out_specs, check_vma=False)
```

time: 204 us -> 57.2 us (0.28)
  blocking collectives: 103 us -> 17.5 us
  local copies, waits for them, and re-layouts: 76.7 us -> 5.95 us
  Pallas kernels: 0 us -> 25.4 us
  matrix products: 14.5 us -> 0 us
  waiting for transfers between devices: 0.01 us -> 7.28 us
  other arithmetic: 4.13 us -> 0 us
  starting transfers between devices: 3.75 us -> 1.56 us
    all_gather x4 -> x1, blocking collectives: 74 us -> 17.5 us  [body(): gathered = lax.all_gather(packed, 'tile')]
    all_to_all x1 -> x0, blocking collectives: 29.4 us -> none  [body(): lax.all_to_all(strip_out, 'chan', split_axis=0, concat_axis=1, tiled=True)]
    gather x14 -> x0, local copies, waits for them, and re-layouts: 27.4 us -> none  [the longest x6 18.4 us: body(): matrices = jnp.take(remap_table, weight_index[:, block_k], axis=0)]
    pallas_call x0 -> x3, Pallas kernels: none -> 25.4 us  [the longest x1 19.7 us: body(): pl.pallas_call(functools.partial(tile_kernel, (side, chans, tiles, cap, t...]
    scatter x4 -> x0, local copies, waits for them, and re-layouts: 19.9 us -> none  [the longest x2 17.9 us: body(): padded.at[:, 1:-1, 0].set(incoming[2]).at[:, 1:-1, -1].set(incoming[3])]
    dot_general x7 -> x0, matrix products: 11.2 us -> none  [the longest x6 10.9 us: body(): jnp.einsum('crq,rqp->crp', chosen, matrices, preferred_element_type=jnp.f...]
    ppermute x0 -> x3, waiting for transfers between devices: none -> 7.28 us  [swap(): return lax.ppermute(value, 'chan', [(i, i ^ flip) for i in range(parts)])]
    another operation x7 -> x0, local copies, waits for them, and re-layouts: 4.86 us -> none
  transfers between devices with their start and end apart: 1 -> 3, of which waited for: 0 -> 2; matrix products, arithmetic and copies ran while one was open for 0% -> 0% of each run, Pallas kernels for 0% -> 0%
where the time goes in v1:
time: 57.2 us; the launch traced here: 57.7 us
  Pallas kernels  25.4 us (44%)
  blocking collectives  17.5 us (31%)
  waiting for transfers between devices  7.28 us (13%)
  local copies, waits for them, and re-layouts  5.95 us (10%)
  starting transfers between devices  1.56 us (3%)
    pallas_call x1, Pallas kernels, body(): pl.pallas_call(functools.partial(tile_kernel, (side, chans, tiles, cap, t...  19.7 us
    all_gather x1, blocking collectives, body(): gathered = lax.all_gather(packed, 'tile')  17.5 us
    ppermute x3, waiting for transfers between devices, swap(): return lax.ppermute(value, 'chan', [(i, i ^ flip) for i in range(parts)])  7.28 us
    unnamed x17, local copies, waits for them, and re-layouts  5.82 us
    pallas_call x1, Pallas kernels, body(): pl.pallas_call(functools.partial(edge_kernel, (side, chans, blocks, tiles...  5.5 us
    ppermute x3, starting transfers between devices, swap(): return lax.ppermute(value, 'chan', [(i, i ^ flip) for i in range(parts)])  1.56 us
  transfers between devices with their start and end apart: 3, of which 2 were waited for; matrix products, arithmetic and copies ran while one was open for 0% of the time, Pallas kernels for 0%

profile of v1, /device:TPU:0, one launch (start us, length us, event | category | flops | bytes accessed | tf_op | source)
XLA Modules:
  0.0 57.7 jit_solution(722949010193875207)
XLA Ops:
  0.0 0.0 copy-start.1
  0.0 0.9 %copy.14.slots_ref.refs_4_ = s32[128,6]{1,0:T(8,128)S(1)} copy(s32[128,6]{0,1:T(8,128)} %param.10) | data formatting | bytes 6144 | tf_op args[2]
  0.9 0.8 %copy.15.weights_ref.refs_5_ = s32[128,6]{1,0:T(8,128)S(1)} copy(s32[128,6]{0,1:T(8,128)} %param.11) | data formatting | bytes 6144 | tf_op args[3]
  1.7 0.0 copy-start.2
  1.7 0.9 %copy-done.2 = bf16[32,2048]{1,0:T(8,128)(2,1)S(1)} copy-done((bf16[32,2048]{1,0:T(8,128)(2,1)S(1)}, bf16[32,2048]{1,0:T(8,128)(2,1)}, u32[]{:S(2)}) %copy-start.2) | copy-done | bytes 131096
  2.6 0.0 copy-start.3
  2.6 0.7 %copy-done.3 = s32[1,4,8]{2,1,0:T(4,128)S(1)} copy-done((s32[1,4,8]{2,1,0:T(4,128)S(1)}, s32[1,4,8]{2,1,0:T(4,128)}, u32[]{:S(2)}) %copy-start.3) | copy-done | bytes 152
  3.3 0.0 copy-start.6
  3.3 0.1 pack.1
  3.4 17.5 %all-gather = bf16[2112,128]{1,0:T(8,128)(2,1)S(1)} all-gather(bf16[528,128]{1,0:T(8,128)(2,1)S(1)} %pack.1), channel_id=2, replica_groups=mesh['group'=2,'tile'=4,'chan'=4] {'tile'}, dimensions={0}, use_global_device_ids=true | all-gather | bytes 675840 | tf_op jit(solution)/shard_map/all_gather | solution.py:223
  20.9 0.0 copy-start
  20.9 1.2 %copy-done = bf16[32,128,128]{2,1,0:T(8,128)(2,1)S(1)} copy-done((bf16[32,128,128]{2,1,0:T(8,128)(2,1)S(1)}, bf16[32,128,128]{2,1,0:T(8,128)(2,1)}, u32[]{:S(2)}) %copy-start) | copy-done | bytes 1048600
  22.1 0.0 copy-start.4
  22.1 0.7 %copy-done.4 = s32[1,4]{1,0:T(1,128)S(1)} copy-done((s32[1,4]{1,0:T(1,128)S(1)}, s32[1,4]{1,0:T(1,128)}, u32[]{:S(2)}) %copy-start.4) | copy-done | bytes 40
  22.8 0.0 copy-start.5
  22.8 0.7 %copy-done.5 = s32[1,4]{1,0:T(1,128)S(1)} copy-done((s32[1,4]{1,0:T(1,128)S(1)}, s32[1,4]{1,0:T(1,128)}, u32[]{:S(2)}) %copy-start.5) | copy-done | bytes 40
  23.4 5.5 %edges.1 = bf16[1152,128]{1,0:T(8,128)(2,1)S(1)} custom-call(s32[1,4]{1,0:T(1,128)S(1)} %copy-done.4, s32[1,4]{1,0:T(1,128)S(1)} %copy-done.5, bf16[4,528,128]{2,1,0:T(8,128)(2,1)S(1)} %bitcast.11, bf16[32,128,128]{2,1,0:T(8,128)(2,1)S(1)} %copy-done), custom_call_target="tpu_custom_call" | custom-call | tf_op jit(solution)/shard_map/edges/pallas_call | solution.py:225
  29.0 1.6 %collective-permute-start.1 = (bf16[1152,128]{1,0:T(8,128)(2,1)S(1)}, bf16[1152,128]{1,0:T(8,128)(2,1)S(1)}, u32[]{:S(2)}, u32[]{:S(2)}) collective-permute-start(bf16[1152,128]{1,0:T(8,128)(2,1)S(1)} %edges.1), channel_id=1, source_target_pairs={{0,2},{1,3},{2,0},{3,1},{4,6},{5,7},{6,4},{7,5},{8,10},{9,11},{10,... | collective-permute-start | bytes 884744 | tf_op jit(solution)/shard_map/ppermute | solution.py:243
  30.5 0.0 collective-permute-start
  30.5 5.9 %collective-permute-done.1 = bf16[1152,128]{1,0:T(8,128)(2,1)S(1)} collective-permute-done((bf16[1152,128]{1,0:T(8,128)(2,1)S(1)}, bf16[1152,128]{1,0:T(8,128)(2,1)S(1)}, u32[]{:S(2)}, u32[]{:S(2)}) %collective-permute-start.1) | collective-permute-done | bytes 294944 | tf_op jit(solution)/shard_map/ppermute | solution.py:243
  36.4 0.0 collective-permute-start.2
  36.4 0.0 copy-done.6
  36.4 0.1 copy.16
  36.6 0.0 collective-permute-done
  36.6 1.4 %collective-permute-done.2 = bf16[1152,128]{1,0:T(8,128)(2,1)S(1)} collective-permute-done((bf16[1152,128]{1,0:T(8,128)(2,1)S(1)}, bf16[1152,128]{1,0:T(8,128)(2,1)S(1)}, u32[]{:S(2)}, u32[]{:S(2)}) %collective-permute-start.2) | collective-permute-done | bytes 294944 | tf_op jit(solution)/shard_map/ppermute | solution.py:243
  38.0 0.0 copy-done.1
  38.0 19.7 %tile.1 = bf16[64,128,128]{2,1,0:T(8,128)(2,1)} custom-call(bf16[36,32,128]{2,1,0:T(8,128)(2,1)S(1)} %bitcast.12, bf16[36,32,128]{2,1,0:T(8,128)(2,1)S(1)} %bitcast.15, bf16[36,32,128]{2,1,0:T(8,128)(2,1)S(1)} %bitcast.14, bf16[36,32,128]{2,1,0:T(8,128)(2,1)S(1)} %bitcast.16, s32[128,6]{1,0:T(8,128)S(1)} %copy.14.slots_ref.refs_4_, ...), custom_call_target="tpu_custom_call" | custom-call | tf_op jit(solution)/shard_map/tile/pallas_call | solution.py:254
  (1 shorter events, 0.0 us)
Async XLA Ops:
  0.0 38.0 %copy-start.1 = (bf16[32,128,128]{2,1,0:T(8,128)(2,1)S(1)}, bf16[32,128,128]{2,1,0:T(8,128)(2,1)}, u32[]{:S(2)}) copy-start(bf16[32,128,128]{2,1,0:T(8,128)(2,1)} %refs_6_.1) | copy-start | bytes 3145732
  1.7 0.9 %copy-start.2 = (bf16[32,2048]{1,0:T(8,128)(2,1)S(1)}, bf16[32,2048]{1,0:T(8,128)(2,1)}, u32[]{:S(2)}) copy-start(bf16[32,2048]{1,0:T(8,128)(2,1)} %source_ref.1) | copy-start | bytes 393220
  2.6 0.7 %copy-start.3 = (s32[1,4,8]{2,1,0:T(4,128)S(1)}, s32[1,4,8]{2,1,0:T(4,128)}, u32[]{:S(2)}) copy-start(s32[1,4,8]{2,1,0:T(4,128)} %lists_ref.1) | copy-start | bytes 388
  3.3 33.1 %copy-start.6 = (bf16[3,3,128,64]{2,3,1,0:T(8,128)(2,1)S(1)}, bf16[3,3,128,64]{2,3,1,0:T(8,128)(2,1)}, u32[]{:S(2)}) copy-start(bf16[3,3,128,64]{2,3,1,0:T(8,128)(2,1)} %param.15) | copy-start | bytes 442372
  20.9 1.2 %copy-start = (bf16[32,128,128]{2,1,0:T(8,128)(2,1)S(1)}, bf16[32,128,128]{2,1,0:T(8,128)(2,1)}, u32[]{:S(2)}) copy-start(bf16[32,128,128]{2,1,0:T(8,128)(2,1)} %refs_6_.1) | copy-start | bytes 3145732
  22.1 0.7 %copy-start.4 = (s32[1,4]{1,0:T(1,128)S(1)}, s32[1,4]{1,0:T(1,128)}, u32[]{:S(2)}) copy-start(s32[1,4]{1,0:T(1,128)} %neigh_ref.1) | copy-start | bytes 52
  22.8 0.7 %copy-start.5 = (s32[1,4]{1,0:T(1,128)S(1)}, s32[1,4]{1,0:T(1,128)}, u32[]{:S(2)}) copy-start(s32[1,4]{1,0:T(1,128)} %codes_ref.1) | copy-start | bytes 52
  29.0 7.4 %collective-permute-start.1 = (bf16[1152,128]{1,0:T(8,128)(2,1)S(1)}, bf16[1152,128]{1,0:T(8,128)(2,1)S(1)}, u32[]{:S(2)}, u32[]{:S(2)}) collective-permute-start(bf16[1152,128]{1,0:T(8,128)(2,1)S(1)} %edges.1), channel_id=1, source_target_pairs={{0,2},{1,3},{2,0},{3,1},{4,6},{5,7},{6,4},{7,5},{8,10},{9,11},{10,... | collective-permute-start | bytes 884744 | tf_op jit(solution)/shard_map/ppermute | solution.py:243
  30.5 6.1 %collective-permute-start = (bf16[1152,128]{1,0:T(8,128)(2,1)S(1)}, bf16[1152,128]{1,0:T(8,128)(2,1)S(1)}, u32[]{:S(2)}, u32[]{:S(2)}) collective-permute-start(bf16[1152,128]{1,0:T(8,128)(2,1)S(1)} %edges.1), channel_id=1, source_target_pairs={{0,1},{1,0},{2,3},{3,2},{4,5},{5,4},{6,7},{7,6},{8,9},{9,8},{10,11... | collective-permute-start | bytes 884744 | tf_op jit(solution)/shard_map/ppermute | solution.py:243
  36.4 1.6 %collective-permute-start.2 = (bf16[1152,128]{1,0:T(8,128)(2,1)S(1)}, bf16[1152,128]{1,0:T(8,128)(2,1)S(1)}, u32[]{:S(2)}, u32[]{:S(2)}) collective-permute-start(bf16[1152,128]{1,0:T(8,128)(2,1)S(1)} %collective-permute-done.1), channel_id=1, source_target_pairs={{0,1},{1,0},{2,3},{3,2},{4,5},{5,4},{6,7},{7,6},{8,9},{9,8},{10,11... | collective-permute-start | bytes 884744 | tf_op jit(solution)/shard_map/ppermute | solution.py:243

commit v2 on v1

v2 whole, which is shorter than its diff:
```python
import functools

import jax
import jax.numpy as jnp
from jax import lax
from jax.experimental import pallas as pl
from jax.experimental.pallas import tpu as pltpu
from jax.sharding import PartitionSpec as P

F32 = jnp.float32
BF16 = jnp.bfloat16
VMEM = pl.BlockSpec(memory_space=pltpu.VMEM)
HBM = pl.BlockSpec(memory_space=pltpu.HBM)
LIMIT = 32 * 2**20
STEP = 16


def round_up(value, step):
    return -(-value // step) * step


def dot(a, b):
    return jnp.dot(a, b, preferred_element_type=F32)


def start_all(sems, pairs):
    copies = [pltpu.make_async_copy(src, dst, sems.at[n]) for n, (src, dst) in enumerate(pairs)]
    for copy in copies:
        copy.start()
    return copies


def pack_kernel(slots_hbm, weights_hbm, lists_hbm, source_hbm, table_hbm, out_ref, table_ref, slots, weights, lists, sems):
    side = out_ref.shape[1]
    chans = source_hbm.shape[0]
    blocks = source_hbm.shape[1] // side
    base = blocks * chans
    copies = start_all(
        sems,
        [(slots_hbm, slots), (weights_hbm, weights), (lists_hbm.at[0], lists)]
        + [
            (source_hbm.at[:, pl.ds(block * side, side)], out_ref.at[pl.ds(block * chans, chans), :])
            for block in range(blocks)
        ]
        + [(table_hbm, table_ref)],
    )
    for copy in copies[:3]:
        copy.wait()
    taps = slots.shape[0]
    tiles, cap = lists.shape
    rows = out_ref.shape[0] - base
    wide = jnp.concatenate([lists[...].astype(F32), jnp.zeros((tiles, side - cap), F32)], axis=1)
    parts = [slots[...].astype(F32), weights[...].astype(F32), wide]
    if rows > 2 * taps + tiles:
        parts.append(jnp.zeros((rows - 2 * taps - tiles, side), F32))
    out_ref[base:, :] = jnp.concatenate(parts, axis=0).astype(BF16)
    for copy in copies[3:]:
        copy.wait()


def edge_kernel(
    dims, neigh_hbm, codes_hbm, gathered_ref, table_ref, out_ref,
    neigh, codes, ints, few_v, few_s, picked, columns, sems,
):
    side, chans, blocks, tiles, cap, taps, rows = dims
    count = tiles * cap
    base = blocks * chans
    kinds = table_ref.shape[0]
    per_group = side // kinds
    me = lax.axis_index("tile")
    scalars = start_all(sems, [(neigh_hbm, neigh), (codes_hbm, codes)])
    for band in range(tiles):
        ints[band * rows : (band + 1) * rows, :] = gathered_ref[band, base:, :].astype(F32).astype(jnp.int32)
    for copy in scalars:
        copy.wait()
    owners = [me] + [neigh[0, s] for s in range(4)]
    for which, owner in enumerate(owners):
        for band in range(tiles):
            few_v[pl.ds(which * tiles + band, 1), :] = ints[pl.ds(band * rows + 2 * taps + owner, 1), :]
    lists_end = 5 * tiles
    for s in range(4):
        for k in range(2 * taps):
            few_v[pl.ds(lists_end + s * 2 * taps + k, 1), :] = ints[pl.ds(owners[s + 1] * rows + k, 1), :]
    copy = pltpu.make_async_copy(few_v, few_s, sems.at[2])
    copy.start()
    lane = lax.broadcasted_iota(jnp.int32, (side, side), 1)
    total = jnp.zeros((side, side), F32)
    for kind in range(kinds):
        moved = pltpu.roll(table_ref[kind].astype(F32), per_group * kind + 1, 1)
        total = jnp.where(lane // per_group == kind, moved, total)
    columns[...] = total
    copy.wait()

    def block_of(which, slot):
        band = slot // cap
        local = few_s[which * tiles + band, slot % cap]
        return gathered_ref[band, pl.ds(pl.multiple_of(local * chans, chans), chans), :]

    for slot in range(count):
        out_ref[slot * chans : (slot + 1) * chans, :] = block_of(0, slot)
    for s in range(4):
        edge = codes[0, s] % 4
        dest = pl.ds((count + s) * chans, chans)

        @pl.when(edge < 2)
        def _():
            at = jnp.where(edge == 0, 0, side - 1)
            acc = jnp.zeros((chans, side), F32)
            for k in range(taps):
                slot = few_s[lists_end + s * 2 * taps + k, at]
                kind = few_s[lists_end + s * 2 * taps + taps + k, at]
                acc = acc + dot(block_of(1 + s, slot), table_ref[kind])
            out_ref[dest, :] = acc.astype(BF16)

        @pl.when(edge >= 2)
        def _():
            for slot in range(count):
                group, member = slot // per_group, slot % per_group
                picked[group * chans : (group + 1) * chans, member * side : (member + 1) * side] = block_of(1 + s, slot)
            col = columns[...]
            col = jnp.where(edge == 2, pltpu.roll(col, side - 1, 1), col)
            col = jnp.where(lane % per_group == 0, col, 0.0)
            spread = jnp.concatenate(
                [col if m == 0 else pltpu.roll(col, m, 1) for m in range(per_group)], axis=0
            ).astype(BF16)
            z = dot(picked[...], spread)
            z_hi = z.astype(BF16)
            z_lo = (z - z_hi.astype(F32)).astype(BF16)
            keys = []
            for k in range(taps):
                slot = few_v[pl.ds(lists_end + s * 2 * taps + k, 1), :]
                kind = few_v[pl.ds(lists_end + s * 2 * taps + taps + k, 1), :]
                keys.append(slot // per_group * side + kind * per_group + slot % per_group)
            acc = jnp.zeros((2 * chans, side), F32)
            for group in range(count // per_group):
                seat = lax.broadcasted_iota(jnp.int32, (side, side), 0) + group * side
                hits = jnp.zeros((side, side), F32)
                for key in keys:
                    hits = hits + jnp.where(seat == key, 1.0, 0.0)
                at = slice(group * chans, (group + 1) * chans)
                acc = acc + dot(jnp.concatenate([z_hi[at], z_lo[at]], axis=0), hits.astype(BF16))
            out_ref[dest, :] = (acc[:chans] + acc[chans:]).astype(BF16)

    row = lax.broadcasted_iota(jnp.int32, (side, side), 0)
    flip = (lane + row == side - 1).astype(BF16)
    plain = out_ref[count * chans :, :]
    turned = dot(plain, flip).astype(BF16)
    for s in range(4):
        at = slice(s * chans, (s + 1) * chans)
        out_ref[(count + s) * chans : (count + s + 1) * chans, :] = jnp.where(codes[0, s] >= 4, turned[at], plain[at])


def tile_kernel(dims, last, many, *refs):
    side, chans, cap, tiles, all_chans, outs = dims
    parts = refs[:many]
    refs = refs[many:]
    if last:
        before_ref, *refs = refs
    slots_hbm, weights_hbm, table_ref, filters_hbm, out_ref, slots, weights, filters, matrix, image, *refs = refs
    if last:
        spread, staged, out_sems, sems = refs
    else:
        (sems,) = refs
    taps = slots.shape[0]
    count = tiles * cap
    half = chans * many
    copies = start_all(sems, [(filters_hbm, filters), (slots_hbm, slots), (weights_hbm, weights)])
    me = lax.axis_index("chan")

    def channels(index):
        return jnp.concatenate([part[index] for part in parts], axis=0)

    copies[0].wait()
    lane = lax.broadcasted_iota(jnp.int32, (outs, all_chans), 1)
    for b in range(3):
        low, high = [], []
        for a in range(3):
            value = filters[a, b].astype(F32)
            width = chans
            bit = 1
            while width < all_chans:
                other = jnp.where(
                    lane // width % 2 == 0, pltpu.roll(value, all_chans - width, 1), pltpu.roll(value, width, 1)
                )
                value = jnp.where((me & bit) != 0, other, value)
                width *= 2
                bit *= 2
            turned = pltpu.roll(value, half, 1)
            low.append(turned if last else value)
            high.append(value if last else turned)
        at = slice(b * outs, (b + 1) * outs)
        matrix[at, :all_chans] = jnp.where(lane < half, low[0], high[1]).astype(BF16)
        matrix[at, all_chans:] = low[2][:, :half].astype(BF16)

    image[0:half, :] = channels(count)
    image[(side + 1) * half :, :] = channels(count + 1)
    wide = lax.broadcasted_iota(jnp.int32, (half, side), 1)

    def around(edge):
        value = channels(count + edge).astype(F32)
        before = jnp.where(wide == 0, 0.0, pltpu.roll(value, 1, 1))
        after = jnp.where(wide == side - 1, 0.0, pltpu.roll(value, side - 1, 1))
        return jnp.concatenate([before, value, after], axis=0).astype(BF16)

    left = dot(matrix[0:outs, :], around(2))
    right = dot(matrix[2 * outs :, :], around(3))
    if last:
        left = left + before_ref[side]
        right = right + before_ref[side + 1]
    else:
        out_ref[side] = left
        out_ref[side + 1] = right
    for copy in copies[1:]:
        copy.wait()

    def remap(r):
        lhs = jnp.concatenate([channels(slots[k, r]) for k in range(taps)], axis=1)
        rhs = jnp.concatenate([table_ref[weights[k, r]] for k in range(taps)], axis=0)
        return dot(lhs, rhs).astype(BF16)

    def place(r, value):
        image[pl.ds(pl.multiple_of((r + 1) * half, half), half), :] = value

    lane = lax.broadcasted_iota(jnp.int32, (outs, side), 1)

    def convolve(first):
        ys = []
        for u in range(0, STEP, 2):
            x0 = image[pl.ds(pl.multiple_of((first + u) * half, half), 3 * half), :]
            x1 = image[pl.ds(pl.multiple_of((first + u + 1) * half, half), 3 * half), :]
            ys.append(dot(matrix[...], jnp.concatenate([x0, x1], axis=1)))
        for u in range(STEP):
            i = first + u
            y = ys[u // 2][:, u % 2 * side : (u % 2 + 1) * side]
            at_left = pltpu.roll(left, lax.rem(side - i, side), 1) if last else 0.0
            at_right = pltpu.roll(right, side - 1 - i, 1) if last else 0.0
            from_left = jnp.where(lane == 0, at_left, pltpu.roll(y[:outs], 1, 1))
            from_right = jnp.where(lane == side - 1, at_right, pltpu.roll(y[2 * outs :], side - 1, 1))
            total = y[outs : 2 * outs] + from_left + from_right
            if last:
                spread[:, u, :] = total + before_ref[i]
            else:
                out_ref[i] = total
        if last:
            rows = pl.ds(pl.multiple_of(first, STEP), STEP)
            staged[:, rows, :] = spread[...].astype(BF16)
            pltpu.make_async_copy(staged.at[:, rows, :], out_ref.at[:, rows, :], out_sems.at[first // STEP]).start()

    for r in range(STEP + 1):
        place(r, remap(r))

    def step(t, carry):
        first = t * STEP
        convolve(first)
        for u in range(STEP):
            r = jnp.minimum(first + STEP + 1 + u, side - 1)
            place(r, remap(r))
        return carry

    lax.fori_loop(0, side // STEP - 1, step, 0)
    convolve(side - STEP)
    if last:
        for t in range(side // STEP):
            rows = pl.ds(t * STEP, STEP)
            pltpu.make_async_copy(staged.at[:, rows, :], out_ref.at[:, rows, :], out_sems.at[t]).wait()


def body(source, send_list, block_slot, weight_index, remap_table, neighbour_tile, neighbour_edge, conv_weight):
    kinds, side = remap_table.shape[:2]
    chans = source.shape[0]
    tiles, cap = send_list.shape[1:]
    taps = block_slot.shape[1]
    blocks = source.shape[1] // side
    count = tiles * cap
    all_chans, outs = conv_weight.shape[2:]
    parts = lax.axis_size("chan")
    rows = round_up(2 * taps + tiles, 16)
    params = pltpu.CompilerParams(vmem_limit_bytes=LIMIT)
    slots, weights = block_slot.T, weight_index.T
    filters = conv_weight.transpose(0, 1, 3, 2)
    packed, table = pl.pallas_call(
        pack_kernel,
        out_shape=[
            jax.ShapeDtypeStruct((blocks * chans + rows, side), BF16),
            jax.ShapeDtypeStruct(remap_table.shape, BF16),
        ],
        in_specs=[HBM] * 5,
        out_specs=[VMEM] * 2,
        scratch_shapes=[
            pltpu.VMEM(slots.shape, jnp.int32),
            pltpu.VMEM(weights.shape, jnp.int32),
            pltpu.VMEM((tiles, cap), jnp.int32),
            pltpu.SemaphoreType.DMA((blocks + 4,)),
        ],
        compiler_params=params,
        name="pack",
    )(slots, weights, send_list, source, remap_table)
    gathered = lax.all_gather(packed, "tile")
    few = 5 * tiles + 4 * 2 * taps
    mine = pl.pallas_call(
        functools.partial(edge_kernel, (side, chans, blocks, tiles, cap, taps, rows)),
        out_shape=jax.ShapeDtypeStruct(((count + 4) * chans, side), BF16),
        in_specs=[HBM, HBM, VMEM, VMEM],
        out_specs=VMEM,
        scratch_shapes=[
            pltpu.SMEM(neighbour_tile.shape, jnp.int32),
            pltpu.SMEM(neighbour_edge.shape, jnp.int32),
            pltpu.VMEM((tiles * rows, side), jnp.int32),
            pltpu.VMEM((few, side), jnp.int32),
            pltpu.SMEM((few, side), jnp.int32),
            pltpu.VMEM((count * kinds // side * chans, side * side // kinds), BF16),
            pltpu.VMEM((side, side), F32),
            pltpu.SemaphoreType.DMA((3,)),
        ],
        compiler_params=params,
        name="edges",
    )(neighbour_tile, neighbour_edge, gathered, table)

    def swap(value, flip):
        return lax.ppermute(value, "chan", [(i, i ^ flip) for i in range(parts)])

    held = {0: mine}
    bit = parts // 2
    while bit:
        for flip in list(held):
            held[flip ^ bit] = swap(held[flip], bit)
        bit //= 2
    many = parts // 2
    half = all_chans // 2
    held = [held[f].reshape(count + 4, chans, side) for f in sorted(held)]
    dims = (side, chans, cap, tiles, all_chans, outs)
    scratch = [
        pltpu.SMEM(slots.shape, jnp.int32),
        pltpu.SMEM(weights.shape, jnp.int32),
        pltpu.VMEM(filters.shape, BF16),
        pltpu.VMEM((3 * outs, 3 * half), BF16),
        pltpu.VMEM(((side + 2) * half, side), BF16),
    ]
    flops = 2 * side * half * taps * side * side + 2 * side * side * 9 * half * outs
    cost = pl.CostEstimate(flops=flops, bytes_accessed=(side + 2) * outs * side * 4, transcendentals=0)
    so_far = pl.pallas_call(
        functools.partial(tile_kernel, dims, False, many),
        out_shape=jax.ShapeDtypeStruct((side + 2, outs, side), F32),
        in_specs=[VMEM] * many + [HBM, HBM, VMEM, HBM],
        out_specs=VMEM,
        scratch_shapes=scratch + [pltpu.SemaphoreType.DMA((3,))],
        compiler_params=params,
        cost_estimate=cost,
        name="near",
    )(*held[:many], slots, weights, table, filters)
    return pl.pallas_call(
        functools.partial(tile_kernel, dims, True, many),
        out_shape=jax.ShapeDtypeStruct((outs, side, side), BF16),
        in_specs=[VMEM] * (many + 1) + [HBM, HBM, VMEM, HBM],
        out_specs=HBM,
        scratch_shapes=scratch
        + [
            pltpu.VMEM((outs, STEP, side), F32),
            pltpu.VMEM((outs, side, side), BF16),
            pltpu.SemaphoreType.DMA((side // STEP,)),
            pltpu.SemaphoreType.DMA((3,)),
        ],
        compiler_params=params,
        cost_estimate=cost,
        name="far",
    )(*held[many:], so_far, slots, weights, table, filters)


def solution(mesh):
    in_specs = (
        P("chan", ("group", "tile")),
        P("tile", None, None),
        P("tile", None),
        P("tile", None),
        P(),
        P("tile", None),
        P("tile", None),
        P(None, None, None, "chan"),
    )
    out_specs = P("chan", ("group", "tile"), None)
    return jax.shard_map(body, mesh=mesh, in_specs=in_specs, out_specs=out_specs, check_vma=False)
```

time: 57.2 us -> 56.2 us (0.983); the launches traced: 57.7 us -> 56 us
  waiting for transfers between devices: 7.28 us -> 5.88 us
  Pallas kernels: 25.4 us -> 24.6 us
    pallas_call x1, Pallas kernels: 5.5 us -> 4.09 us  [body(): pl.pallas_call(functools.partial(edge_kernel, (side, chans, blocks, tiles...]
    ppermute x3, waiting for transfers between devices: 7.28 us -> 5.88 us  [swap(): return lax.ppermute(value, 'chan', [(i, i ^ flip) for i in range(parts)])]
    pallas_call x2 -> x3, Pallas kernels: 19.9 us -> 20.5 us  [the longest x1 11.7 us: body(): pl.pallas_call(functools.partial(tile_kernel, dims, True, many), out_shap...]
    unnamed x17 -> x16, local copies, waits for them, and re-layouts: 5.82 us -> 6.4 us
  transfers between devices with their start and end apart: 3 -> 3, of which waited for: 2 -> 1; matrix products, arithmetic and copies ran while one was open for 0% -> 0% of each run, Pallas kernels for 0% -> 15%
where the time goes in v2:
time: 56.2 us; the launch traced here: 56 us
  Pallas kernels  24.6 us (44%)
  blocking collectives  17.5 us (31%)
  local copies, waits for them, and re-layouts  6.4 us (11%)
  waiting for transfers between devices  5.88 us (10%)
  starting transfers between devices  1.56 us (3%)
    all_gather x1, blocking collectives, body(): gathered = lax.all_gather(packed, 'tile')  17.5 us
    pallas_call x1, Pallas kernels, body(): pl.pallas_call(functools.partial(tile_kernel, dims, True, many), out_shap...  11.7 us
    pallas_call x1, Pallas kernels, body(): pl.pallas_call(functools.partial(tile_kernel, dims, False, many), out_sha...  8.48 us
    unnamed x16, local copies, waits for them, and re-layouts  6.4 us
    ppermute x3, waiting for transfers between devices, swap(): return lax.ppermute(value, 'chan', [(i, i ^ flip) for i in range(parts)])  5.88 us
    pallas_call x1, Pallas kernels, body(): pl.pallas_call(functools.partial(edge_kernel, (side, chans, blocks, tiles...  4.09 us
    ppermute x3, starting transfers between devices, swap(): return lax.ppermute(value, 'chan', [(i, i ^ flip) for i in range(parts)])  1.56 us
  transfers between devices with their start and end apart: 3, of which 1 were waited for; matrix products, arithmetic and copies ran while one was open for 0% of the time, Pallas kernels for 15%

profile of v2, /device:TPU:0, one launch (start us, length us, event | category | flops | bytes accessed | tf_op | source)
XLA Modules:
  0.0 56.0 jit_solution(8056230090621967273)
XLA Ops:
  0.0 0.0 copy-start
  0.0 1.2 %copy-done = bf16[32,128,128]{2,1,0:T(8,128)(2,1)S(1)} copy-done((bf16[32,128,128]{2,1,0:T(8,128)(2,1)S(1)}, bf16[32,128,128]{2,1,0:T(8,128)(2,1)}, u32[]{:S(2)}) %copy-start) | copy-done | bytes 1048600
  1.2 0.0 copy-start.1
  1.2 0.9 %copy-done.1 = bf16[32,2048]{1,0:T(8,128)(2,1)S(1)} copy-done((bf16[32,2048]{1,0:T(8,128)(2,1)S(1)}, bf16[32,2048]{1,0:T(8,128)(2,1)}, u32[]{:S(2)}) %copy-start.1) | copy-done | bytes 131096
  2.1 0.0 copy-start.2
  2.1 0.7 %copy-done.2 = s32[128,6]{0,1:T(8,128)S(1)} copy-done((s32[128,6]{0,1:T(8,128)S(1)}, s32[128,6]{0,1:T(8,128)}, u32[]{:S(2)}) %copy-start.2) | copy-done | bytes 3096
  2.8 0.0 copy-start.3
  2.8 0.7 %copy-done.3 = s32[128,6]{0,1:T(8,128)S(1)} copy-done((s32[128,6]{0,1:T(8,128)S(1)}, s32[128,6]{0,1:T(8,128)}, u32[]{:S(2)}) %copy-start.3) | copy-done | bytes 3096
  3.5 0.0 copy-start.4
  3.5 0.7 %copy-done.4 = s32[1,4,8]{2,1,0:T(4,128)S(1)} copy-done((s32[1,4,8]{2,1,0:T(4,128)S(1)}, s32[1,4,8]{2,1,0:T(4,128)}, u32[]{:S(2)}) %copy-start.4) | copy-done | bytes 152
  4.2 0.3 pack.1
  4.5 17.5 %all-gather = bf16[2112,128]{1,0:T(8,128)(2,1)S(1)} all-gather(bf16[528,128]{1,0:T(8,128)(2,1)S(1)} %get-tuple-element.7), channel_id=2, replica_groups=mesh['group'=2,'tile'=4,'chan'=4] {'tile'}, dimensions={0}, use_global_device_ids=true | all-gather | bytes 675840 | tf_op jit(solution)/shard_map/all_gather | solution.py:298
  22.0 0.0 copy-start.5
  22.0 0.7 %copy-done.5 = s32[1,4]{1,0:T(1,128)S(1)} copy-done((s32[1,4]{1,0:T(1,128)S(1)}, s32[1,4]{1,0:T(1,128)}, u32[]{:S(2)}) %copy-start.5) | copy-done | bytes 40
  22.7 0.0 copy-start.6
  22.7 0.7 %copy-done.6 = s32[1,4]{1,0:T(1,128)S(1)} copy-done((s32[1,4]{1,0:T(1,128)S(1)}, s32[1,4]{1,0:T(1,128)}, u32[]{:S(2)}) %copy-start.6) | copy-done | bytes 40
  23.4 4.1 %edges.1 = bf16[1152,128]{1,0:T(8,128)(2,1)S(1)} custom-call(s32[1,4]{1,0:T(1,128)S(1)} %copy-done.5, s32[1,4]{1,0:T(1,128)S(1)} %copy-done.6, bf16[4,528,128]{2,1,0:T(8,128)(2,1)S(1)} %bitcast.8, bf16[32,128,128]{2,1,0:T(8,128)(2,1)S(1)} %get-tuple-element.8.table_ref.refs_4_.refs_5_), custom_call_target="tpu_custom_call" | custom-call | tf_op jit(solution)/shard_map/edges/pallas_call | solution.py:300
  27.4 1.6 %collective-permute-start = (bf16[1152,128]{1,0:T(8,128)(2,1)S(1)}, bf16[1152,128]{1,0:T(8,128)(2,1)S(1)}, u32[]{:S(2)}, u32[]{:S(2)}) collective-permute-start(bf16[1152,128]{1,0:T(8,128)(2,1)S(1)} %edges.1), channel_id=1, source_target_pairs={{0,2},{1,3},{2,0},{3,1},{4,6},{5,7},{6,4},{7,5},{8,10},{9,11},{10,... | collective-permute-start | bytes 884744 | tf_op jit(solution)/shard_map/ppermute | solution.py:320
  29.0 0.0 collective-permute-start.2
  29.0 5.9 %collective-permute-done = bf16[1152,128]{1,0:T(8,128)(2,1)S(1)} collective-permute-done((bf16[1152,128]{1,0:T(8,128)(2,1)S(1)}, bf16[1152,128]{1,0:T(8,128)(2,1)S(1)}, u32[]{:S(2)}, u32[]{:S(2)}) %collective-permute-start) | collective-permute-done | bytes 294944 | tf_op jit(solution)/shard_map/ppermute | solution.py:320
  34.9 0.0 collective-permute-start.1
  34.9 0.0 collective-permute-done.2
  34.9 0.0 copy-start.7
  34.9 0.9 %copy-done.7 = bf16[3,3,128,64]{2,3,1,0:T(8,128)(2,1)S(1)} copy-done((bf16[3,3,128,64]{2,3,1,0:T(8,128)(2,1)S(1)}, bf16[3,3,128,64]{2,3,1,0:T(8,128)(2,1)}, u32[]{:S(2)}) %copy-start.7) | copy-done | bytes 147480
  35.8 8.5 %near.1.refs_2_ = f32[130,64,128]{2,1,0:T(8,128)S(1)} custom-call(bf16[36,32,128]{2,1,0:T(8,128)(2,1)S(1)} %bitcast.9, bf16[36,32,128]{2,1,0:T(8,128)(2,1)S(1)} %bitcast.17, s32[6,128]{1,0:T(8,128)S(1)} %bitcast.11, s32[6,128]{1,0:T(8,128)S(1)} %bitcast.14, bf16[32,128,128]{2,1,0:T(8,128)(2,1)S(1)} %get-tuple-element.8.table_ref.refs_4_.refs_5_, ...), custom_call_target="tpu_custom_call" | custom-call | flops 2818572288 | bytes 4259840 | tf_op jit(solution)/shard_map/near/pallas_call | solution.py:341
  44.3 0.0 collective-permute-done.1
  44.3 11.7 %far.1 = bf16[64,128,128]{2,1,0:T(8,128)(2,1)} custom-call(bf16[36,32,128]{2,1,0:T(8,128)(2,1)S(1)} %bitcast.16, bf16[36,32,128]{2,1,0:T(8,128)(2,1)S(1)} %bitcast.18, f32[130,64,128]{2,1,0:T(8,128)S(1)} %near.1.refs_2_, s32[6,128]{1,0:T(8,128)S(1)} %bitcast.12, s32[6,128]{1,0:T(8,128)S(1)} %bitcast.15, ...), custom_call_target="tpu_custom_call" | custom-call | flops 2818572288 | bytes 4259840 | tf_op jit(solution)/shard_map/far/pallas_call | solution.py:351
Async XLA Ops:
  0.0 1.2 %copy-start = (bf16[32,128,128]{2,1,0:T(8,128)(2,1)S(1)}, bf16[32,128,128]{2,1,0:T(8,128)(2,1)}, u32[]{:S(2)}) copy-start(bf16[32,128,128]{2,1,0:T(8,128)(2,1)} %table_hbm.1) | copy-start | bytes 3145732
  1.2 0.9 %copy-start.1 = (bf16[32,2048]{1,0:T(8,128)(2,1)S(1)}, bf16[32,2048]{1,0:T(8,128)(2,1)}, u32[]{:S(2)}) copy-start(bf16[32,2048]{1,0:T(8,128)(2,1)} %source_hbm.1) | copy-start | bytes 393220
  2.1 0.7 %copy-start.2 = (s32[128,6]{0,1:T(8,128)S(1)}, s32[128,6]{0,1:T(8,128)}, u32[]{:S(2)}) copy-start(s32[128,6]{0,1:T(8,128)} %param.10) | copy-start | bytes 9220
  2.8 0.7 %copy-start.3 = (s32[128,6]{0,1:T(8,128)S(1)}, s32[128,6]{0,1:T(8,128)}, u32[]{:S(2)}) copy-start(s32[128,6]{0,1:T(8,128)} %param.11) | copy-start | bytes 9220
  3.5 0.7 %copy-start.4 = (s32[1,4,8]{2,1,0:T(4,128)S(1)}, s32[1,4,8]{2,1,0:T(4,128)}, u32[]{:S(2)}) copy-start(s32[1,4,8]{2,1,0:T(4,128)} %lists_hbm.1) | copy-start | bytes 388
  22.0 0.7 %copy-start.5 = (s32[1,4]{1,0:T(1,128)S(1)}, s32[1,4]{1,0:T(1,128)}, u32[]{:S(2)}) copy-start(s32[1,4]{1,0:T(1,128)} %neigh_hbm.1) | copy-start | bytes 52
  22.7 0.7 %copy-start.6 = (s32[1,4]{1,0:T(1,128)S(1)}, s32[1,4]{1,0:T(1,128)}, u32[]{:S(2)}) copy-start(s32[1,4]{1,0:T(1,128)} %codes_hbm.1) | copy-start | bytes 52
  27.4 7.4 %collective-permute-start = (bf16[1152,128]{1,0:T(8,128)(2,1)S(1)}, bf16[1152,128]{1,0:T(8,128)(2,1)S(1)}, u32[]{:S(2)}, u32[]{:S(2)}) collective-permute-start(bf16[1152,128]{1,0:T(8,128)(2,1)S(1)} %edges.1), channel_id=1, source_target_pairs={{0,2},{1,3},{2,0},{3,1},{4,6},{5,7},{6,4},{7,5},{8,10},{9,11},{10,... | collective-permute-start | bytes 884744 | tf_op jit(solution)/shard_map/ppermute | solution.py:320
  29.0 5.9 %collective-permute-start.2 = (bf16[1152,128]{1,0:T(8,128)(2,1)S(1)}, bf16[1152,128]{1,0:T(8,128)(2,1)S(1)}, u32[]{:S(2)}, u32[]{:S(2)}) collective-permute-start(bf16[1152,128]{1,0:T(8,128)(2,1)S(1)} %edges.1), channel_id=1, source_target_pairs={{0,1},{1,0},{2,3},{3,2},{4,5},{5,4},{6,7},{7,6},{8,9},{9,8},{10,11... | collective-permute-start | bytes 884744 | tf_op jit(solution)/shard_map/ppermute | solution.py:320
  34.9 9.4 %collective-permute-start.1 = (bf16[1152,128]{1,0:T(8,128)(2,1)S(1)}, bf16[1152,128]{1,0:T(8,128)(2,1)S(1)}, u32[]{:S(2)}, u32[]{:S(2)}) collective-permute-start(bf16[1152,128]{1,0:T(8,128)(2,1)S(1)} %collective-permute-done), channel_id=1, source_target_pairs={{0,1},{1,0},{2,3},{3,2},{4,5},{5,4},{6,7},{7,6},{8,9},{9,8},{10,11... | collective-permute-start | bytes 884744 | tf_op jit(solution)/shard_map/ppermute | solution.py:320
  34.9 0.9 %copy-start.7 = (bf16[3,3,128,64]{2,3,1,0:T(8,128)(2,1)S(1)}, bf16[3,3,128,64]{2,3,1,0:T(8,128)(2,1)}, u32[]{:S(2)}) copy-start(bf16[3,3,128,64]{2,3,1,0:T(8,128)(2,1)} %param.15) | copy-start | bytes 442372

commit v3 on v2

--- a/solution.py
+++ b/solution.py
@@ -17,6 +17,10 @@
 
 def round_up(value, step):
     return -(-value // step) * step
+
+
+def in_hbm(value):
+    return pltpu.with_memory_space_constraint(value, pltpu.HBM)
 
 
 def dot(a, b):
@@ -238,12 +242,13 @@
             from_right = jnp.where(lane == side - 1, at_right, pltpu.roll(y[2 * outs :], side - 1, 1))
             total = y[outs : 2 * outs] + from_left + from_right
             if last:
-                spread[:, u, :] = total + before_ref[i]
+                spread[pl.ds(u * (outs + 1), outs), :] = total + before_ref[i]
             else:
                 out_ref[i] = total
         if last:
             rows = pl.ds(pl.multiple_of(first, STEP), STEP)
-            staged[:, rows, :] = spread[...].astype(BF16)
+            for o in range(outs):
+                staged[o, rows, :] = spread[pl.ds(o, STEP, stride=outs + 1), :].astype(BF16)
             pltpu.make_async_copy(staged.at[:, rows, :], out_ref.at[:, rows, :], out_sems.at[first // STEP]).start()
 
     for r in range(STEP + 1):
@@ -276,8 +281,8 @@
     parts = lax.axis_size("chan")
     rows = round_up(2 * taps + tiles, 16)
     params = pltpu.CompilerParams(vmem_limit_bytes=LIMIT)
-    slots, weights = block_slot.T, weight_index.T
-    filters = conv_weight.transpose(0, 1, 3, 2)
+    slots, weights = in_hbm(block_slot.T), in_hbm(weight_index.T)
+    filters = in_hbm(conv_weight.transpose(0, 1, 3, 2))
     packed, table = pl.pallas_call(
         pack_kernel,
         out_shape=[
@@ -294,7 +299,7 @@
         ],
         compiler_params=params,
         name="pack",
-    )(slots, weights, send_list, source, remap_table)
+    )(slots, weights, in_hbm(send_list), in_hbm(source), in_hbm(remap_table))
     gathered = lax.all_gather(packed, "tile")
     few = 5 * tiles + 4 * 2 * taps
     mine = pl.pallas_call(
@@ -314,20 +319,23 @@
         ],
         compiler_params=params,
         name="edges",
-    )(neighbour_tile, neighbour_edge, gathered, table)
+    )(in_hbm(neighbour_tile), in_hbm(neighbour_edge), gathered, table)
 
     def swap(value, flip):
         return lax.ppermute(value, "chan", [(i, i ^ flip) for i in range(parts)])
 
-    held = {0: mine}
-    bit = parts // 2
-    while bit:
-        for flip in list(held):
-            held[flip ^ bit] = swap(held[flip], bit)
-        bit //= 2
+    def spread(held, bit):
+        while bit:
+            for flip in list(held):
+                held[flip ^ bit] = swap(held[flip], bit)
+            bit //= 2
+        return [held[f].reshape(count + 4, chans, side) for f in sorted(held)]
+
     many = parts // 2
     half = all_chans // 2
-    held = [held[f].reshape(count + 4, chans, side) for f in sorted(held)]
+    near = spread({0: mine}, many // 2)
+    mine, *near = lax.optimization_barrier((mine, *near))
+    across = swap(mine, many)
     dims = (side, chans, cap, tiles, all_chans, outs)
     scratch = [
         pltpu.SMEM(slots.shape, jnp.int32),
@@ -347,7 +355,9 @@
         compiler_params=params,
         cost_estimate=cost,
         name="near",
-    )(*held[:many], slots, weights, table, filters)
+    )(*near, slots, weights, table, filters)
+    across, so_far = lax.optimization_barrier((across, so_far))
+    far = spread({many: across}, many // 2)
     return pl.pallas_call(
         functools.partial(tile_kernel, dims, True, many),
         out_shape=jax.ShapeDtypeStruct((outs, side, side), BF16),
@@ -355,7 +365,7 @@
         out_specs=HBM,
         scratch_shapes=scratch
         + [
-            pltpu.VMEM((outs, STEP, side), F32),
+            pltpu.VMEM((round_up(STEP * (outs + 1), 8), side), F32),
             pltpu.VMEM((outs, side, side), BF16),
             pltpu.SemaphoreType.DMA((side // STEP,)),
             pltpu.SemaphoreType.DMA((3,)),
@@ -363,7 +373,7 @@
         compiler_params=params,
         cost_estimate=cost,
         name="far",
-    )(*held[many:], so_far, slots, weights, table, filters)
+    )(*far, so_far, slots, weights, table, filters)
 
 
 def solution(mesh):

time: 56.2 us -> 48.3 us (0.86)
  local copies, waits for them, and re-layouts: 6.4 us -> 0 us
  waiting for transfers between devices: 5.88 us -> 3.14 us
  Pallas kernels: 24.6 us -> 25.8 us
    unnamed x16 -> x0, local copies, waits for them, and re-layouts: 6.4 us -> none
    ppermute x3, waiting for transfers between devices: 5.88 us -> 3.14 us  [swap(): return lax.ppermute(value, 'chan', [(i, i ^ flip) for i in range(parts)])]
    pallas_call x1, Pallas kernels: 0.33 us -> 1.58 us  [body(): pl.pallas_call(pack_kernel, out_shape=[jax.ShapeDtypeStruct((blocks * cha...]
    pallas_call x1, Pallas kernels: 11.7 us -> 10.6 us  [body(): pl.pallas_call(functools.partial(tile_kernel, dims, True, many), out_shap...]
    pallas_call x1, Pallas kernels: 4.09 us -> 4.8 us  [body(): pl.pallas_call(functools.partial(edge_kernel, (side, chans, blocks, tiles...]
  transfers between devices with their start and end apart: 3 -> 3, of which waited for: 1 -> 2; matrix products, arithmetic and copies ran while one was open for 0% -> 0% of each run, Pallas kernels for 15% -> 18%
where the time goes in v3:
time: 48.3 us; the launch traced here: 48.1 us
  Pallas kernels  25.8 us (53%)
  blocking collectives  17.5 us (36%)
  waiting for transfers between devices  3.14 us (7%)
  starting transfers between devices  1.63 us (3%)
    all_gather x1, blocking collectives, body(): gathered = lax.all_gather(packed, 'tile')  17.5 us
    pallas_call x1, Pallas kernels, body(): pl.pallas_call(functools.partial(tile_kernel, dims, True, many), out_shap...  10.6 us
    pallas_call x1, Pallas kernels, body(): pl.pallas_call(functools.partial(tile_kernel, dims, False, many), out_sha...  8.83 us
    pallas_call x1, Pallas kernels, body(): pl.pallas_call(functools.partial(edge_kernel, (side, chans, blocks, tiles...  4.8 us
    ppermute x3, waiting for transfers between devices, swap(): return lax.ppermute(value, 'chan', [(i, i ^ flip) for i in range(parts)])  3.14 us
    ppermute x3, starting transfers between devices, swap(): return lax.ppermute(value, 'chan', [(i, i ^ flip) for i in range(parts)])  1.63 us
    pallas_call x1, Pallas kernels, body(): pl.pallas_call(pack_kernel, out_shape=[jax.ShapeDtypeStruct((blocks * cha...  1.58 us
  transfers between devices with their start and end apart: 3, of which 2 were waited for; matrix products, arithmetic and copies ran while one was open for 0% of the time, Pallas kernels for 18%

profile of v3, /device:TPU:0, one launch (start us, length us, event | category | flops | bytes accessed | tf_op | source)
XLA Modules:
  0.0 48.1 jit_solution(163235807115470186)
XLA Ops:
  0.0 1.6 %pack.1 = (bf16[528,128]{1,0:T(8,128)(2,1)S(1)}, bf16[32,128,128]{2,1,0:T(8,128)(2,1)S(1)}) custom-call(s32[6,128]{1,0:T(8,128)} %bitcast.13, s32[6,128]{1,0:T(8,128)} %bitcast.16, s32[1,4,8]{2,1,0:T(4,128)} %lists_hbm.1, bf16[32,2048]{1,0:T(8,128)(2,1)} %source_hbm.1, bf16[32,128,128]{2,1,0:T(8,128)(2,1)} %table_hbm.1), custom_call_target="tpu_custom_call" | custom-call | tf_op jit(solution)/shard_map/pack/pallas_call | solution.py:286
  1.6 17.5 %all-gather = bf16[2112,128]{1,0:T(8,128)(2,1)S(1)} all-gather(bf16[528,128]{1,0:T(8,128)(2,1)S(1)} %get-tuple-element.12), channel_id=2, replica_groups=mesh['group'=2,'tile'=4,'chan'=4] {'tile'}, dimensions={0}, use_global_device_ids=true | all-gather | bytes 675840 | tf_op jit(solution)/shard_map/all_gather | solution.py:303
  19.1 4.8 %edges.1 = bf16[1152,128]{1,0:T(8,128)(2,1)S(1)} custom-call(s32[1,4]{1,0:T(1,128)} %neigh_hbm.1, s32[1,4]{1,0:T(1,128)} %codes_hbm.1, bf16[4,528,128]{2,1,0:T(8,128)(2,1)S(1)} %bitcast.8, bf16[32,128,128]{2,1,0:T(8,128)(2,1)S(1)} %get-tuple-element.13.table_ref.refs_4_.refs_5_), custom_call_target="tpu_custom_call" | custom-call | tf_op jit(solution)/shard_map/edges/pallas_call | solution.py:305
  23.9 0.1 collective-permute-start
  24.0 1.6 %collective-permute-done = bf16[1152,128]{1,0:T(8,128)(2,1)S(1)} collective-permute-done((bf16[1152,128]{1,0:T(8,128)(2,1)S(1)}, bf16[1152,128]{1,0:T(8,128)(2,1)S(1)}, u32[]{:S(2)}, u32[]{:S(2)}) %collective-permute-start) | collective-permute-done | bytes 294944 | tf_op jit(solution)/shard_map/ppermute | solution.py:325
  25.6 1.5 %collective-permute-start.1 = (bf16[1152,128]{1,0:T(8,128)(2,1)S(1)}, bf16[1152,128]{1,0:T(8,128)(2,1)S(1)}, u32[]{:S(2)}, u32[]{:S(2)}) collective-permute-start(bf16[1152,128]{1,0:T(8,128)(2,1)S(1)} %edges.1), channel_id=1, source_target_pairs={{0,2},{1,3},{2,0},{3,1},{4,6},{5,7},{6,4},{7,5},{8,10},{9,11},{10,... | collective-permute-start | bytes 884744 | tf_op jit(solution)/shard_map/ppermute | solution.py:325
  27.0 8.8 %near.1.refs_2_ = f32[130,64,128]{2,1,0:T(8,128)S(1)} custom-call(bf16[36,32,128]{2,1,0:T(8,128)(2,1)S(1)} %bitcast.9, bf16[36,32,128]{2,1,0:T(8,128)(2,1)S(1)} %bitcast.11, s32[6,128]{1,0:T(8,128)} %bitcast.14, s32[6,128]{1,0:T(8,128)} %bitcast.17, bf16[32,128,128]{2,1,0:T(8,128)(2,1)S(1)} %get-tuple-element.13.table_ref.refs_4_.refs_5_, ...), custom_call_target="tpu_custom_call" | custom-call | flops 2818572288 | bytes 4259840 | tf_op jit(solution)/shard_map/near/pallas_call | solution.py:349
  35.9 0.0 collective-permute-done.1
  35.9 0.1 collective-permute-start.2
  36.0 1.6 %collective-permute-done.2 = bf16[1152,128]{1,0:T(8,128)(2,1)S(1)} collective-permute-done((bf16[1152,128]{1,0:T(8,128)(2,1)S(1)}, bf16[1152,128]{1,0:T(8,128)(2,1)S(1)}, u32[]{:S(2)}, u32[]{:S(2)}) %collective-permute-start.2) | collective-permute-done | bytes 294944 | tf_op jit(solution)/shard_map/ppermute | solution.py:325
  37.5 10.6 %far.1 = bf16[64,128,128]{2,1,0:T(8,128)(2,1)} custom-call(bf16[36,32,128]{2,1,0:T(8,128)(2,1)S(1)} %bitcast.10, bf16[36,32,128]{2,1,0:T(8,128)(2,1)S(1)} %bitcast.12, f32[130,64,128]{2,1,0:T(8,128)S(1)} %near.1.refs_2_, s32[6,128]{1,0:T(8,128)} %bitcast.15, s32[6,128]{1,0:T(8,128)} %bitcast.18, ...), custom_call_target="tpu_custom_call" | custom-call | flops 2818572288 | bytes 4259840 | tf_op jit(solution)/shard_map/far/pallas_call | solution.py:361
Async XLA Ops:
  23.9 1.6 %collective-permute-start = (bf16[1152,128]{1,0:T(8,128)(2,1)S(1)}, bf16[1152,128]{1,0:T(8,128)(2,1)S(1)}, u32[]{:S(2)}, u32[]{:S(2)}) collective-permute-start(bf16[1152,128]{1,0:T(8,128)(2,1)S(1)} %edges.1), channel_id=1, source_target_pairs={{0,1},{1,0},{2,3},{3,2},{4,5},{5,4},{6,7},{7,6},{8,9},{9,8},{10,11... | collective-permute-start | bytes 884744 | tf_op jit(solution)/shard_map/ppermute | solution.py:325
  25.6 10.3 %collective-permute-start.1 = (bf16[1152,128]{1,0:T(8,128)(2,1)S(1)}, bf16[1152,128]{1,0:T(8,128)(2,1)S(1)}, u32[]{:S(2)}, u32[]{:S(2)}) collective-permute-start(bf16[1152,128]{1,0:T(8,128)(2,1)S(1)} %edges.1), channel_id=1, source_target_pairs={{0,2},{1,3},{2,0},{3,1},{4,6},{5,7},{6,4},{7,5},{8,10},{9,11},{10,... | collective-permute-start | bytes 884744 | tf_op jit(solution)/shard_map/ppermute | solution.py:325
  35.9 1.6 %collective-permute-start.2 = (bf16[1152,128]{1,0:T(8,128)(2,1)S(1)}, bf16[1152,128]{1,0:T(8,128)(2,1)S(1)}, u32[]{:S(2)}, u32[]{:S(2)}) collective-permute-start(bf16[1152,128]{1,0:T(8,128)(2,1)S(1)} %collective-permute-done.1), channel_id=1, source_target_pairs={{0,1},{1,0},{2,3},{3,2},{4,5},{5,4},{6,7},{7,6},{8,9},{9,8},{10,11... | collective-permute-start | bytes 884744 | tf_op jit(solution)/shard_map/ppermute | solution.py:325

commit v4 on v3

--- a/solution.py
+++ b/solution.py
@@ -34,58 +34,55 @@
     return copies
 
 
-def pack_kernel(slots_hbm, weights_hbm, lists_hbm, source_hbm, table_hbm, out_ref, table_ref, slots, weights, lists, sems):
+def pack_kernel(
+    slots_hbm, weights_hbm, lists_hbm, neigh_hbm, codes_hbm, source_hbm, table_hbm, filters_hbm,
+    out_ref, slots, weights, table_ref, filters, lists, neigh, codes, sems,
+):
     side = out_ref.shape[1]
     chans = source_hbm.shape[0]
     blocks = source_hbm.shape[1] // side
     base = blocks * chans
     copies = start_all(
         sems,
-        [(slots_hbm, slots), (weights_hbm, weights), (lists_hbm.at[0], lists)]
+        [(slots_hbm, slots), (weights_hbm, weights), (lists_hbm.at[0], lists), (neigh_hbm, neigh), (codes_hbm, codes)]
         + [
             (source_hbm.at[:, pl.ds(block * side, side)], out_ref.at[pl.ds(block * chans, chans), :])
             for block in range(blocks)
         ]
-        + [(table_hbm, table_ref)],
+        + [(table_hbm, table_ref), (filters_hbm, filters)],
     )
-    for copy in copies[:3]:
+    for copy in copies[:5]:
         copy.wait()
     taps = slots.shape[0]
     tiles, cap = lists.shape
     rows = out_ref.shape[0] - base
-    wide = jnp.concatenate([lists[...].astype(F32), jnp.zeros((tiles, side - cap), F32)], axis=1)
+    sides = jnp.concatenate([neigh[...], codes[...]], axis=1).astype(F32)
+    wide = jnp.concatenate(
+        [
+            lists[...].astype(F32),
+            jnp.concatenate([sides, jnp.zeros((tiles - 1, sides.shape[1]), F32)], axis=0),
+            jnp.zeros((tiles, side - cap - sides.shape[1]), F32),
+        ],
+        axis=1,
+    )
     parts = [slots[...].astype(F32), weights[...].astype(F32), wide]
     if rows > 2 * taps + tiles:
         parts.append(jnp.zeros((rows - 2 * taps - tiles, side), F32))
     out_ref[base:, :] = jnp.concatenate(parts, axis=0).astype(BF16)
-    for copy in copies[3:]:
+    for copy in copies[5:]:
         copy.wait()
 
 
-def edge_kernel(
-    dims, neigh_hbm, codes_hbm, gathered_ref, table_ref, out_ref,
-    neigh, codes, ints, few_v, few_s, picked, columns, sems,
-):
+def edge_kernel(dims, gathered_ref, table_ref, out_ref, ints, scalars, picked, columns, sem):
     side, chans, blocks, tiles, cap, taps, rows = dims
     count = tiles * cap
     base = blocks * chans
     kinds = table_ref.shape[0]
     per_group = side // kinds
     me = lax.axis_index("tile")
-    scalars = start_all(sems, [(neigh_hbm, neigh), (codes_hbm, codes)])
     for band in range(tiles):
         ints[band * rows : (band + 1) * rows, :] = gathered_ref[band, base:, :].astype(F32).astype(jnp.int32)
-    for copy in scalars:
-        copy.wait()
-    owners = [me] + [neigh[0, s] for s in range(4)]
-    for which, owner in enumerate(owners):
-        for band in range(tiles):
-            few_v[pl.ds(which * tiles + band, 1), :] = ints[pl.ds(band * rows + 2 * taps + owner, 1), :]
-    lists_end = 5 * tiles
-    for s in range(4):
-        for k in range(2 * taps):
-            few_v[pl.ds(lists_end + s * 2 * taps + k, 1), :] = ints[pl.ds(owners[s + 1] * rows + k, 1), :]
-    copy = pltpu.make_async_copy(few_v, few_s, sems.at[2])
+    copy = pltpu.make_async_copy(ints, scalars, sem)
     copy.start()
     lane = lax.broadcasted_iota(jnp.int32, (side, side), 1)
     total = jnp.zeros((side, side), F32)
@@ -94,16 +91,20 @@
         total = jnp.where(lane // per_group == kind, moved, total)
     columns[...] = total
     copy.wait()
-
-    def block_of(which, slot):
+    own_row = me * rows + 2 * taps
+    neigh = [scalars[own_row, cap + s] for s in range(4)]
+    codes = [scalars[own_row, cap + 4 + s] for s in range(4)]
+
+    def block_of(owner, slot):
         band = slot // cap
-        local = few_s[which * tiles + band, slot % cap]
+        local = scalars[band * rows + 2 * taps + owner, slot % cap]
         return gathered_ref[band, pl.ds(pl.multiple_of(local * chans, chans), chans), :]
 
     for slot in range(count):
-        out_ref[slot * chans : (slot + 1) * chans, :] = block_of(0, slot)
+        out_ref[slot * chans : (slot + 1) * chans, :] = block_of(me, slot)
     for s in range(4):
-        edge = codes[0, s] % 4
+        owner = neigh[s]
+        edge = codes[s] % 4
         dest = pl.ds((count + s) * chans, chans)
 
         @pl.when(edge < 2)
@@ -111,16 +112,16 @@
             at = jnp.where(edge == 0, 0, side - 1)
             acc = jnp.zeros((chans, side), F32)
             for k in range(taps):
-                slot = few_s[lists_end + s * 2 * taps + k, at]
-                kind = few_s[lists_end + s * 2 * taps + taps + k, at]
-                acc = acc + dot(block_of(1 + s, slot), table_ref[kind])
+                slot = scalars[owner * rows + k, at]
+                kind = scalars[owner * rows + taps + k, at]
+                acc = acc + dot(block_of(owner, slot), table_ref[kind])
             out_ref[dest, :] = acc.astype(BF16)
 
         @pl.when(edge >= 2)
         def _():
             for slot in range(count):
                 group, member = slot // per_group, slot % per_group
-                picked[group * chans : (group + 1) * chans, member * side : (member + 1) * side] = block_of(1 + s, slot)
+                picked[group * chans : (group + 1) * chans, member * side : (member + 1) * side] = block_of(owner, slot)
             col = columns[...]
             col = jnp.where(edge == 2, pltpu.roll(col, side - 1, 1), col)
             col = jnp.where(lane % per_group == 0, col, 0.0)
@@ -132,8 +133,8 @@
             z_lo = (z - z_hi.astype(F32)).astype(BF16)
             keys = []
             for k in range(taps):
-                slot = few_v[pl.ds(lists_end + s * 2 * taps + k, 1), :]
-                kind = few_v[pl.ds(lists_end + s * 2 * taps + taps + k, 1), :]
+                slot = ints[pl.ds(owner * rows + k, 1), :]
+                kind = ints[pl.ds(owner * rows + taps + k, 1), :]
                 keys.append(slot // per_group * side + kind * per_group + slot % per_group)
             acc = jnp.zeros((2 * chans, side), F32)
             for group in range(count // per_group):
@@ -151,33 +152,16 @@
     turned = dot(plain, flip).astype(BF16)
     for s in range(4):
         at = slice(s * chans, (s + 1) * chans)
-        out_ref[(count + s) * chans : (count + s + 1) * chans, :] = jnp.where(codes[0, s] >= 4, turned[at], plain[at])
-
-
-def tile_kernel(dims, last, many, *refs):
-    side, chans, cap, tiles, all_chans, outs = dims
-    parts = refs[:many]
-    refs = refs[many:]
-    if last:
-        before_ref, *refs = refs
-    slots_hbm, weights_hbm, table_ref, filters_hbm, out_ref, slots, weights, filters, matrix, image, *refs = refs
-    if last:
-        spread, staged, out_sems, sems = refs
-    else:
-        (sems,) = refs
-    taps = slots.shape[0]
-    count = tiles * cap
-    half = chans * many
-    copies = start_all(sems, [(filters_hbm, filters), (slots_hbm, slots), (weights_hbm, weights)])
+        out_ref[(count + s) * chans : (count + s + 1) * chans, :] = jnp.where(codes[s] >= 4, turned[at], plain[at])
+
+
+def filter_kernel(chans, filters, near_ref, far_ref):
+    outs, all_chans = filters.shape[2:]
+    half = all_chans // 2
     me = lax.axis_index("chan")
-
-    def channels(index):
-        return jnp.concatenate([part[index] for part in parts], axis=0)
-
-    copies[0].wait()
     lane = lax.broadcasted_iota(jnp.int32, (outs, all_chans), 1)
     for b in range(3):
-        low, high = [], []
+        first, second = [], []
         for a in range(3):
             value = filters[a, b].astype(F32)
             width = chans
@@ -189,12 +173,33 @@
                 value = jnp.where((me & bit) != 0, other, value)
                 width *= 2
                 bit *= 2
-            turned = pltpu.roll(value, half, 1)
-            low.append(turned if last else value)
-            high.append(value if last else turned)
+            first.append(value)
+            second.append(pltpu.roll(value, half, 1))
         at = slice(b * outs, (b + 1) * outs)
-        matrix[at, :all_chans] = jnp.where(lane < half, low[0], high[1]).astype(BF16)
-        matrix[at, all_chans:] = low[2][:, :half].astype(BF16)
+        near_ref[at, :all_chans] = jnp.where(lane < half, first[0], second[1]).astype(BF16)
+        near_ref[at, all_chans:] = first[2][:, :half].astype(BF16)
+        far_ref[at, :all_chans] = jnp.where(lane < half, second[0], first[1]).astype(BF16)
+        far_ref[at, all_chans:] = second[2][:, :half].astype(BF16)
+
+
+def tile_kernel(dims, last, many, *refs):
+    side, chans, cap, tiles, all_chans, outs = dims
+    parts = refs[:many]
+    refs = refs[many:]
+    if last:
+        before_ref, *refs = refs
+    slots_ref, weights_ref, table_ref, matrix, out_ref, slots, weights, image, *refs = refs
+    if last:
+        spread, staged, out_sems, sems = refs
+    else:
+        (sems,) = refs
+    taps = slots.shape[0]
+    count = tiles * cap
+    half = chans * many
+    copies = start_all(sems, [(slots_ref, slots), (weights_ref, weights)])
+
+    def channels(index):
+        return jnp.concatenate([part[index] for part in parts], axis=0)
 
     image[0:half, :] = channels(count)
     image[(side + 1) * half :, :] = channels(count + 1)
@@ -214,7 +219,7 @@
     else:
         out_ref[side] = left
         out_ref[side + 1] = right
-    for copy in copies[1:]:
+    for copy in copies:
         copy.wait()
 
     def remap(r):
@@ -283,43 +288,45 @@
     params = pltpu.CompilerParams(vmem_limit_bytes=LIMIT)
     slots, weights = in_hbm(block_slot.T), in_hbm(weight_index.T)
     filters = in_hbm(conv_weight.transpose(0, 1, 3, 2))
-    packed, table = pl.pallas_call(
+    packed, slots, weights, table, filters = pl.pallas_call(
         pack_kernel,
         out_shape=[
             jax.ShapeDtypeStruct((blocks * chans + rows, side), BF16),
+            jax.ShapeDtypeStruct(slots.shape, jnp.int32),
+            jax.ShapeDtypeStruct(weights.shape, jnp.int32),
             jax.ShapeDtypeStruct(remap_table.shape, BF16),
+            jax.ShapeDtypeStruct(filters.shape, BF16),
         ],
-        in_specs=[HBM] * 5,
-        out_specs=[VMEM] * 2,
+        in_specs=[HBM] * 8,
+        out_specs=[VMEM] * 5,
         scratch_shapes=[
-            pltpu.VMEM(slots.shape, jnp.int32),
-            pltpu.VMEM(weights.shape, jnp.int32),
             pltpu.VMEM((tiles, cap), jnp.int32),
-            pltpu.SemaphoreType.DMA((blocks + 4,)),
+            pltpu.VMEM(neighbour_tile.shape, jnp.int32),
+            pltpu.VMEM(neighbour_edge.shape, jnp.int32),
+            pltpu.SemaphoreType.DMA((blocks + 7,)),
         ],
         compiler_params=params,
         name="pack",
-    )(slots, weights, in_hbm(send_list), in_hbm(source), in_hbm(remap_table))
+    )(
+        slots, weights, in_hbm(send_list), in_hbm(neighbour_tile), in_hbm(neighbour_edge), in_hbm(source),
+        in_hbm(remap_table), filters,
+    )
     gathered = lax.all_gather(packed, "tile")
-    few = 5 * tiles + 4 * 2 * taps
     mine = pl.pallas_call(
         functools.partial(edge_kernel, (side, chans, blocks, tiles, cap, taps, rows)),
         out_shape=jax.ShapeDtypeStruct(((count + 4) * chans, side), BF16),
-        in_specs=[HBM, HBM, VMEM, VMEM],
+        in_specs=[VMEM, VMEM],
         out_specs=VMEM,
         scratch_shapes=[
-            pltpu.SMEM(neighbour_tile.shape, jnp.int32),
-            pltpu.SMEM(neighbour_edge.shape, jnp.int32),
             pltpu.VMEM((tiles * rows, side), jnp.int32),
-            pltpu.VMEM((few, side), jnp.int32),
-            pltpu.SMEM((few, side), jnp.int32),
+            pltpu.SMEM((tiles * rows, side), jnp.int32),
             pltpu.VMEM((count * kinds // side * chans, side * side // kinds), BF16),
             pltpu.VMEM((side, side), F32),
-            pltpu.SemaphoreType.DMA((3,)),
+            pltpu.SemaphoreType.DMA,
         ],
         compiler_params=params,
         name="edges",
-    )(in_hbm(neighbour_tile), in_hbm(neighbour_edge), gathered, table)
+    )(gathered, table)
 
     def swap(value, flip):
         return lax.ppermute(value, "chan", [(i, i ^ flip) for i in range(parts)])
@@ -333,15 +340,22 @@
 
     many = parts // 2
     half = all_chans // 2
+    mine, filters = lax.optimization_barrier((mine, filters))
     near = spread({0: mine}, many // 2)
-    mine, *near = lax.optimization_barrier((mine, *near))
+    near_filters, far_filters = pl.pallas_call(
+        functools.partial(filter_kernel, chans),
+        out_shape=[jax.ShapeDtypeStruct((3 * outs, 3 * half), BF16)] * 2,
+        in_specs=[VMEM],
+        out_specs=[VMEM] * 2,
+        compiler_params=params,
+        name="filters",
+    )(filters)
+    mine, near_filters = lax.optimization_barrier((mine, near_filters))
     across = swap(mine, many)
     dims = (side, chans, cap, tiles, all_chans, outs)
     scratch = [
         pltpu.SMEM(slots.shape, jnp.int32),
         pltpu.SMEM(weights.shape, jnp.int32),
-        pltpu.VMEM(filters.shape, BF16),
-        pltpu.VMEM((3 * outs, 3 * half), BF16),
         pltpu.VMEM(((side + 2) * half, side), BF16),
     ]
     flops = 2 * side * half * taps * side * side + 2 * side * side * 9 * half * outs
@@ -349,31 +363,31 @@
     so_far = pl.pallas_call(
         functools.partial(tile_kernel, dims, False, many),
         out_shape=jax.ShapeDtypeStruct((side + 2, outs, side), F32),
-        in_specs=[VMEM] * many + [HBM, HBM, VMEM, HBM],
+        in_specs=[VMEM] * (many + 4),
         out_specs=VMEM,
-        scratch_shapes=scratch + [pltpu.SemaphoreType.DMA((3,))],
+        scratch_shapes=scratch + [pltpu.SemaphoreType.DMA((2,))],
         compiler_params=params,
         cost_estimate=cost,
         name="near",
-    )(*near, slots, weights, table, filters)
+    )(*near, slots, weights, table, near_filters)
     across, so_far = lax.optimization_barrier((across, so_far))
     far = spread({many: across}, many // 2)
     return pl.pallas_call(
         functools.partial(tile_kernel, dims, True, many),
         out_shape=jax.ShapeDtypeStruct((outs, side, side), BF16),
-        in_specs=[VMEM] * (many + 1) + [HBM, HBM, VMEM, HBM],
+        in_specs=[VMEM] * (many + 5),
         out_specs=HBM,
         scratch_shapes=scratch
         + [
             pltpu.VMEM((round_up(STEP * (outs + 1), 8), side), F32),
             pltpu.VMEM((outs, side, side), BF16),
             pltpu.SemaphoreType.DMA((side // STEP,)),
-            pltpu.SemaphoreType.DMA((3,)),
+            pltpu.SemaphoreType.DMA((2,)),
         ],
         compiler_params=params,
         cost_estimate=cost,
         name="far",
-    )(*far, so_far, slots, weights, table, filters)
+    )(*far, so_far, slots, weights, table, far_filters)
 
 
 def solution(mesh):

time: 48.3 us -> 45.7 us (0.946)
  waiting for transfers between devices: 3.14 us -> 1.37 us
  Pallas kernels: 25.8 us -> 24.7 us
    ppermute x3, waiting for transfers between devices: 3.14 us -> 1.37 us  [swap(): return lax.ppermute(value, 'chan', [(i, i ^ flip) for i in range(parts)])]
    pallas_call x1, Pallas kernels: 4.8 us -> 4.11 us  [body(): pl.pallas_call(functools.partial(edge_kernel, (side, chans, blocks, tiles...]
    pallas_call x1, Pallas kernels: 8.83 us -> 8.3 us  [body(): pl.pallas_call(functools.partial(tile_kernel, dims, False, many), out_sha...]
  transfers between devices with their start and end apart: 3 -> 3, of which waited for: 2 -> 1; matrix products, arithmetic and copies ran while one was open for 0% -> 0% of each run, Pallas kernels for 18% -> 19%
where the time goes in v4:
time: 45.7 us; the launch traced here: 45.5 us
  Pallas kernels  24.7 us (54%)
  blocking collectives  17.5 us (38%)
  starting transfers between devices  1.91 us (4%)
  waiting for transfers between devices  1.37 us (3%)
    all_gather x1, blocking collectives, body(): gathered = lax.all_gather(packed, 'tile')  17.5 us
    pallas_call x1, Pallas kernels, body(): pl.pallas_call(functools.partial(tile_kernel, dims, True, many), out_shap...  10.3 us
    pallas_call x1, Pallas kernels, body(): pl.pallas_call(functools.partial(tile_kernel, dims, False, many), out_sha...  8.3 us
    pallas_call x1, Pallas kernels, body(): pl.pallas_call(functools.partial(edge_kernel, (side, chans, blocks, tiles...  4.11 us
    ppermute x3, starting transfers between devices, swap(): return lax.ppermute(value, 'chan', [(i, i ^ flip) for i in range(parts)])  1.91 us
    pallas_call x1, Pallas kernels, body(): pl.pallas_call(pack_kernel, out_shape=[jax.ShapeDtypeStruct((blocks * cha...  1.62 us
    ppermute x3, waiting for transfers between devices, swap(): return lax.ppermute(value, 'chan', [(i, i ^ flip) for i in range(parts)])  1.37 us
  transfers between devices with their start and end apart: 3, of which 1 were waited for; matrix products, arithmetic and copies ran while one was open for 0% of the time, Pallas kernels for 19%

profile of v4, /device:TPU:0, one launch (start us, length us, event | category | flops | bytes accessed | tf_op | source)
XLA Modules:
  0.0 45.5 jit_solution(12433910260275333187)
XLA Ops:
  0.0 1.6 %pack.1 = (bf16[528,128]{1,0:T(8,128)(2,1)S(1)}, s32[6,128]{1,0:T(8,128)S(1)}, s32[6,128]{1,0:T(8,128)S(1)}, bf16[32,128,128]{2,1,0:T(8,128)(2,1)S(1)}, bf16[3,3,64,128]{3,2,1,0:T(8,128)(2,1)S(1)}) custom-call(s32[6,128]{1,0:T(8,128)} %bitcast.14, s32[6,128]{1,0:T(8,128)} %bitcast.15, s32[1,4,8]{2,1,0:T(4,128)} %lists_hbm.1, s32[1,4]{1,0:T(1,128)} %neigh_hbm.1, ...), custom_call_target="tpu_custom_call" | custom-call | tf_op jit(solution)/shard_map/pack/pallas_call | solution.py:291
  1.6 17.5 %all-gather = bf16[2112,128]{1,0:T(8,128)(2,1)S(1)} all-gather(bf16[528,128]{1,0:T(8,128)(2,1)S(1)} %get-tuple-element.18), channel_id=2, replica_groups=mesh['group'=2,'tile'=4,'chan'=4] {'tile'}, dimensions={0}, use_global_device_ids=true | all-gather | bytes 675840 | tf_op jit(solution)/shard_map/all_gather | solution.py:314
  19.1 4.1 %edges.1 = bf16[1152,128]{1,0:T(8,128)(2,1)S(1)} custom-call(bf16[4,528,128]{2,1,0:T(8,128)(2,1)S(1)} %bitcast.8, bf16[32,128,128]{2,1,0:T(8,128)(2,1)S(1)} %get-tuple-element.19.table_ref.refs_4_.refs_5_), custom_call_target="tpu_custom_call" | custom-call | tf_op jit(solution)/shard_map/edges/pallas_call | solution.py:315
  23.3 0.1 collective-permute-start.1
  23.3 0.4 filters.1
  23.7 1.6 %collective-permute-start = (bf16[1152,128]{1,0:T(8,128)(2,1)S(1)}, bf16[1152,128]{1,0:T(8,128)(2,1)S(1)}, u32[]{:S(2)}, u32[]{:S(2)}) collective-permute-start(bf16[1152,128]{1,0:T(8,128)(2,1)S(1)} %edges.1), channel_id=1, source_target_pairs={{0,2},{1,3},{2,0},{3,1},{4,6},{5,7},{6,4},{7,5},{8,10},{9,11},{10,... | collective-permute-start | bytes 884744 | tf_op jit(solution)/shard_map/ppermute | solution.py:332
  25.3 0.0 collective-permute-done.1
  25.3 8.3 %near.1.refs_2_ = f32[130,64,128]{2,1,0:T(8,128)S(1)} custom-call(bf16[36,32,128]{2,1,0:T(8,128)(2,1)S(1)} %bitcast.9, bf16[36,32,128]{2,1,0:T(8,128)(2,1)S(1)} %bitcast.11, s32[6,128]{1,0:T(8,128)S(1)} %get-tuple-element.25.refs_2_.refs_3_, s32[6,128]{1,0:T(8,128)S(1)} %get-tuple-element.26.refs_3_.refs_4_, ...), custom_call_target="tpu_custom_call" | custom-call | flops 2818572288 | bytes 4259840 | tf_op jit(solution)/shard_map/near/pallas_call | solution.py:363
  33.6 0.0 collective-permute-done
  33.6 0.3 collective-permute-start.2
  33.9 1.4 %collective-permute-done.2 = bf16[1152,128]{1,0:T(8,128)(2,1)S(1)} collective-permute-done((bf16[1152,128]{1,0:T(8,128)(2,1)S(1)}, bf16[1152,128]{1,0:T(8,128)(2,1)S(1)}, u32[]{:S(2)}, u32[]{:S(2)}) %collective-permute-start.2) | collective-permute-done | bytes 294944 | tf_op jit(solution)/shard_map/ppermute | solution.py:332
  35.2 10.3 %far.1 = bf16[64,128,128]{2,1,0:T(8,128)(2,1)} custom-call(bf16[36,32,128]{2,1,0:T(8,128)(2,1)S(1)} %bitcast.10, bf16[36,32,128]{2,1,0:T(8,128)(2,1)S(1)} %bitcast.12, f32[130,64,128]{2,1,0:T(8,128)S(1)} %near.1.refs_2_, s32[6,128]{1,0:T(8,128)S(1)} %get-tuple-element.25.refs_2_.refs_3_, s32[6,128]{1,0:T(8,128)S(1)} %get-tuple-element.26.refs_3_.refs_4_, ...), custom_call_target="tpu_custom_call" | custom-call | flops 2818572288 | bytes 4259840 | tf_op jit(solution)/shard_map/far/pallas_call | solution.py:375
Async XLA Ops:
  23.3 2.0 %collective-permute-start.1 = (bf16[1152,128]{1,0:T(8,128)(2,1)S(1)}, bf16[1152,128]{1,0:T(8,128)(2,1)S(1)}, u32[]{:S(2)}, u32[]{:S(2)}) collective-permute-start(bf16[1152,128]{1,0:T(8,128)(2,1)S(1)} %edges.1), channel_id=1, source_target_pairs={{0,1},{1,0},{2,3},{3,2},{4,5},{5,4},{6,7},{7,6},{8,9},{9,8},{10,11... | collective-permute-start | bytes 884744 | tf_op jit(solution)/shard_map/ppermute | solution.py:332
  23.7 9.9 %collective-permute-start = (bf16[1152,128]{1,0:T(8,128)(2,1)S(1)}, bf16[1152,128]{1,0:T(8,128)(2,1)S(1)}, u32[]{:S(2)}, u32[]{:S(2)}) collective-permute-start(bf16[1152,128]{1,0:T(8,128)(2,1)S(1)} %edges.1), channel_id=1, source_target_pairs={{0,2},{1,3},{2,0},{3,1},{4,6},{5,7},{6,4},{7,5},{8,10},{9,11},{10,... | collective-permute-start | bytes 884744 | tf_op jit(solution)/shard_map/ppermute | solution.py:332
  33.6 1.6 %collective-permute-start.2 = (bf16[1152,128]{1,0:T(8,128)(2,1)S(1)}, bf16[1152,128]{1,0:T(8,128)(2,1)S(1)}, u32[]{:S(2)}, u32[]{:S(2)}) collective-permute-start(bf16[1152,128]{1,0:T(8,128)(2,1)S(1)} %collective-permute-done), channel_id=1, source_target_pairs={{0,1},{1,0},{2,3},{3,2},{4,5},{5,4},{6,7},{7,6},{8,9},{9,8},{10,11... | collective-permute-start | bytes 884744 | tf_op jit(solution)/shard_map/ppermute | solution.py:332

commit v5 on v4

--- a/solution.py
+++ b/solution.py
@@ -80,10 +80,13 @@
     kinds = table_ref.shape[0]
     per_group = side // kinds
     me = lax.axis_index("tile")
-    for band in range(tiles):
-        ints[band * rows : (band + 1) * rows, :] = gathered_ref[band, base:, :].astype(F32).astype(jnp.int32)
-    copy = pltpu.make_async_copy(ints, scalars, sem)
+    tables = jnp.concatenate([gathered_ref[band, base:, :] for band in range(tiles)], axis=0)
+    ints[: tiles * rows, :] = tables.astype(F32).astype(jnp.int32)
+    copy = pltpu.make_async_copy(ints.at[pl.ds(0, tiles * rows), :], scalars, sem)
     copy.start()
+    row = lax.broadcasted_iota(jnp.int32, (side, side), 0)
+    flip = (lax.broadcasted_iota(jnp.int32, (side, side), 1) + row == side - 1).astype(BF16)
+    ints[tiles * rows :, :] = dot(tables, flip).astype(jnp.int32)
     lane = lax.broadcasted_iota(jnp.int32, (side, side), 1)
     total = jnp.zeros((side, side), F32)
     for kind in range(kinds):
@@ -116,6 +119,10 @@
                 kind = scalars[owner * rows + taps + k, at]
                 acc = acc + dot(block_of(owner, slot), table_ref[kind])
             out_ref[dest, :] = acc.astype(BF16)
+
+            @pl.when(codes[s] >= 4)
+            def _():
+                out_ref[dest, :] = dot(acc.astype(BF16), flip).astype(BF16)
 
         @pl.when(edge >= 2)
         def _():
@@ -131,28 +138,17 @@
             z = dot(picked[...], spread)
             z_hi = z.astype(BF16)
             z_lo = (z - z_hi.astype(F32)).astype(BF16)
-            keys = []
-            for k in range(taps):
-                slot = ints[pl.ds(owner * rows + k, 1), :]
-                kind = ints[pl.ds(owner * rows + taps + k, 1), :]
-                keys.append(slot // per_group * side + kind * per_group + slot % per_group)
+            first = owner * rows + jnp.where(codes[s] >= 4, tiles * rows, 0)
+            slots = ints[pl.ds(first, taps), :]
+            inside = slots % per_group + ints[pl.ds(first + taps, taps), :] * per_group
+            spots = [jnp.where(row == inside[k : k + 1], 1.0, 0.0).astype(BF16) for k in range(taps)]
             acc = jnp.zeros((2 * chans, side), F32)
             for group in range(count // per_group):
-                seat = lax.broadcasted_iota(jnp.int32, (side, side), 0) + group * side
-                hits = jnp.zeros((side, side), F32)
-                for key in keys:
-                    hits = hits + jnp.where(seat == key, 1.0, 0.0)
+                here = jnp.where(slots // per_group == group, 1.0, 0.0).astype(BF16)
+                hits = sum(spots[k] * here[k : k + 1] for k in range(taps))
                 at = slice(group * chans, (group + 1) * chans)
-                acc = acc + dot(jnp.concatenate([z_hi[at], z_lo[at]], axis=0), hits.astype(BF16))
+                acc = acc + dot(jnp.concatenate([z_hi[at], z_lo[at]], axis=0), hits)
             out_ref[dest, :] = (acc[:chans] + acc[chans:]).astype(BF16)
-
-    row = lax.broadcasted_iota(jnp.int32, (side, side), 0)
-    flip = (lane + row == side - 1).astype(BF16)
-    plain = out_ref[count * chans :, :]
-    turned = dot(plain, flip).astype(BF16)
-    for s in range(4):
-        at = slice(s * chans, (s + 1) * chans)
-        out_ref[(count + s) * chans : (count + s + 1) * chans, :] = jnp.where(codes[s] >= 4, turned[at], plain[at])
 
 
 def filter_kernel(chans, filters, near_ref, far_ref):
@@ -318,7 +314,7 @@
         in_specs=[VMEM, VMEM],
         out_specs=VMEM,
         scratch_shapes=[
-            pltpu.VMEM((tiles * rows, side), jnp.int32),
+            pltpu.VMEM((2 * tiles * rows, side), jnp.int32),
             pltpu.SMEM((tiles * rows, side), jnp.int32),
             pltpu.VMEM((count * kinds // side * chans, side * side // kinds), BF16),
             pltpu.VMEM((side, side), F32),

time: 45.7 us -> 44.7 us (0.978)
  Pallas kernels: 24.7 us -> 23.6 us
    pallas_call x1, Pallas kernels: 4.11 us -> 3.04 us  [body(): pl.pallas_call(functools.partial(edge_kernel, (side, chans, blocks, tiles...]
where the time goes in v5:
time: 44.7 us; the launch traced here: 44.5 us
  Pallas kernels  23.6 us (53%)
  blocking collectives  17.5 us (39%)
  starting transfers between devices  1.91 us (4%)
  waiting for transfers between devices  1.37 us (3%)
    all_gather x1, blocking collectives, body(): gathered = lax.all_gather(packed, 'tile')  17.5 us
    pallas_call x1, Pallas kernels, body(): pl.pallas_call(functools.partial(tile_kernel, dims, True, many), out_shap...  10.3 us
    pallas_call x1, Pallas kernels, body(): pl.pallas_call(functools.partial(tile_kernel, dims, False, many), out_sha...  8.31 us
    pallas_call x1, Pallas kernels, body(): pl.pallas_call(functools.partial(edge_kernel, (side, chans, blocks, tiles...  3.04 us
    ppermute x3, starting transfers between devices, swap(): return lax.ppermute(value, 'chan', [(i, i ^ flip) for i in range(parts)])  1.91 us
    pallas_call x1, Pallas kernels, body(): pl.pallas_call(pack_kernel, out_shape=[jax.ShapeDtypeStruct((blocks * cha...  1.62 us
    ppermute x3, waiting for transfers between devices, swap(): return lax.ppermute(value, 'chan', [(i, i ^ flip) for i in range(parts)])  1.37 us
  transfers between devices with their start and end apart: 3, of which 1 were waited for; matrix products, arithmetic and copies ran while one was open for 0% of the time, Pallas kernels for 19%

profile of v5, /device:TPU:0, one launch (start us, length us, event | category | flops | bytes accessed | tf_op | source)
XLA Modules:
  0.0 44.5 jit_solution(9791445604180859370)
XLA Ops:
  0.0 1.6 %pack.1 = (bf16[528,128]{1,0:T(8,128)(2,1)S(1)}, s32[6,128]{1,0:T(8,128)S(1)}, s32[6,128]{1,0:T(8,128)S(1)}, bf16[32,128,128]{2,1,0:T(8,128)(2,1)S(1)}, bf16[3,3,64,128]{3,2,1,0:T(8,128)(2,1)S(1)}) custom-call(s32[6,128]{1,0:T(8,128)} %bitcast.14, s32[6,128]{1,0:T(8,128)} %bitcast.15, s32[1,4,8]{2,1,0:T(4,128)} %lists_hbm.1, s32[1,4]{1,0:T(1,128)} %neigh_hbm.1, ...), custom_call_target="tpu_custom_call" | custom-call | tf_op jit(solution)/shard_map/pack/pallas_call | solution.py:287
  1.6 17.5 %all-gather = bf16[2112,128]{1,0:T(8,128)(2,1)S(1)} all-gather(bf16[528,128]{1,0:T(8,128)(2,1)S(1)} %get-tuple-element.18), channel_id=2, replica_groups=mesh['group'=2,'tile'=4,'chan'=4] {'tile'}, dimensions={0}, use_global_device_ids=true | all-gather | bytes 675840 | tf_op jit(solution)/shard_map/all_gather | solution.py:310
  19.1 3.0 %edges.1 = bf16[1152,128]{1,0:T(8,128)(2,1)S(1)} custom-call(bf16[4,528,128]{2,1,0:T(8,128)(2,1)S(1)} %bitcast.8, bf16[32,128,128]{2,1,0:T(8,128)(2,1)S(1)} %get-tuple-element.19.table_ref.refs_4_.refs_5_), custom_call_target="tpu_custom_call" | custom-call | tf_op jit(solution)/shard_map/edges/pallas_call | solution.py:311
  22.2 0.1 collective-permute-start.1
  22.3 0.4 filters.1
  22.6 1.6 %collective-permute-start = (bf16[1152,128]{1,0:T(8,128)(2,1)S(1)}, bf16[1152,128]{1,0:T(8,128)(2,1)S(1)}, u32[]{:S(2)}, u32[]{:S(2)}) collective-permute-start(bf16[1152,128]{1,0:T(8,128)(2,1)S(1)} %edges.1), channel_id=1, source_target_pairs={{0,2},{1,3},{2,0},{3,1},{4,6},{5,7},{6,4},{7,5},{8,10},{9,11},{10,... | collective-permute-start | bytes 884744 | tf_op jit(solution)/shard_map/ppermute | solution.py:328
  24.2 0.0 collective-permute-done.1
  24.2 8.3 %near.1.refs_2_ = f32[130,64,128]{2,1,0:T(8,128)S(1)} custom-call(bf16[36,32,128]{2,1,0:T(8,128)(2,1)S(1)} %bitcast.9, bf16[36,32,128]{2,1,0:T(8,128)(2,1)S(1)} %bitcast.11, s32[6,128]{1,0:T(8,128)S(1)} %get-tuple-element.25.refs_2_.refs_3_, s32[6,128]{1,0:T(8,128)S(1)} %get-tuple-element.26.refs_3_.refs_4_, ...), custom_call_target="tpu_custom_call" | custom-call | flops 2818572288 | bytes 4259840 | tf_op jit(solution)/shard_map/near/pallas_call | solution.py:359
  32.5 0.0 collective-permute-done
  32.5 0.3 collective-permute-start.2
  32.8 1.4 %collective-permute-done.2 = bf16[1152,128]{1,0:T(8,128)(2,1)S(1)} collective-permute-done((bf16[1152,128]{1,0:T(8,128)(2,1)S(1)}, bf16[1152,128]{1,0:T(8,128)(2,1)S(1)}, u32[]{:S(2)}, u32[]{:S(2)}) %collective-permute-start.2) | collective-permute-done | bytes 294944 | tf_op jit(solution)/shard_map/ppermute | solution.py:328
  34.2 10.3 %far.1 = bf16[64,128,128]{2,1,0:T(8,128)(2,1)} custom-call(bf16[36,32,128]{2,1,0:T(8,128)(2,1)S(1)} %bitcast.10, bf16[36,32,128]{2,1,0:T(8,128)(2,1)S(1)} %bitcast.12, f32[130,64,128]{2,1,0:T(8,128)S(1)} %near.1.refs_2_, s32[6,128]{1,0:T(8,128)S(1)} %get-tuple-element.25.refs_2_.refs_3_, s32[6,128]{1,0:T(8,128)S(1)} %get-tuple-element.26.refs_3_.refs_4_, ...), custom_call_target="tpu_custom_call" | custom-call | flops 2818572288 | bytes 4259840 | tf_op jit(solution)/shard_map/far/pallas_call | solution.py:371
Async XLA Ops:
  22.2 2.0 %collective-permute-start.1 = (bf16[1152,128]{1,0:T(8,128)(2,1)S(1)}, bf16[1152,128]{1,0:T(8,128)(2,1)S(1)}, u32[]{:S(2)}, u32[]{:S(2)}) collective-permute-start(bf16[1152,128]{1,0:T(8,128)(2,1)S(1)} %edges.1), channel_id=1, source_target_pairs={{0,1},{1,0},{2,3},{3,2},{4,5},{5,4},{6,7},{7,6},{8,9},{9,8},{10,11... | collective-permute-start | bytes 884744 | tf_op jit(solution)/shard_map/ppermute | solution.py:328
  22.6 9.9 %collective-permute-start = (bf16[1152,128]{1,0:T(8,128)(2,1)S(1)}, bf16[1152,128]{1,0:T(8,128)(2,1)S(1)}, u32[]{:S(2)}, u32[]{:S(2)}) collective-permute-start(bf16[1152,128]{1,0:T(8,128)(2,1)S(1)} %edges.1), channel_id=1, source_target_pairs={{0,2},{1,3},{2,0},{3,1},{4,6},{5,7},{6,4},{7,5},{8,10},{9,11},{10,... | collective-permute-start | bytes 884744 | tf_op jit(solution)/shard_map/ppermute | solution.py:328
  32.5 1.6 %collective-permute-start.2 = (bf16[1152,128]{1,0:T(8,128)(2,1)S(1)}, bf16[1152,128]{1,0:T(8,128)(2,1)S(1)}, u32[]{:S(2)}, u32[]{:S(2)}) collective-permute-start(bf16[1152,128]{1,0:T(8,128)(2,1)S(1)} %collective-permute-done), channel_id=1, source_target_pairs={{0,1},{1,0},{2,3},{3,2},{4,5},{5,4},{6,7},{7,6},{8,9},{9,8},{10,11... | collective-permute-start | bytes 884744 | tf_op jit(solution)/shard_map/ppermute | solution.py:328

commit v6 on v5

--- a/solution.py
+++ b/solution.py
@@ -80,7 +80,7 @@
     kinds = table_ref.shape[0]
     per_group = side // kinds
     me = lax.axis_index("tile")
-    tables = jnp.concatenate([gathered_ref[band, base:, :] for band in range(tiles)], axis=0)
+    tables = jnp.concatenate([gathered_ref[base:, band * side : (band + 1) * side] for band in range(tiles)], axis=0)
     ints[: tiles * rows, :] = tables.astype(F32).astype(jnp.int32)
     copy = pltpu.make_async_copy(ints.at[pl.ds(0, tiles * rows), :], scalars, sem)
     copy.start()
@@ -101,7 +101,7 @@
     def block_of(owner, slot):
         band = slot // cap
         local = scalars[band * rows + 2 * taps + owner, slot % cap]
-        return gathered_ref[band, pl.ds(pl.multiple_of(local * chans, chans), chans), :]
+        return gathered_ref[pl.ds(pl.multiple_of(local * chans, chans), chans), pl.ds(pl.multiple_of(band * side, side), side)]
 
     for slot in range(count):
         out_ref[slot * chans : (slot + 1) * chans, :] = block_of(me, slot)
@@ -307,7 +307,7 @@
         slots, weights, in_hbm(send_list), in_hbm(neighbour_tile), in_hbm(neighbour_edge), in_hbm(source),
         in_hbm(remap_table), filters,
     )
-    gathered = lax.all_gather(packed, "tile")
+    gathered = lax.all_gather(packed, "tile", axis=1, tiled=True)
     mine = pl.pallas_call(
         functools.partial(edge_kernel, (side, chans, blocks, tiles, cap, taps, rows)),
         out_shape=jax.ShapeDtypeStruct(((count + 4) * chans, side), BF16),

time: 44.7 us -> 44.4 us (level); the launches traced: 44.5 us -> 44.7 us
  Pallas kernels: 23.6 us -> 24.4 us
  blocking collectives: 17.5 us -> 17 us
    pallas_call x1, Pallas kernels: 3.04 us -> 3.78 us  [body(): pl.pallas_call(functools.partial(edge_kernel, (side, chans, blocks, tiles...]
    all_gather x1, blocking collectives: 17.5 us -> 17 us  [body(): gathered = lax.all_gather(packed, 'tile', axis=1, tiled=True)]
where the time goes in v6:
time: 44.4 us; the launch traced here: 44.7 us
  Pallas kernels  24.4 us (55%)
  blocking collectives  17 us (38%)
  starting transfers between devices  1.91 us (4%)
  waiting for transfers between devices  1.37 us (3%)
    all_gather x1, blocking collectives, body(): gathered = lax.all_gather(packed, 'tile', axis=1, tiled=True)  17 us
    pallas_call x1, Pallas kernels, body(): pl.pallas_call(functools.partial(tile_kernel, dims, True, many), out_shap...  10.3 us
    pallas_call x1, Pallas kernels, body(): pl.pallas_call(functools.partial(tile_kernel, dims, False, many), out_sha...  8.3 us
    pallas_call x1, Pallas kernels, body(): pl.pallas_call(functools.partial(edge_kernel, (side, chans, blocks, tiles...  3.78 us
    ppermute x3, starting transfers between devices, swap(): return lax.ppermute(value, 'chan', [(i, i ^ flip) for i in range(parts)])  1.91 us
    pallas_call x1, Pallas kernels, body(): pl.pallas_call(pack_kernel, out_shape=[jax.ShapeDtypeStruct((blocks * cha...  1.62 us
    ppermute x3, waiting for transfers between devices, swap(): return lax.ppermute(value, 'chan', [(i, i ^ flip) for i in range(parts)])  1.37 us
  transfers between devices with their start and end apart: 3, of which 1 were waited for; matrix products, arithmetic and copies ran while one was open for 0% of the time, Pallas kernels for 19%

profile of v6, /device:TPU:0, one launch (start us, length us, event | category | flops | bytes accessed | tf_op | source)
XLA Modules:
  0.0 44.7 jit_solution(13580887638783549039)
XLA Ops:
  0.0 1.6 %pack.1 = (bf16[528,128]{1,0:T(8,128)(2,1)S(1)}, s32[6,128]{1,0:T(8,128)S(1)}, s32[6,128]{1,0:T(8,128)S(1)}, bf16[32,128,128]{2,1,0:T(8,128)(2,1)S(1)}, bf16[3,3,64,128]{3,2,1,0:T(8,128)(2,1)S(1)}) custom-call(s32[6,128]{1,0:T(8,128)} %bitcast.12, s32[6,128]{1,0:T(8,128)} %bitcast.13, s32[1,4,8]{2,1,0:T(4,128)} %lists_hbm.1, s32[1,4]{1,0:T(1,128)} %neigh_hbm.1, ...), custom_call_target="tpu_custom_call" | custom-call | tf_op jit(solution)/shard_map/pack/pallas_call | solution.py:287
  1.6 17.0 %all_gather.3.gathered_ref = bf16[528,512]{1,0:T(8,128)(2,1)S(1)} all-gather(bf16[528,128]{1,0:T(8,128)(2,1)S(1)} %get-tuple-element.18), channel_id=1, replica_groups=mesh['group'=2,'tile'=4,'chan'=4] {'tile'}, dimensions={1}, use_global_device_ids=true | all-gather | bytes 675840 | tf_op jit(solution)/shard_map/all_gather | solution.py:310
  18.6 3.8 %edges.1 = bf16[1152,128]{1,0:T(8,128)(2,1)S(1)} custom-call(bf16[528,512]{1,0:T(8,128)(2,1)S(1)} %all_gather.3.gathered_ref, bf16[32,128,128]{2,1,0:T(8,128)(2,1)S(1)} %get-tuple-element.19.table_ref.refs_4_.refs_5_), custom_call_target="tpu_custom_call" | custom-call | tf_op jit(solution)/shard_map/edges/pallas_call | solution.py:311
  22.4 0.1 collective-permute-start.1
  22.5 0.4 filters.1
  22.9 1.6 %collective-permute-start = (bf16[1152,128]{1,0:T(8,128)(2,1)S(1)}, bf16[1152,128]{1,0:T(8,128)(2,1)S(1)}, u32[]{:S(2)}, u32[]{:S(2)}) collective-permute-start(bf16[1152,128]{1,0:T(8,128)(2,1)S(1)} %edges.1), channel_id=1, source_target_pairs={{0,2},{1,3},{2,0},{3,1},{4,6},{5,7},{6,4},{7,5},{8,10},{9,11},{10,... | collective-permute-start | bytes 884744 | tf_op jit(solution)/shard_map/ppermute | solution.py:328
  24.4 0.0 collective-permute-done.1
  24.4 8.3 %near.1.refs_2_ = f32[130,64,128]{2,1,0:T(8,128)S(1)} custom-call(bf16[36,32,128]{2,1,0:T(8,128)(2,1)S(1)} %bitcast.7, bf16[36,32,128]{2,1,0:T(8,128)(2,1)S(1)} %bitcast.9, s32[6,128]{1,0:T(8,128)S(1)} %get-tuple-element.25.refs_2_.refs_3_, s32[6,128]{1,0:T(8,128)S(1)} %get-tuple-element.26.refs_3_.refs_4_, ...), custom_call_target="tpu_custom_call" | custom-call | flops 2818572288 | bytes 4259840 | tf_op jit(solution)/shard_map/near/pallas_call | solution.py:359
  32.7 0.0 collective-permute-done
  32.7 0.3 collective-permute-start.2
  33.0 1.4 %collective-permute-done.2 = bf16[1152,128]{1,0:T(8,128)(2,1)S(1)} collective-permute-done((bf16[1152,128]{1,0:T(8,128)(2,1)S(1)}, bf16[1152,128]{1,0:T(8,128)(2,1)S(1)}, u32[]{:S(2)}, u32[]{:S(2)}) %collective-permute-start.2) | collective-permute-done | bytes 294944 | tf_op jit(solution)/shard_map/ppermute | solution.py:328
  34.4 10.3 %far.1 = bf16[64,128,128]{2,1,0:T(8,128)(2,1)} custom-call(bf16[36,32,128]{2,1,0:T(8,128)(2,1)S(1)} %bitcast.8, bf16[36,32,128]{2,1,0:T(8,128)(2,1)S(1)} %bitcast.10, f32[130,64,128]{2,1,0:T(8,128)S(1)} %near.1.refs_2_, s32[6,128]{1,0:T(8,128)S(1)} %get-tuple-element.25.refs_2_.refs_3_, s32[6,128]{1,0:T(8,128)S(1)} %get-tuple-element.26.refs_3_.refs_4_, ...), custom_call_target="tpu_custom_call" | custom-call | flops 2818572288 | bytes 4259840 | tf_op jit(solution)/shard_map/far/pallas_call | solution.py:371
Async XLA Ops:
  22.4 2.0 %collective-permute-start.1 = (bf16[1152,128]{1,0:T(8,128)(2,1)S(1)}, bf16[1152,128]{1,0:T(8,128)(2,1)S(1)}, u32[]{:S(2)}, u32[]{:S(2)}) collective-permute-start(bf16[1152,128]{1,0:T(8,128)(2,1)S(1)} %edges.1), channel_id=1, source_target_pairs={{0,1},{1,0},{2,3},{3,2},{4,5},{5,4},{6,7},{7,6},{8,9},{9,8},{10,11... | collective-permute-start | bytes 884744 | tf_op jit(solution)/shard_map/ppermute | solution.py:328
  22.9 9.9 %collective-permute-start = (bf16[1152,128]{1,0:T(8,128)(2,1)S(1)}, bf16[1152,128]{1,0:T(8,128)(2,1)S(1)}, u32[]{:S(2)}, u32[]{:S(2)}) collective-permute-start(bf16[1152,128]{1,0:T(8,128)(2,1)S(1)} %edges.1), channel_id=1, source_target_pairs={{0,2},{1,3},{2,0},{3,1},{4,6},{5,7},{6,4},{7,5},{8,10},{9,11},{10,... | collective-permute-start | bytes 884744 | tf_op jit(solution)/shard_map/ppermute | solution.py:328
  32.7 1.6 %collective-permute-start.2 = (bf16[1152,128]{1,0:T(8,128)(2,1)S(1)}, bf16[1152,128]{1,0:T(8,128)(2,1)S(1)}, u32[]{:S(2)}, u32[]{:S(2)}) collective-permute-start(bf16[1152,128]{1,0:T(8,128)(2,1)S(1)} %collective-permute-done), channel_id=1, source_target_pairs={{0,1},{1,0},{2,3},{3,2},{4,5},{5,4},{6,7},{7,6},{8,9},{9,8},{10,11... | collective-permute-start | bytes 884744 | tf_op jit(solution)/shard_map/ppermute | solution.py:328

commit v7 on v6

--- a/solution.py
+++ b/solution.py
@@ -151,124 +151,185 @@
             out_ref[dest, :] = (acc[:chans] + acc[chans:]).astype(BF16)
 
 
-def filter_kernel(chans, filters, near_ref, far_ref):
+def filter_kernel(chans, filters, partner_filters, near_ref, far_ref):
     outs, all_chans = filters.shape[2:]
     half = all_chans // 2
     me = lax.axis_index("chan")
     lane = lax.broadcasted_iota(jnp.int32, (outs, all_chans), 1)
-    for b in range(3):
-        first, second = [], []
-        for a in range(3):
-            value = filters[a, b].astype(F32)
-            width = chans
-            bit = 1
-            while width < all_chans:
-                other = jnp.where(
-                    lane // width % 2 == 0, pltpu.roll(value, all_chans - width, 1), pltpu.roll(value, width, 1)
-                )
-                value = jnp.where((me & bit) != 0, other, value)
-                width *= 2
-                bit *= 2
-            first.append(value)
-            second.append(pltpu.roll(value, half, 1))
-        at = slice(b * outs, (b + 1) * outs)
-        near_ref[at, :all_chans] = jnp.where(lane < half, first[0], second[1]).astype(BF16)
-        near_ref[at, all_chans:] = first[2][:, :half].astype(BF16)
-        far_ref[at, :all_chans] = jnp.where(lane < half, second[0], first[1]).astype(BF16)
-        far_ref[at, all_chans:] = second[2][:, :half].astype(BF16)
-
-
-def tile_kernel(dims, last, many, *refs):
-    side, chans, cap, tiles, all_chans, outs = dims
+    for n, source in enumerate([partner_filters, filters]):
+        for b in range(3):
+            first, second = [], []
+            for a in range(3):
+                value = source[a, b].astype(F32)
+                width = chans
+                bit = 1
+                while width < all_chans:
+                    other = jnp.where(
+                        lane // width % 2 == 0, pltpu.roll(value, all_chans - width, 1), pltpu.roll(value, width, 1)
+                    )
+                    value = jnp.where((me & bit) != 0, other, value)
+                    width *= 2
+                    bit *= 2
+                first.append(value)
+                second.append(pltpu.roll(value, half, 1))
+            at = slice((3 * n + b) * outs, (3 * n + b + 1) * outs)
+            near_ref[at, :all_chans] = jnp.where(lane < half, first[0], second[1]).astype(BF16)
+            near_ref[at, all_chans:] = first[2][:, :half].astype(BF16)
+            far_ref[at, :all_chans] = jnp.where(lane < half, second[0], first[1]).astype(BF16)
+            far_ref[at, all_chans:] = second[2][:, :half].astype(BF16)
+
+
+class Remap:
+    def __init__(self, dims, parts, slots_ref, weights_ref, table_ref, slots, weights, image, sems):
+        self.side, self.chans, self.cap, self.tiles, self.outs = dims
+        self.parts, self.table, self.slots, self.weights, self.image = parts, table_ref, slots, weights, image
+        self.half = self.chans * len(parts)
+        self.rows = self.side // 2
+        self.count = self.tiles * self.cap
+        self.lower = lax.rem(lax.axis_index("chan"), 2)
+        self.copies = start_all(sems, [(slots_ref, slots), (weights_ref, weights)])
+
+    def channels(self, index):
+        return jnp.concatenate([part[index] for part in self.parts], axis=0)
+
+    def around(self, edge):
+        value = self.channels(self.count + edge).astype(F32)
+        wide = lax.broadcasted_iota(jnp.int32, value.shape, 1)
+        before = jnp.where(wide == 0, 0.0, pltpu.roll(value, 1, 1))
+        after = jnp.where(wide == self.side - 1, 0.0, pltpu.roll(value, self.side - 1, 1))
+        return jnp.concatenate([before, value, after], axis=0).astype(BF16)
+
+    def row(self, at):
+        taps = self.slots.shape[0]
+        r = jnp.clip(self.lower * self.rows + at - 1, 0, self.side - 1)
+        lhs = jnp.concatenate([self.channels(self.slots[k, r]) for k in range(taps)], axis=1)
+        rhs = jnp.concatenate([self.table[self.weights[k, r]] for k in range(taps)], axis=0)
+        return dot(lhs, rhs).astype(BF16)
+
+    def run(self, convolve):
+        for copy in self.copies:
+            copy.wait()
+        half, image = self.half, self.image
+        image[0:half, :] = jnp.where(self.lower == 0, self.channels(self.count), self.row(0))
+        for at in range(1, STEP + 2):
+            image[at * half : (at + 1) * half, :] = self.row(at)
+
+        def step(t, carry):
+            first = t * STEP
+            convolve(first)
+            for u in range(STEP):
+                at = first + STEP + 2 + u
+                image[pl.ds(pl.multiple_of(at * half, half), half), :] = self.row(at)
+            return carry
+
+        lax.fori_loop(0, self.rows // STEP - 1, step, 0)
+        end = slice((self.rows + 1) * half, (self.rows + 2) * half)
+        image[end, :] = jnp.where(self.lower == 1, self.channels(self.count + 1), image[end, :])
+        convolve(self.rows - STEP)
+
+
+def convolve_step(outs, matrix, image, first, left, right, emit):
+    half = matrix.shape[1] // 3
+    side = image.shape[1]
+    lane = lax.broadcasted_iota(jnp.int32, (outs, side), 1)
+    ys = []
+    for u in range(0, STEP, 2):
+        x0 = image[pl.ds(pl.multiple_of((first + u) * half, half), 3 * half), :]
+        x1 = image[pl.ds(pl.multiple_of((first + u + 1) * half, half), 3 * half), :]
+        ys.append(dot(matrix, jnp.concatenate([x0, x1], axis=1)))
+    for u in range(STEP):
+        for n in range(matrix.shape[0] // (3 * outs)):
+            y = ys[u // 2][3 * n * outs : 3 * (n + 1) * outs, u % 2 * side : (u % 2 + 1) * side]
+            from_left = jnp.where(lane == 0, left(first + u), pltpu.roll(y[:outs], 1, 1))
+            from_right = jnp.where(lane == side - 1, right(first + u), pltpu.roll(y[2 * outs :], side - 1, 1))
+            emit(n, u, y[outs : 2 * outs] + from_left + from_right)
+
+
+def near_kernel(dims, many, *refs):
     parts = refs[:many]
-    refs = refs[many:]
-    if last:
-        before_ref, *refs = refs
-    slots_ref, weights_ref, table_ref, matrix, out_ref, slots, weights, image, *refs = refs
-    if last:
-        spread, staged, out_sems, sems = refs
-    else:
-        (sems,) = refs
-    taps = slots.shape[0]
-    count = tiles * cap
-    half = chans * many
-    copies = start_all(sems, [(slots_ref, slots), (weights_ref, weights)])
-
-    def channels(index):
-        return jnp.concatenate([part[index] for part in parts], axis=0)
-
-    image[0:half, :] = channels(count)
-    image[(side + 1) * half :, :] = channels(count + 1)
-    wide = lax.broadcasted_iota(jnp.int32, (half, side), 1)
-
-    def around(edge):
-        value = channels(count + edge).astype(F32)
-        before = jnp.where(wide == 0, 0.0, pltpu.roll(value, 1, 1))
-        after = jnp.where(wide == side - 1, 0.0, pltpu.roll(value, side - 1, 1))
-        return jnp.concatenate([before, value, after], axis=0).astype(BF16)
-
-    left = dot(matrix[0:outs, :], around(2))
-    right = dot(matrix[2 * outs :, :], around(3))
-    if last:
-        left = left + before_ref[side]
-        right = right + before_ref[side + 1]
-    else:
-        out_ref[side] = left
-        out_ref[side + 1] = right
+    slots_ref, weights_ref, table_ref, matrix, sums_ref, ends_ref, slots, weights, image, sems = refs[many:]
+    work = Remap(dims, parts, slots_ref, weights_ref, table_ref, slots, weights, image, sems)
+    outs = work.outs
+    for n in range(2):
+        ends_ref[n, 0] = dot(matrix[3 * n * outs : (3 * n + 1) * outs, :], work.around(2))
+        ends_ref[n, 1] = dot(matrix[(3 * n + 2) * outs : (3 * n + 3) * outs, :], work.around(3))
+
+    def convolve(first):
+        def emit(n, u, total):
+            sums_ref[first + u, n] = total
+
+        convolve_step(outs, matrix[...], image, first, lambda i: 0.0, lambda i: 0.0, emit)
+
+    work.run(convolve)
+
+
+def finish_step(outs, matrix, image, first, base, ends, sums_ref, n, spread, dest):
+    side = image.shape[1]
+
+    def left(i):
+        return pltpu.roll(ends[0], lax.rem(side - (base + i), side), 1)
+
+    def right(i):
+        return pltpu.roll(ends[1], side - 1 - (base + i), 1)
+
+    def emit(_, u, total):
+        spread[pl.ds(u * (outs + 1), outs), :] = total + sums_ref[first + u, n]
+
+    convolve_step(outs, matrix, image, first, left, right, emit)
+    rows = pl.ds(pl.multiple_of(first, STEP), STEP)
+    for o in range(outs):
+        dest[o, rows, :] = spread[pl.ds(o, STEP, stride=outs + 1), :].astype(BF16)
+
+
+def far_kernel(dims, many, *refs):
+    parts = refs[:many]
+    (
+        slots_ref, weights_ref, table_ref, matrix, sums_ref, ends_ref,
+        done_ref, image, own_ends_ref, slots, weights, spread, sems,
+    ) = refs[many:]
+    work = Remap(dims, parts, slots_ref, weights_ref, table_ref, slots, weights, image, sems)
+    outs = work.outs
+    base = work.lower * work.rows
+    ends = []
+    for n in range(2):
+        ends.append([
+            ends_ref[n, 0] + dot(matrix[3 * n * outs : (3 * n + 1) * outs, :], work.around(2)),
+            ends_ref[n, 1] + dot(matrix[(3 * n + 2) * outs : (3 * n + 3) * outs, :], work.around(3)),
+        ])
+    own_ends_ref[0] = ends[1][0]
+    own_ends_ref[1] = ends[1][1]
+
+    def convolve(first):
+        finish_step(outs, matrix[: 3 * outs, :], image, first, base, ends[0], sums_ref, 0, spread, done_ref)
+
+    work.run(convolve)
+
+
+def own_kernel(dims, steps, *refs):
+    side, chans, cap, tiles, outs = dims
+    rows = side // 2
+    image, matrix, sums_ref, ends_ref, *refs = refs
+    received = None
+    if len(refs) > 4:
+        received, _, *refs = refs
+    out_hbm, spread, staged, sems = refs
+    lower = lax.rem(lax.axis_index("chan"), 2)
+    base = lower * rows
+    copies = []
+    if received is not None:
+        there = pl.ds(pl.multiple_of((1 - lower) * rows, rows), rows)
+        copies.append(pltpu.make_async_copy(received, out_hbm.at[:, there, :], sems.at[len(steps)]))
+        copies[0].start()
+    for n, step in enumerate(steps):
+        first = step * STEP
+        finish_step(
+            outs, matrix[3 * outs :, :], image, first, base, [ends_ref[0], ends_ref[1]], sums_ref, 1, spread, staged
+        )
+        to = pl.ds(pl.multiple_of(base + first, STEP), STEP)
+        copies.append(pltpu.make_async_copy(staged.at[:, pl.ds(first, STEP), :], out_hbm.at[:, to, :], sems.at[n]))
+        copies[-1].start()
     for copy in copies:
         copy.wait()
-
-    def remap(r):
-        lhs = jnp.concatenate([channels(slots[k, r]) for k in range(taps)], axis=1)
-        rhs = jnp.concatenate([table_ref[weights[k, r]] for k in range(taps)], axis=0)
-        return dot(lhs, rhs).astype(BF16)
-
-    def place(r, value):
-        image[pl.ds(pl.multiple_of((r + 1) * half, half), half), :] = value
-
-    lane = lax.broadcasted_iota(jnp.int32, (outs, side), 1)
-
-    def convolve(first):
-        ys = []
-        for u in range(0, STEP, 2):
-            x0 = image[pl.ds(pl.multiple_of((first + u) * half, half), 3 * half), :]
-            x1 = image[pl.ds(pl.multiple_of((first + u + 1) * half, half), 3 * half), :]
-            ys.append(dot(matrix[...], jnp.concatenate([x0, x1], axis=1)))
-        for u in range(STEP):
-            i = first + u
-            y = ys[u // 2][:, u % 2 * side : (u % 2 + 1) * side]
-            at_left = pltpu.roll(left, lax.rem(side - i, side), 1) if last else 0.0
-            at_right = pltpu.roll(right, side - 1 - i, 1) if last else 0.0
-            from_left = jnp.where(lane == 0, at_left, pltpu.roll(y[:outs], 1, 1))
-            from_right = jnp.where(lane == side - 1, at_right, pltpu.roll(y[2 * outs :], side - 1, 1))
-            total = y[outs : 2 * outs] + from_left + from_right
-            if last:
-                spread[pl.ds(u * (outs + 1), outs), :] = total + before_ref[i]
-            else:
-                out_ref[i] = total
-        if last:
-            rows = pl.ds(pl.multiple_of(first, STEP), STEP)
-            for o in range(outs):
-                staged[o, rows, :] = spread[pl.ds(o, STEP, stride=outs + 1), :].astype(BF16)
-            pltpu.make_async_copy(staged.at[:, rows, :], out_ref.at[:, rows, :], out_sems.at[first // STEP]).start()
-
-    for r in range(STEP + 1):
-        place(r, remap(r))
-
-    def step(t, carry):
-        first = t * STEP
-        convolve(first)
-        for u in range(STEP):
-            r = jnp.minimum(first + STEP + 1 + u, side - 1)
-            place(r, remap(r))
-        return carry
-
-    lax.fori_loop(0, side // STEP - 1, step, 0)
-    convolve(side - STEP)
-    if last:
-        for t in range(side // STEP):
-            rows = pl.ds(t * STEP, STEP)
-            pltpu.make_async_copy(staged.at[:, rows, :], out_ref.at[:, rows, :], out_sems.at[t]).wait()
 
 
 def body(source, send_list, block_slot, weight_index, remap_table, neighbour_tile, neighbour_edge, conv_weight):
@@ -307,6 +368,17 @@
         slots, weights, in_hbm(send_list), in_hbm(neighbour_tile), in_hbm(neighbour_edge), in_hbm(source),
         in_hbm(remap_table), filters,
     )
+    def swap(value, flip):
+        return lax.ppermute(value, "chan", [(i, i ^ flip) for i in range(parts)])
+
+    def spread(held, bit):
+        while bit:
+            for flip in list(held):
+                held[flip ^ bit] = swap(held[flip], bit)
+            bit //= 2
+        return [held[f].reshape(count + 4, chans, side) for f in sorted(held)]
+
+    partner_filters = swap(filters, 1)
     gathered = lax.all_gather(packed, "tile", axis=1, tiled=True)
     mine = pl.pallas_call(
         functools.partial(edge_kernel, (side, chans, blocks, tiles, cap, taps, rows)),
@@ -324,66 +396,85 @@
         name="edges",
     )(gathered, table)
 
-    def swap(value, flip):
-        return lax.ppermute(value, "chan", [(i, i ^ flip) for i in range(parts)])
-
-    def spread(held, bit):
-        while bit:
-            for flip in list(held):
-                held[flip ^ bit] = swap(held[flip], bit)
-            bit //= 2
-        return [held[f].reshape(count + 4, chans, side) for f in sorted(held)]
-
     many = parts // 2
     half = all_chans // 2
-    mine, filters = lax.optimization_barrier((mine, filters))
+    mine, filters, partner_filters = lax.optimization_barrier((mine, filters, partner_filters))
     near = spread({0: mine}, many // 2)
-    near_filters, far_filters = pl.pallas_call(
+    near_matrix, far_matrix = pl.pallas_call(
         functools.partial(filter_kernel, chans),
-        out_shape=[jax.ShapeDtypeStruct((3 * outs, 3 * half), BF16)] * 2,
-        in_specs=[VMEM],
+        out_shape=[jax.ShapeDtypeStruct((6 * outs, 3 * half), BF16)] * 2,
+        in_specs=[VMEM] * 2,
         out_specs=[VMEM] * 2,
         compiler_params=params,
         name="filters",
-    )(filters)
-    mine, near_filters = lax.optimization_barrier((mine, near_filters))
+    )(filters, partner_filters)
+    mine, near_matrix = lax.optimization_barrier((mine, near_matrix))
     across = swap(mine, many)
-    dims = (side, chans, cap, tiles, all_chans, outs)
-    scratch = [
-        pltpu.SMEM(slots.shape, jnp.int32),
-        pltpu.SMEM(weights.shape, jnp.int32),
-        pltpu.VMEM(((side + 2) * half, side), BF16),
-    ]
-    flops = 2 * side * half * taps * side * side + 2 * side * side * 9 * half * outs
-    cost = pl.CostEstimate(flops=flops, bytes_accessed=(side + 2) * outs * side * 4, transcendentals=0)
-    so_far = pl.pallas_call(
-        functools.partial(tile_kernel, dims, False, many),
-        out_shape=jax.ShapeDtypeStruct((side + 2, outs, side), F32),
+    dims = (side, chans, cap, tiles, outs)
+    half_rows = side // 2
+    image_shape = ((half_rows + 2) * half, side)
+    scratch = [pltpu.SMEM(slots.shape, jnp.int32), pltpu.SMEM(weights.shape, jnp.int32)]
+    turning = pltpu.VMEM((round_up(STEP * (outs + 1), 8), side), F32)
+    remap_flops = 2 * half_rows * half * taps * side * side
+    conv_flops = 2 * half_rows * side * 9 * half * outs
+
+    def cost(flops):
+        return pl.CostEstimate(flops=flops, bytes_accessed=side * outs * side * 4, transcendentals=0)
+
+    sums, ends = pl.pallas_call(
+        functools.partial(near_kernel, dims, many),
+        out_shape=[
+            jax.ShapeDtypeStruct((half_rows, 2, outs, side), F32),
+            jax.ShapeDtypeStruct((2, 2, outs, side), F32),
+        ],
         in_specs=[VMEM] * (many + 4),
-        out_specs=VMEM,
-        scratch_shapes=scratch + [pltpu.SemaphoreType.DMA((2,))],
-        compiler_params=params,
-        cost_estimate=cost,
+        out_specs=[VMEM] * 2,
+        scratch_shapes=scratch + [pltpu.VMEM(image_shape, BF16), pltpu.SemaphoreType.DMA((2,))],
+        compiler_params=params,
+        cost_estimate=cost(remap_flops + 2 * conv_flops),
         name="near",
-    )(*near, slots, weights, table, near_filters)
-    across, so_far = lax.optimization_barrier((across, so_far))
+    )(*near, slots, weights, table, near_matrix)
+    across, sums = lax.optimization_barrier((across, sums))
     far = spread({many: across}, many // 2)
+    done, image, own_ends = pl.pallas_call(
+        functools.partial(far_kernel, dims, many),
+        out_shape=[
+            jax.ShapeDtypeStruct((outs, half_rows, side), BF16),
+            jax.ShapeDtypeStruct(image_shape, BF16),
+            jax.ShapeDtypeStruct((2, outs, side), F32),
+        ],
+        in_specs=[VMEM] * (many + 6),
+        out_specs=[VMEM] * 3,
+        scratch_shapes=scratch + [turning, pltpu.SemaphoreType.DMA((2,))],
+        compiler_params=params,
+        cost_estimate=cost(remap_flops + conv_flops),
+        name="far",
+    )(*far, slots, weights, table, far_matrix, sums, ends)
+    received = swap(done, 1)
+    steps = list(range(half_rows // STEP))
+    shared = (image, far_matrix, sums, own_ends)
+    last_scratch = [turning, pltpu.VMEM((outs, half_rows, side), BF16), pltpu.SemaphoreType.DMA((len(steps) + 1,))]
+    begun = pl.pallas_call(
+        functools.partial(own_kernel, dims, steps[:-1]),
+        out_shape=jax.ShapeDtypeStruct((outs, side, side), BF16),
+        in_specs=[VMEM] * 4,
+        out_specs=HBM,
+        scratch_shapes=last_scratch,
+        compiler_params=params,
+        cost_estimate=cost(conv_flops),
+        name="own",
+    )(*shared)
     return pl.pallas_call(
-        functools.partial(tile_kernel, dims, True, many),
+        functools.partial(own_kernel, dims, steps[-1:]),
         out_shape=jax.ShapeDtypeStruct((outs, side, side), BF16),
-        in_specs=[VMEM] * (many + 5),
+        in_specs=[VMEM] * 5 + [HBM],
         out_specs=HBM,
-        scratch_shapes=scratch
-        + [
-            pltpu.VMEM((round_up(STEP * (outs + 1), 8), side), F32),
-            pltpu.VMEM((outs, side, side), BF16),
-            pltpu.SemaphoreType.DMA((side // STEP,)),
-            pltpu.SemaphoreType.DMA((2,)),
-        ],
-        compiler_params=params,
-        cost_estimate=cost,
-        name="far",
-    )(*far, so_far, slots, weights, table, far_filters)
+        scratch_shapes=last_scratch,
+        input_output_aliases={5: 0},
+        compiler_params=params,
+        cost_estimate=cost(conv_flops // 4),
+        name="last",
+    )(*shared, received, begun)
 
 
 def solution(mesh):

time: 44.4 us -> 45.5 us (1.025); the launches traced: 44.7 us -> 44.9 us
  Pallas kernels: 24.4 us -> 21.4 us
  waiting for transfers between devices: 1.37 us -> 3.9 us
    pallas_call x2 -> x4, Pallas kernels: 18.6 us -> 15.2 us  [the longest x1 5.59 us: body(): pl.pallas_call(functools.partial(near_kernel, dims, many), out_shape=[jax...]
    ppermute x3 -> x5, waiting for transfers between devices: 1.37 us -> 3.9 us  [swap(): return lax.ppermute(value, 'chan', [(i, i ^ flip) for i in range(parts)])]
    pallas_call x1, Pallas kernels: 0.36 us -> 1.63 us  [body(): pl.pallas_call(functools.partial(filter_kernel, chans), out_shape=[jax.Sh...]
    pallas_call x1, Pallas kernels: 3.78 us -> 2.95 us  [body(): pl.pallas_call(functools.partial(edge_kernel, (side, chans, blocks, tiles...]
    ppermute x3 -> x5, starting transfers between devices: 1.91 us -> 2.35 us  [swap(): return lax.ppermute(value, 'chan', [(i, i ^ flip) for i in range(parts)])]
  transfers between devices with their start and end apart: 3 -> 5, of which waited for: 1 -> 2; matrix products, arithmetic and copies ran while one was open for 0% -> 0% of each run, Pallas kernels for 19% -> 29%
where the time goes in v7:
time: 45.5 us; the launch traced here: 44.9 us
  Pallas kernels  21.4 us (47%)
  blocking collectives  17.1 us (38%)
  waiting for transfers between devices  3.9 us (9%)
  starting transfers between devices  2.35 us (5%)
    all_gather x1, blocking collectives, body(): gathered = lax.all_gather(packed, 'tile', axis=1, tiled=True)  17.1 us
    pallas_call x1, Pallas kernels, body(): pl.pallas_call(functools.partial(near_kernel, dims, many), out_shape=[jax...  5.59 us
    pallas_call x1, Pallas kernels, body(): pl.pallas_call(functools.partial(far_kernel, dims, many), out_shape=[jax....  5.26 us
    ppermute x5, waiting for transfers between devices, swap(): return lax.ppermute(value, 'chan', [(i, i ^ flip) for i in range(parts)])  3.9 us
    pallas_call x1, Pallas kernels, body(): pl.pallas_call(functools.partial(edge_kernel, (side, chans, blocks, tiles...  2.95 us
    pallas_call x1, Pallas kernels, body(): pl.pallas_call(functools.partial(own_kernel, dims, steps[:-1]), out_shape...  2.69 us
    ppermute x5, starting transfers between devices, swap(): return lax.ppermute(value, 'chan', [(i, i ^ flip) for i in range(parts)])  2.35 us
    pallas_call x1, Pallas kernels, body(): pl.pallas_call(functools.partial(own_kernel, dims, steps[-1:]), out_shape...  1.71 us
  transfers between devices with their start and end apart: 5, of which 2 were waited for; matrix products, arithmetic and copies ran while one was open for 0% of the time, Pallas kernels for 29%

profile of v7, /device:TPU:0, one launch (start us, length us, event | category | flops | bytes accessed | tf_op | source)
XLA Modules:
  0.0 44.9 jit_solution(2266963819341951821)
XLA Ops:
  0.0 1.6 %pack.1 = (bf16[528,128]{1,0:T(8,128)(2,1)S(1)}, s32[6,128]{1,0:T(8,128)S(1)}, s32[6,128]{1,0:T(8,128)S(1)}, bf16[32,128,128]{2,1,0:T(8,128)(2,1)S(1)}, bf16[3,3,64,128]{3,2,1,0:T(8,128)(2,1)S(1)}) custom-call(s32[6,128]{1,0:T(8,128)} %bitcast.12, s32[6,128]{1,0:T(8,128)} %bitcast.13, s32[1,4,8]{2,1,0:T(4,128)} %lists_hbm.1, s32[1,4]{1,0:T(1,128)} %neigh_hbm.1, ...), custom_call_target="tpu_custom_call" | custom-call | tf_op jit(solution)/shard_map/pack/pallas_call | solution.py:348
  1.6 0.5 %collective-permute-start = (bf16[3,3,64,128]{3,2,1,0:T(8,128)(2,1)S(1)}, bf16[3,3,64,128]{3,2,1,0:T(8,128)(2,1)S(1)}, u32[]{:S(2)}, u32[]{:S(2)}) collective-permute-start(bf16[3,3,64,128]{3,2,1,0:T(8,128)(2,1)S(1)} %get-tuple-element.28.filters), channel_id=1, source_target_pairs={{0,1},{1,0},{2,3},{3,2},{4,5},{5,4},{6,7},{7,6},{8,9},{9,8},{10,11... | collective-permute-start | bytes 442376 | tf_op jit(solution)/shard_map/ppermute | solution.py:372
  2.1 17.1 %all_gather.3.gathered_ref = bf16[528,512]{1,0:T(8,128)(2,1)S(1)} all-gather(bf16[528,128]{1,0:T(8,128)(2,1)S(1)} %get-tuple-element.24), channel_id=1, replica_groups=mesh['group'=2,'tile'=4,'chan'=4] {'tile'}, dimensions={1}, use_global_device_ids=true | all-gather | bytes 675840 | tf_op jit(solution)/shard_map/all_gather | solution.py:382
  19.3 2.9 %edges.1 = bf16[1152,128]{1,0:T(8,128)(2,1)S(1)} custom-call(bf16[528,512]{1,0:T(8,128)(2,1)S(1)} %all_gather.3.gathered_ref, bf16[32,128,128]{2,1,0:T(8,128)(2,1)S(1)} %get-tuple-element.25.table_ref.refs_4_), custom_call_target="tpu_custom_call" | custom-call | tf_op jit(solution)/shard_map/edges/pallas_call | solution.py:383
  22.2 0.0 collective-permute-done.partner_filters
  22.2 0.1 collective-permute-start.2
  22.3 1.6 %filters.1 = (bf16[384,192]{1,0:T(8,128)(2,1)S(1)}, bf16[384,192]{1,0:T(8,128)(2,1)S(1)}) custom-call(bf16[3,3,64,128]{3,2,1,0:T(8,128)(2,1)S(1)} %get-tuple-element.28.filters, bf16[3,3,64,128]{3,2,1,0:T(8,128)(2,1)S(1)} %collective-permute-done.partner_filters), custom_call_target="tpu_custom_call" | custom-call | tf_op jit(solution)/shard_map/filters/pallas_call | solution.py:403
  23.9 1.6 %collective-permute-start.1 = (bf16[1152,128]{1,0:T(8,128)(2,1)S(1)}, bf16[1152,128]{1,0:T(8,128)(2,1)S(1)}, u32[]{:S(2)}, u32[]{:S(2)}) collective-permute-start(bf16[1152,128]{1,0:T(8,128)(2,1)S(1)} %edges.1), channel_id=1, source_target_pairs={{0,2},{1,3},{2,0},{3,1},{4,6},{5,7},{6,4},{7,5},{8,10},{9,11},{10,... | collective-permute-start | bytes 884744 | tf_op jit(solution)/shard_map/ppermute | solution.py:372
  25.5 0.0 collective-permute-done.2
  25.5 5.6 %near.1 = (f32[64,2,64,128]{3,2,1,0:T(8,128)S(1)}, f32[2,2,64,128]{3,2,1,0:T(8,128)S(1)}) custom-call(bf16[36,32,128]{2,1,0:T(8,128)(2,1)S(1)} %bitcast.9, bf16[36,32,128]{2,1,0:T(8,128)(2,1)S(1)} %bitcast.10, s32[6,128]{1,0:T(8,128)S(1)} %get-tuple-element.32.refs_2_, s32[6,128]{1,0:T(8,128)S(1)} %get-tuple-element.33.refs_3_, ...), custom_call_target="tpu_custom_call" | custom-call | flops 2013265920 | bytes 4194304 | tf_op jit(solution)/shard_map/near/pallas_call | solution.py:424
  31.1 2.3 %collective-permute-done.1 = bf16[1152,128]{1,0:T(8,128)(2,1)S(1)} collective-permute-done((bf16[1152,128]{1,0:T(8,128)(2,1)S(1)}, bf16[1152,128]{1,0:T(8,128)(2,1)S(1)}, u32[]{:S(2)}, u32[]{:S(2)}) %collective-permute-start.1) | collective-permute-done | bytes 294944 | tf_op jit(solution)/shard_map/ppermute | solution.py:372
  33.4 0.0 collective-permute-start.3
  33.4 1.6 %collective-permute-done.3 = bf16[1152,128]{1,0:T(8,128)(2,1)S(1)} collective-permute-done((bf16[1152,128]{1,0:T(8,128)(2,1)S(1)}, bf16[1152,128]{1,0:T(8,128)(2,1)S(1)}, u32[]{:S(2)}, u32[]{:S(2)}) %collective-permute-start.3) | collective-permute-done | bytes 294944 | tf_op jit(solution)/shard_map/ppermute | solution.py:372
  35.0 5.3 %far.1 = (bf16[64,64,128]{2,1,0:T(8,128)(2,1)S(1)}, bf16[4224,128]{1,0:T(8,128)(2,1)S(1)}, f32[2,64,128]{2,1,0:T(8,128)S(1)}) custom-call(bf16[36,32,128]{2,1,0:T(8,128)(2,1)S(1)} %bitcast.7, bf16[36,32,128]{2,1,0:T(8,128)(2,1)S(1)} %bitcast.8, s32[6,128]{1,0:T(8,128)S(1)} %get-tuple-element.32.refs_2_, s32[6,128]{1,0:T(8,128)S(1)} %get-tuple-element.33.refs_3_, ...), custom_call_target="tpu_custom_call" | custom-call | flops 1409286144 | bytes 4194304 | tf_op jit(solution)/shard_map/far/pallas_call | solution.py:439
  40.3 0.2 collective-permute-start.4
  40.5 2.7 %own.1.refs_5_ = bf16[64,128,128]{2,1,0:T(8,128)(2,1)} custom-call(bf16[4224,128]{1,0:T(8,128)(2,1)S(1)} %get-tuple-element.40.refs_0_, bf16[384,192]{1,0:T(8,128)(2,1)S(1)} %get-tuple-element.37.refs_5_.refs_1_, f32[64,2,64,128]{3,2,1,0:T(8,128)S(1)} %get-tuple-element.38.refs_6_.refs_2_, f32[2,64,128]{2,1,0:T(8,128)S(1)} %get-tuple-element.41.refs_3_), custom_call_target="tpu_custom_call" | custom-call | flops 603979776 | bytes 4194304 | tf_op jit(solution)/shard_map/own/pallas_call | solution.py:457
  43.2 0.0 collective-permute-done.4.refs_4_
  43.2 1.7 %last.1 = bf16[64,128,128]{2,1,0:T(8,128)(2,1)} custom-call(bf16[4224,128]{1,0:T(8,128)(2,1)S(1)} %get-tuple-element.40.refs_0_, bf16[384,192]{1,0:T(8,128)(2,1)S(1)} %get-tuple-element.37.refs_5_.refs_1_, f32[64,2,64,128]{3,2,1,0:T(8,128)S(1)} %get-tuple-element.38.refs_6_.refs_2_, ...), custom_call_target="tpu_custom_call", output_to_operand_aliasing={{}: (5, {})} | custom-call | flops 150994944 | bytes 4194304 | tf_op jit(solution)/shard_map/last/pallas_call | solution.py:467
Async XLA Ops:
  1.6 20.6 %collective-permute-start = (bf16[3,3,64,128]{3,2,1,0:T(8,128)(2,1)S(1)}, bf16[3,3,64,128]{3,2,1,0:T(8,128)(2,1)S(1)}, u32[]{:S(2)}, u32[]{:S(2)}) collective-permute-start(bf16[3,3,64,128]{3,2,1,0:T(8,128)(2,1)S(1)} %get-tuple-element.28.filters), channel_id=1, source_target_pairs={{0,1},{1,0},{2,3},{3,2},{4,5},{5,4},{6,7},{7,6},{8,9},{9,8},{10,11... | collective-permute-start | bytes 442376 | tf_op jit(solution)/shard_map/ppermute | solution.py:372
  22.2 3.3 %collective-permute-start.2 = (bf16[1152,128]{1,0:T(8,128)(2,1)S(1)}, bf16[1152,128]{1,0:T(8,128)(2,1)S(1)}, u32[]{:S(2)}, u32[]{:S(2)}) collective-permute-start(bf16[1152,128]{1,0:T(8,128)(2,1)S(1)} %edges.1), channel_id=1, source_target_pairs={{0,1},{1,0},{2,3},{3,2},{4,5},{5,4},{6,7},{7,6},{8,9},{9,8},{10,11... | collective-permute-start | bytes 884744 | tf_op jit(solution)/shard_map/ppermute | solution.py:372
  23.9 9.5 %collective-permute-start.1 = (bf16[1152,128]{1,0:T(8,128)(2,1)S(1)}, bf16[1152,128]{1,0:T(8,128)(2,1)S(1)}, u32[]{:S(2)}, u32[]{:S(2)}) collective-permute-start(bf16[1152,128]{1,0:T(8,128)(2,1)S(1)} %edges.1), channel_id=1, source_target_pairs={{0,2},{1,3},{2,0},{3,1},{4,6},{5,7},{6,4},{7,5},{8,10},{9,11},{10,... | collective-permute-start | bytes 884744 | tf_op jit(solution)/shard_map/ppermute | solution.py:372
  33.4 1.6 %collective-permute-start.3 = (bf16[1152,128]{1,0:T(8,128)(2,1)S(1)}, bf16[1152,128]{1,0:T(8,128)(2,1)S(1)}, u32[]{:S(2)}, u32[]{:S(2)}) collective-permute-start(bf16[1152,128]{1,0:T(8,128)(2,1)S(1)} %collective-permute-done.1), channel_id=1, source_target_pairs={{0,1},{1,0},{2,3},{3,2},{4,5},{5,4},{6,7},{7,6},{8,9},{9,8},{10,11... | collective-permute-start | bytes 884744 | tf_op jit(solution)/shard_map/ppermute | solution.py:372
  40.3 2.9 %collective-permute-start.4 = (bf16[64,64,128]{2,1,0:T(8,128)(2,1)S(1)}, bf16[64,64,128]{2,1,0:T(8,128)(2,1)S(1)}, u32[]{:S(2)}, u32[]{:S(2)}) collective-permute-start(bf16[64,64,128]{2,1,0:T(8,128)(2,1)S(1)} %get-tuple-element.42), channel_id=1, source_target_pairs={{0,1},{1,0},{2,3},{3,2},{4,5},{5,4},{6,7},{7,6},{8,9},{9,8},{10,11... | collective-permute-start | bytes 3145736 | tf_op jit(solution)/shard_map/ppermute | solution.py:372

commit v8 on v6

--- a/solution.py
+++ b/solution.py
@@ -12,7 +12,8 @@
 VMEM = pl.BlockSpec(memory_space=pltpu.VMEM)
 HBM = pl.BlockSpec(memory_space=pltpu.HBM)
 LIMIT = 32 * 2**20
-STEP = 16
+SEND = 16
+AHEAD = 8
 
 
 def round_up(value, step):
@@ -151,7 +152,7 @@
             out_ref[dest, :] = (acc[:chans] + acc[chans:]).astype(BF16)
 
 
-def filter_kernel(chans, filters, near_ref, far_ref):
+def filter_kernel(chans, last, filters, out_ref):
     outs, all_chans = filters.shape[2:]
     half = all_chans // 2
     me = lax.axis_index("chan")
@@ -171,11 +172,10 @@
                 bit *= 2
             first.append(value)
             second.append(pltpu.roll(value, half, 1))
+        low, high = (second, first) if last else (first, second)
         at = slice(b * outs, (b + 1) * outs)
-        near_ref[at, :all_chans] = jnp.where(lane < half, first[0], second[1]).astype(BF16)
-        near_ref[at, all_chans:] = first[2][:, :half].astype(BF16)
-        far_ref[at, :all_chans] = jnp.where(lane < half, second[0], first[1]).astype(BF16)
-        far_ref[at, all_chans:] = second[2][:, :half].astype(BF16)
+        out_ref[at, :all_chans] = jnp.where(lane < half, low[0], high[1]).astype(BF16)
+        out_ref[at, all_chans:] = low[2][:, :half].astype(BF16)
 
 
 def tile_kernel(dims, last, many, *refs):
@@ -223,52 +223,51 @@
         rhs = jnp.concatenate([table_ref[weights[k, r]] for k in range(taps)], axis=0)
         return dot(lhs, rhs).astype(BF16)
 
-    def place(r, value):
-        image[pl.ds(pl.multiple_of((r + 1) * half, half), half), :] = value
+    def place(r):
+        image[(r + 1) * half : (r + 2) * half, :] = remap(r)
 
     lane = lax.broadcasted_iota(jnp.int32, (outs, side), 1)
 
-    def convolve(first):
-        ys = []
-        for u in range(0, STEP, 2):
-            x0 = image[pl.ds(pl.multiple_of((first + u) * half, half), 3 * half), :]
-            x1 = image[pl.ds(pl.multiple_of((first + u + 1) * half, half), 3 * half), :]
-            ys.append(dot(matrix[...], jnp.concatenate([x0, x1], axis=1)))
-        for u in range(STEP):
-            i = first + u
-            y = ys[u // 2][:, u % 2 * side : (u % 2 + 1) * side]
-            at_left = pltpu.roll(left, lax.rem(side - i, side), 1) if last else 0.0
-            at_right = pltpu.roll(right, side - 1 - i, 1) if last else 0.0
-            from_left = jnp.where(lane == 0, at_left, pltpu.roll(y[:outs], 1, 1))
-            from_right = jnp.where(lane == side - 1, at_right, pltpu.roll(y[2 * outs :], side - 1, 1))
-            total = y[outs : 2 * outs] + from_left + from_right
-            if last:
-                spread[pl.ds(u * (outs + 1), outs), :] = total + before_ref[i]
-            else:
-                out_ref[i] = total
+    def multiply(i):
+        x0 = image[i * half : (i + 3) * half, :]
+        x1 = image[(i + 1) * half : (i + 4) * half, :]
+        return dot(matrix[...], jnp.concatenate([x0, x1], axis=1))
+
+    def combine(i, y):
+        at_left = pltpu.roll(left, (side - i) % side, 1) if last else 0.0
+        at_right = pltpu.roll(right, side - 1 - i, 1) if last else 0.0
+        from_left = jnp.where(lane == 0, at_left, pltpu.roll(y[:outs], 1, 1))
+        from_right = jnp.where(lane == side - 1, at_right, pltpu.roll(y[2 * outs :], side - 1, 1))
+        total = y[outs : 2 * outs] + from_left + from_right
         if last:
-            rows = pl.ds(pl.multiple_of(first, STEP), STEP)
+            at = i % SEND * (outs + 1)
+            spread[at : at + outs, :] = total + before_ref[i]
+        else:
+            out_ref[i] = total
+
+    sent = []
+
+    def finish(i, y):
+        for h in range(2):
+            combine(i + h, y[:, h * side : (h + 1) * side])
+        if last and (i + 2) % SEND == 0:
+            rows = pl.ds(i + 2 - SEND, SEND)
             for o in range(outs):
-                staged[o, rows, :] = spread[pl.ds(o, STEP, stride=outs + 1), :].astype(BF16)
-            pltpu.make_async_copy(staged.at[:, rows, :], out_ref.at[:, rows, :], out_sems.at[first // STEP]).start()
-
-    for r in range(STEP + 1):
-        place(r, remap(r))
-
-    def step(t, carry):
-        first = t * STEP
-        convolve(first)
-        for u in range(STEP):
-            r = jnp.minimum(first + STEP + 1 + u, side - 1)
-            place(r, remap(r))
-        return carry
-
-    lax.fori_loop(0, side // STEP - 1, step, 0)
-    convolve(side - STEP)
-    if last:
-        for t in range(side // STEP):
-            rows = pl.ds(t * STEP, STEP)
-            pltpu.make_async_copy(staged.at[:, rows, :], out_ref.at[:, rows, :], out_sems.at[t]).wait()
+                staged[o, rows, :] = spread[pl.ds(o, SEND, stride=outs + 1), :].astype(BF16)
+            sent.append(
+                pltpu.make_async_copy(staged.at[:, rows, :], out_ref.at[:, rows, :], out_sems.at[(i + 2) // SEND - 1])
+            )
+            sent[-1].start()
+
+    for r in range(AHEAD + 1):
+        place(r)
+    for i in range(0, side, 2):
+        y = multiply(i)
+        for r in range(i + AHEAD + 1, min(i + AHEAD + 3, side)):
+            place(r)
+        finish(i, y)
+    for copy in sent:
+        copy.wait()
 
 
 def body(source, send_list, block_slot, weight_index, remap_table, neighbour_tile, neighbour_edge, conv_weight):
@@ -338,14 +337,17 @@
     half = all_chans // 2
     mine, filters = lax.optimization_barrier((mine, filters))
     near = spread({0: mine}, many // 2)
-    near_filters, far_filters = pl.pallas_call(
-        functools.partial(filter_kernel, chans),
-        out_shape=[jax.ShapeDtypeStruct((3 * outs, 3 * half), BF16)] * 2,
-        in_specs=[VMEM],
-        out_specs=[VMEM] * 2,
-        compiler_params=params,
-        name="filters",
-    )(filters)
+    def matrix(last, filters):
+        return pl.pallas_call(
+            functools.partial(filter_kernel, chans, last),
+            out_shape=jax.ShapeDtypeStruct((3 * outs, 3 * half), BF16),
+            in_specs=[VMEM],
+            out_specs=VMEM,
+            compiler_params=params,
+            name="filters",
+        )(filters)
+
+    near_filters = matrix(False, filters)
     mine, near_filters = lax.optimization_barrier((mine, near_filters))
     across = swap(mine, many)
     dims = (side, chans, cap, tiles, all_chans, outs)
@@ -366,7 +368,9 @@
         cost_estimate=cost,
         name="near",
     )(*near, slots, weights, table, near_filters)
-    across, so_far = lax.optimization_barrier((across, so_far))
+    filters, so_far = lax.optimization_barrier((filters, so_far))
+    far_filters = matrix(True, filters)
+    across, so_far, far_filters = lax.optimization_barrier((across, so_far, far_filters))
     far = spread({many: across}, many // 2)
     return pl.pallas_call(
         functools.partial(tile_kernel, dims, True, many),
@@ -375,9 +379,9 @@
         out_specs=HBM,
         scratch_shapes=scratch
         + [
-            pltpu.VMEM((round_up(STEP * (outs + 1), 8), side), F32),
+            pltpu.VMEM((round_up(SEND * (outs + 1), 8), side), F32),
             pltpu.VMEM((outs, side, side), BF16),
-            pltpu.SemaphoreType.DMA((side // STEP,)),
+            pltpu.SemaphoreType.DMA((side // SEND,)),
             pltpu.SemaphoreType.DMA((2,)),
         ],
         compiler_params=params,

time: 44.4 us -> 42.8 us (0.964); the launches traced: 44.7 us -> 42.6 us
  Pallas kernels: 24.4 us -> 22 us
    pallas_call x1, Pallas kernels: 10.3 us -> 9.19 us  [body(): pl.pallas_call(functools.partial(tile_kernel, dims, True, many), out_shap...]
    pallas_call x1, Pallas kernels: 8.3 us -> 7.35 us  [body(): pl.pallas_call(functools.partial(tile_kernel, dims, False, many), out_sha...]
    pallas_call x1, Pallas kernels: 3.78 us -> 3.12 us  [body(): pl.pallas_call(functools.partial(edge_kernel, (side, chans, blocks, tiles...]
  transfers between devices with their start and end apart: 3 -> 3, of which waited for: 1 -> 2; matrix products, arithmetic and copies ran while one was open for 0% -> 0% of each run, Pallas kernels for 19% -> 19%
where the time goes in v8:
time: 42.8 us; the launch traced here: 42.6 us
  Pallas kernels  22 us (51%)
  blocking collectives  17 us (40%)
  starting transfers between devices  1.72 us (4%)
  waiting for transfers between devices  1.69 us (4%)
    all_gather x1, blocking collectives, body(): gathered = lax.all_gather(packed, 'tile', axis=1, tiled=True)  17 us
    pallas_call x1, Pallas kernels, body(): pl.pallas_call(functools.partial(tile_kernel, dims, True, many), out_shap...  9.19 us
    pallas_call x1, Pallas kernels, body(): pl.pallas_call(functools.partial(tile_kernel, dims, False, many), out_sha...  7.35 us
    pallas_call x1, Pallas kernels, body(): pl.pallas_call(functools.partial(edge_kernel, (side, chans, blocks, tiles...  3.12 us
    ppermute x3, starting transfers between devices, swap(): return lax.ppermute(value, 'chan', [(i, i ^ flip) for i in range(parts)])  1.72 us
    ppermute x3, waiting for transfers between devices, swap(): return lax.ppermute(value, 'chan', [(i, i ^ flip) for i in range(parts)])  1.69 us
    pallas_call x1, Pallas kernels, body(): pl.pallas_call(pack_kernel, out_shape=[jax.ShapeDtypeStruct((blocks * cha...  1.62 us
  transfers between devices with their start and end apart: 3, of which 2 were waited for; matrix products, arithmetic and copies ran while one was open for 0% of the time, Pallas kernels for 19%

profile of v8, /device:TPU:0, one launch (start us, length us, event | category | flops | bytes accessed | tf_op | source)
XLA Modules:
  0.0 42.6 jit_solution(16735182051752817758)
XLA Ops:
  0.0 1.6 %pack.1 = (bf16[528,128]{1,0:T(8,128)(2,1)S(1)}, s32[6,128]{1,0:T(8,128)S(1)}, s32[6,128]{1,0:T(8,128)S(1)}, bf16[32,128,128]{2,1,0:T(8,128)(2,1)S(1)}, bf16[3,3,64,128]{3,2,1,0:T(8,128)(2,1)S(1)}) custom-call(s32[6,128]{1,0:T(8,128)} %bitcast.12, s32[6,128]{1,0:T(8,128)} %bitcast.13, s32[1,4,8]{2,1,0:T(4,128)} %lists_hbm.1, s32[1,4]{1,0:T(1,128)} %neigh_hbm.1, ...), custom_call_target="tpu_custom_call" | custom-call | tf_op jit(solution)/shard_map/pack/pallas_call | solution.py:286
  1.6 17.0 %all_gather.3.gathered_ref = bf16[528,512]{1,0:T(8,128)(2,1)S(1)} all-gather(bf16[528,128]{1,0:T(8,128)(2,1)S(1)} %get-tuple-element.19), channel_id=1, replica_groups=mesh['group'=2,'tile'=4,'chan'=4] {'tile'}, dimensions={1}, use_global_device_ids=true | all-gather | bytes 675840 | tf_op jit(solution)/shard_map/all_gather | solution.py:309
  18.6 3.1 %edges.1 = bf16[1152,128]{1,0:T(8,128)(2,1)S(1)} custom-call(bf16[528,512]{1,0:T(8,128)(2,1)S(1)} %all_gather.3.gathered_ref, bf16[32,128,128]{2,1,0:T(8,128)(2,1)S(1)} %get-tuple-element.20.table_ref.refs_4_.refs_5_), custom_call_target="tpu_custom_call" | custom-call | tf_op jit(solution)/shard_map/edges/pallas_call | solution.py:310
  21.8 0.1 collective-permute-start.1
  21.8 0.4 filters.2.refs_5_
  22.2 1.6 %collective-permute-start = (bf16[1152,128]{1,0:T(8,128)(2,1)S(1)}, bf16[1152,128]{1,0:T(8,128)(2,1)S(1)}, u32[]{:S(2)}, u32[]{:S(2)}) collective-permute-start(bf16[1152,128]{1,0:T(8,128)(2,1)S(1)} %edges.1), channel_id=1, source_target_pairs={{0,2},{1,3},{2,0},{3,1},{4,6},{5,7},{6,4},{7,5},{8,10},{9,11},{10,... | collective-permute-start | bytes 884744 | tf_op jit(solution)/shard_map/ppermute | solution.py:327
  23.8 0.0 collective-permute-done.1
  23.8 7.3 %near.1.refs_2_ = f32[130,64,128]{2,1,0:T(8,128)S(1)} custom-call(bf16[36,32,128]{2,1,0:T(8,128)(2,1)S(1)} %bitcast.7, bf16[36,32,128]{2,1,0:T(8,128)(2,1)S(1)} %bitcast.9, s32[6,128]{1,0:T(8,128)S(1)} %get-tuple-element.25.refs_2_.refs_3_, s32[6,128]{1,0:T(8,128)S(1)} %get-tuple-element.26.refs_3_.refs_4_, ...), custom_call_target="tpu_custom_call" | custom-call | flops 2818572288 | bytes 4259840 | tf_op jit(solution)/shard_map/near/pallas_call | solution.py:361
  31.1 0.3 filters.3.refs_6_
  31.5 0.2 collective-permute-done
  31.7 0.1 collective-permute-start.2
  31.8 1.5 %collective-permute-done.2 = bf16[1152,128]{1,0:T(8,128)(2,1)S(1)} collective-permute-done((bf16[1152,128]{1,0:T(8,128)(2,1)S(1)}, bf16[1152,128]{1,0:T(8,128)(2,1)S(1)}, u32[]{:S(2)}, u32[]{:S(2)}) %collective-permute-start.2) | collective-permute-done | bytes 294944 | tf_op jit(solution)/shard_map/ppermute | solution.py:327
  33.3 9.2 %far.1 = bf16[64,128,128]{2,1,0:T(8,128)(2,1)} custom-call(bf16[36,32,128]{2,1,0:T(8,128)(2,1)S(1)} %bitcast.8, bf16[36,32,128]{2,1,0:T(8,128)(2,1)S(1)} %bitcast.10, f32[130,64,128]{2,1,0:T(8,128)S(1)} %near.1.refs_2_, s32[6,128]{1,0:T(8,128)S(1)} %get-tuple-element.25.refs_2_.refs_3_, s32[6,128]{1,0:T(8,128)S(1)} %get-tuple-element.26.refs_3_.refs_4_, ...), custom_call_target="tpu_custom_call" | custom-call | flops 2818572288 | bytes 4259840 | tf_op jit(solution)/shard_map/far/pallas_call | solution.py:375
Async XLA Ops:
  21.8 2.0 %collective-permute-start.1 = (bf16[1152,128]{1,0:T(8,128)(2,1)S(1)}, bf16[1152,128]{1,0:T(8,128)(2,1)S(1)}, u32[]{:S(2)}, u32[]{:S(2)}) collective-permute-start(bf16[1152,128]{1,0:T(8,128)(2,1)S(1)} %edges.1), channel_id=1, source_target_pairs={{0,1},{1,0},{2,3},{3,2},{4,5},{5,4},{6,7},{7,6},{8,9},{9,8},{10,11... | collective-permute-start | bytes 884744 | tf_op jit(solution)/shard_map/ppermute | solution.py:327
  22.2 9.5 %collective-permute-start = (bf16[1152,128]{1,0:T(8,128)(2,1)S(1)}, bf16[1152,128]{1,0:T(8,128)(2,1)S(1)}, u32[]{:S(2)}, u32[]{:S(2)}) collective-permute-start(bf16[1152,128]{1,0:T(8,128)(2,1)S(1)} %edges.1), channel_id=1, source_target_pairs={{0,2},{1,3},{2,0},{3,1},{4,6},{5,7},{6,4},{7,5},{8,10},{9,11},{10,... | collective-permute-start | bytes 884744 | tf_op jit(solution)/shard_map/ppermute | solution.py:327
  31.7 1.6 %collective-permute-start.2 = (bf16[1152,128]{1,0:T(8,128)(2,1)S(1)}, bf16[1152,128]{1,0:T(8,128)(2,1)S(1)}, u32[]{:S(2)}, u32[]{:S(2)}) collective-permute-start(bf16[1152,128]{1,0:T(8,128)(2,1)S(1)} %collective-permute-done), channel_id=1, source_target_pairs={{0,1},{1,0},{2,3},{3,2},{4,5},{5,4},{6,7},{7,6},{8,9},{9,8},{10,11... | collective-permute-start | bytes 884744 | tf_op jit(solution)/shard_map/ppermute | solution.py:327

commit v9 on v8

--- a/solution.py
+++ b/solution.py
@@ -74,7 +74,36 @@
         copy.wait()
 
 
-def edge_kernel(dims, gathered_ref, table_ref, out_ref, ints, scalars, picked, columns, sem):
+def lay_filters(chans, filters, near_ref, far_ref):
+    outs, all_chans = filters.shape[2:]
+    half = all_chans // 2
+    me = lax.axis_index("chan")
+    lane = lax.broadcasted_iota(jnp.int32, (outs, all_chans), 1)
+    for b in range(3):
+        first, second = [], []
+        for a in range(3):
+            value = filters[a, b].astype(F32)
+            width = chans
+            bit = 1
+            while width < all_chans:
+                other = jnp.where(
+                    lane // width % 2 == 0, pltpu.roll(value, all_chans - width, 1), pltpu.roll(value, width, 1)
+                )
+                value = jnp.where((me & bit) != 0, other, value)
+                width *= 2
+                bit *= 2
+            first.append(value)
+            second.append(pltpu.roll(value, half, 1))
+        at = slice(b * outs, (b + 1) * outs)
+        near_ref[at, :all_chans] = jnp.where(lane < half, first[0], second[1]).astype(BF16)
+        near_ref[at, all_chans:] = first[2][:, :half].astype(BF16)
+        far_ref[at, :all_chans] = jnp.where(lane < half, second[0], first[1]).astype(BF16)
+        far_ref[at, all_chans:] = second[2][:, :half].astype(BF16)
+
+
+def edge_kernel(
+    dims, gathered_ref, table_ref, filters, out_ref, near_ref, far_ref, ints, scalars, picked, columns, sem
+):
     side, chans, blocks, tiles, cap, taps, rows = dims
     count = tiles * cap
     base = blocks * chans
@@ -94,6 +123,7 @@
         moved = pltpu.roll(table_ref[kind].astype(F32), per_group * kind + 1, 1)
         total = jnp.where(lane // per_group == kind, moved, total)
     columns[...] = total
+    lay_filters(chans, filters, near_ref, far_ref)
     copy.wait()
     own_row = me * rows + 2 * taps
     neigh = [scalars[own_row, cap + s] for s in range(4)]
@@ -152,32 +182,6 @@
             out_ref[dest, :] = (acc[:chans] + acc[chans:]).astype(BF16)
 
 
-def filter_kernel(chans, last, filters, out_ref):
-    outs, all_chans = filters.shape[2:]
-    half = all_chans // 2
-    me = lax.axis_index("chan")
-    lane = lax.broadcasted_iota(jnp.int32, (outs, all_chans), 1)
-    for b in range(3):
-        first, second = [], []
-        for a in range(3):
-            value = filters[a, b].astype(F32)
-            width = chans
-            bit = 1
-            while width < all_chans:
-                other = jnp.where(
-                    lane // width % 2 == 0, pltpu.roll(value, all_chans - width, 1), pltpu.roll(value, width, 1)
-                )
-                value = jnp.where((me & bit) != 0, other, value)
-                width *= 2
-                bit *= 2
-            first.append(value)
-            second.append(pltpu.roll(value, half, 1))
-        low, high = (second, first) if last else (first, second)
-        at = slice(b * outs, (b + 1) * outs)
-        out_ref[at, :all_chans] = jnp.where(lane < half, low[0], high[1]).astype(BF16)
-        out_ref[at, all_chans:] = low[2][:, :half].astype(BF16)
-
-
 def tile_kernel(dims, last, many, *refs):
     side, chans, cap, tiles, all_chans, outs = dims
     parts = refs[:many]
@@ -307,11 +311,14 @@
         in_hbm(remap_table), filters,
     )
     gathered = lax.all_gather(packed, "tile", axis=1, tiled=True)
-    mine = pl.pallas_call(
+    many = parts // 2
+    half = all_chans // 2
+    matrix_shape = jax.ShapeDtypeStruct((3 * outs, 3 * half), BF16)
+    mine, near_filters, far_filters = pl.pallas_call(
         functools.partial(edge_kernel, (side, chans, blocks, tiles, cap, taps, rows)),
-        out_shape=jax.ShapeDtypeStruct(((count + 4) * chans, side), BF16),
-        in_specs=[VMEM, VMEM],
-        out_specs=VMEM,
+        out_shape=[jax.ShapeDtypeStruct(((count + 4) * chans, side), BF16), matrix_shape, matrix_shape],
+        in_specs=[VMEM] * 3,
+        out_specs=[VMEM] * 3,
         scratch_shapes=[
             pltpu.VMEM((2 * tiles * rows, side), jnp.int32),
             pltpu.SMEM((tiles * rows, side), jnp.int32),
@@ -321,7 +328,7 @@
         ],
         compiler_params=params,
         name="edges",
-    )(gathered, table)
+    )(gathered, table, filters)
 
     def swap(value, flip):
         return lax.ppermute(value, "chan", [(i, i ^ flip) for i in range(parts)])
@@ -333,22 +340,7 @@
             bit //= 2
         return [held[f].reshape(count + 4, chans, side) for f in sorted(held)]
 
-    many = parts // 2
-    half = all_chans // 2
-    mine, filters = lax.optimization_barrier((mine, filters))
     near = spread({0: mine}, many // 2)
-    def matrix(last, filters):
-        return pl.pallas_call(
-            functools.partial(filter_kernel, chans, last),
-            out_shape=jax.ShapeDtypeStruct((3 * outs, 3 * half), BF16),
-            in_specs=[VMEM],
-            out_specs=VMEM,
-            compiler_params=params,
-            name="filters",
-        )(filters)
-
-    near_filters = matrix(False, filters)
-    mine, near_filters = lax.optimization_barrier((mine, near_filters))
     across = swap(mine, many)
     dims = (side, chans, cap, tiles, all_chans, outs)
     scratch = [
@@ -368,9 +360,7 @@
         cost_estimate=cost,
         name="near",
     )(*near, slots, weights, table, near_filters)
-    filters, so_far = lax.optimization_barrier((filters, so_far))
-    far_filters = matrix(True, filters)
-    across, so_far, far_filters = lax.optimization_barrier((across, so_far, far_filters))
+    across, so_far = lax.optimization_barrier((across, so_far))
     far = spread({many: across}, many // 2)
     return pl.pallas_call(
         functools.partial(tile_kernel, dims, True, many),

time: 42.8 us -> 43.9 us (1.026)
  Pallas kernels: 22 us -> 22.6 us
    pallas_call x1, Pallas kernels: 3.12 us -> 4.57 us  [body(): pl.pallas_call(functools.partial(edge_kernel, (side, chans, blocks, tiles...]
    pallas_call x2 -> x0, Pallas kernels: 0.71 us -> none  [matrix(): pl.pallas_call(functools.partial(filter_kernel, chans, last), out_shape=j...]
  transfers between devices with their start and end apart: 3 -> 3, of which waited for: 2 -> 2; matrix products, arithmetic and copies ran while one was open for 0% -> 0% of each run, Pallas kernels for 19% -> 17%
where the time goes in v9:
time: 43.9 us; the launch traced here: 43.6 us
  Pallas kernels  22.6 us (51%)
  blocking collectives  17 us (39%)
  waiting for transfers between devices  2.11 us (5%)
  starting transfers between devices  1.63 us (4%)
    all_gather x1, blocking collectives, body(): gathered = lax.all_gather(packed, 'tile', axis=1, tiled=True)  17 us
    pallas_call x1, Pallas kernels, body(): pl.pallas_call(functools.partial(tile_kernel, dims, True, many), out_shap...  9.12 us
    pallas_call x1, Pallas kernels, body(): pl.pallas_call(functools.partial(tile_kernel, dims, False, many), out_sha...  7.33 us
    pallas_call x1, Pallas kernels, body(): pl.pallas_call(functools.partial(edge_kernel, (side, chans, blocks, tiles...  4.57 us
    ppermute x3, waiting for transfers between devices, swap(): return lax.ppermute(value, 'chan', [(i, i ^ flip) for i in range(parts)])  2.11 us
    ppermute x3, starting transfers between devices, swap(): return lax.ppermute(value, 'chan', [(i, i ^ flip) for i in range(parts)])  1.63 us
    pallas_call x1, Pallas kernels, body(): pl.pallas_call(pack_kernel, out_shape=[jax.ShapeDtypeStruct((blocks * cha...  1.62 us
  transfers between devices with their start and end apart: 3, of which 2 were waited for; matrix products, arithmetic and copies ran while one was open for 0% of the time, Pallas kernels for 17%

profile of v9, /device:TPU:0, one launch (start us, length us, event | category | flops | bytes accessed | tf_op | source)
XLA Modules:
  0.0 43.6 jit_solution(7731983580046348043)
XLA Ops:
  0.0 1.6 %pack.1 = (bf16[528,128]{1,0:T(8,128)(2,1)S(1)}, s32[6,128]{1,0:T(8,128)S(1)}, s32[6,128]{1,0:T(8,128)S(1)}, bf16[32,128,128]{2,1,0:T(8,128)(2,1)S(1)}, bf16[3,3,64,128]{3,2,1,0:T(8,128)(2,1)S(1)}) custom-call(s32[6,128]{1,0:T(8,128)} %bitcast.12, s32[6,128]{1,0:T(8,128)} %bitcast.13, s32[1,4,8]{2,1,0:T(4,128)} %lists_hbm.1, s32[1,4]{1,0:T(1,128)} %neigh_hbm.1, ...), custom_call_target="tpu_custom_call" | custom-call | tf_op jit(solution)/shard_map/pack/pallas_call | solution.py:290
  1.6 17.0 %all_gather.3.gathered_ref = bf16[528,512]{1,0:T(8,128)(2,1)S(1)} all-gather(bf16[528,128]{1,0:T(8,128)(2,1)S(1)} %get-tuple-element.15), channel_id=1, replica_groups=mesh['group'=2,'tile'=4,'chan'=4] {'tile'}, dimensions={1}, use_global_device_ids=true | all-gather | bytes 675840 | tf_op jit(solution)/shard_map/all_gather | solution.py:313
  18.6 4.6 %edges.1 = (bf16[1152,128]{1,0:T(8,128)(2,1)S(1)}, bf16[192,192]{1,0:T(8,128)(2,1)S(1)}, bf16[192,192]{1,0:T(8,128)(2,1)S(1)}) custom-call(bf16[528,512]{1,0:T(8,128)(2,1)S(1)} %all_gather.3.gathered_ref, bf16[32,128,128]{2,1,0:T(8,128)(2,1)S(1)} %get-tuple-element.16.table_ref.refs_4_.refs_5_, bf16[3,3,64,128]{3,2,1,0:T(8,128)(2,1)S(1)} %get-tuple-element.17.filters), custom_call_target="tpu_custom_call" | custom-call | tf_op jit(solution)/shard_map/edges/pallas_call | solution.py:317
  23.2 0.1 collective-permute-start.1
  23.3 1.6 %collective-permute-start = (bf16[1152,128]{1,0:T(8,128)(2,1)S(1)}, bf16[1152,128]{1,0:T(8,128)(2,1)S(1)}, u32[]{:S(2)}, u32[]{:S(2)}) collective-permute-start(bf16[1152,128]{1,0:T(8,128)(2,1)S(1)} %get-tuple-element.18), channel_id=1, source_target_pairs={{0,2},{1,3},{2,0},{3,1},{4,6},{5,7},{6,4},{7,5},{8,10},{9,11},{10,... | collective-permute-start | bytes 884744 | tf_op jit(solution)/shard_map/ppermute | solution.py:334
  24.8 0.0 collective-permute-done.1
  24.9 7.3 %near.1.refs_2_ = f32[130,64,128]{2,1,0:T(8,128)S(1)} custom-call(bf16[36,32,128]{2,1,0:T(8,128)(2,1)S(1)} %bitcast.8, bf16[36,32,128]{2,1,0:T(8,128)(2,1)S(1)} %bitcast.10, s32[6,128]{1,0:T(8,128)S(1)} %get-tuple-element.19.refs_2_.refs_3_, s32[6,128]{1,0:T(8,128)S(1)} %get-tuple-element.20.refs_3_.refs_4_, ...), custom_call_target="tpu_custom_call" | custom-call | flops 2818572288 | bytes 4259840 | tf_op jit(solution)/shard_map/near/pallas_call | solution.py:353
  32.2 0.5 %collective-permute-done = bf16[1152,128]{1,0:T(8,128)(2,1)S(1)} collective-permute-done((bf16[1152,128]{1,0:T(8,128)(2,1)S(1)}, bf16[1152,128]{1,0:T(8,128)(2,1)S(1)}, u32[]{:S(2)}, u32[]{:S(2)}) %collective-permute-start) | collective-permute-done | bytes 294944 | tf_op jit(solution)/shard_map/ppermute | solution.py:334
  32.7 0.0 collective-permute-start.2
  32.7 1.6 %collective-permute-done.2 = bf16[1152,128]{1,0:T(8,128)(2,1)S(1)} collective-permute-done((bf16[1152,128]{1,0:T(8,128)(2,1)S(1)}, bf16[1152,128]{1,0:T(8,128)(2,1)S(1)}, u32[]{:S(2)}, u32[]{:S(2)}) %collective-permute-start.2) | collective-permute-done | bytes 294944 | tf_op jit(solution)/shard_map/ppermute | solution.py:334
  34.3 9.1 %far.1 = bf16[64,128,128]{2,1,0:T(8,128)(2,1)} custom-call(bf16[36,32,128]{2,1,0:T(8,128)(2,1)S(1)} %bitcast.7, bf16[36,32,128]{2,1,0:T(8,128)(2,1)S(1)} %bitcast.9, f32[130,64,128]{2,1,0:T(8,128)S(1)} %near.1.refs_2_, s32[6,128]{1,0:T(8,128)S(1)} %get-tuple-element.19.refs_2_.refs_3_, s32[6,128]{1,0:T(8,128)S(1)} %get-tuple-element.20.refs_3_.refs_4_, ...), custom_call_target="tpu_custom_call" | custom-call | flops 2818572288 | bytes 4259840 | tf_op jit(solution)/shard_map/far/pallas_call | solution.py:365
Async XLA Ops:
  23.2 1.6 %collective-permute-start.1 = (bf16[1152,128]{1,0:T(8,128)(2,1)S(1)}, bf16[1152,128]{1,0:T(8,128)(2,1)S(1)}, u32[]{:S(2)}, u32[]{:S(2)}) collective-permute-start(bf16[1152,128]{1,0:T(8,128)(2,1)S(1)} %get-tuple-element.18), channel_id=1, source_target_pairs={{0,1},{1,0},{2,3},{3,2},{4,5},{5,4},{6,7},{7,6},{8,9},{9,8},{10,11... | collective-permute-start | bytes 884744 | tf_op jit(solution)/shard_map/ppermute | solution.py:334
  23.3 9.4 %collective-permute-start = (bf16[1152,128]{1,0:T(8,128)(2,1)S(1)}, bf16[1152,128]{1,0:T(8,128)(2,1)S(1)}, u32[]{:S(2)}, u32[]{:S(2)}) collective-permute-start(bf16[1152,128]{1,0:T(8,128)(2,1)S(1)} %get-tuple-element.18), channel_id=1, source_target_pairs={{0,2},{1,3},{2,0},{3,1},{4,6},{5,7},{6,4},{7,5},{8,10},{9,11},{10,... | collective-permute-start | bytes 884744 | tf_op jit(solution)/shard_map/ppermute | solution.py:334
  32.7 1.6 %collective-permute-start.2 = (bf16[1152,128]{1,0:T(8,128)(2,1)S(1)}, bf16[1152,128]{1,0:T(8,128)(2,1)S(1)}, u32[]{:S(2)}, u32[]{:S(2)}) collective-permute-start(bf16[1152,128]{1,0:T(8,128)(2,1)S(1)} %collective-permute-done), channel_id=1, source_target_pairs={{0,1},{1,0},{2,3},{3,2},{4,5},{5,4},{6,7},{7,6},{8,9},{9,8},{10,11... | collective-permute-start | bytes 884744 | tf_op jit(solution)/shard_map/ppermute | solution.py:334

commit v10 on v8

--- a/solution.py
+++ b/solution.py
@@ -74,7 +74,7 @@
         copy.wait()
 
 
-def edge_kernel(dims, gathered_ref, table_ref, out_ref, ints, scalars, picked, columns, sem):
+def edge_kernel(dims, gathered_ref, table_ref, out_ref, ints, scalars, picked, columns, sems):
     side, chans, blocks, tiles, cap, taps, rows = dims
     count = tiles * cap
     base = blocks * chans
@@ -82,26 +82,37 @@
     per_group = side // kinds
     me = lax.axis_index("tile")
     tables = jnp.concatenate([gathered_ref[base:, band * side : (band + 1) * side] for band in range(tiles)], axis=0)
-    ints[: tiles * rows, :] = tables.astype(F32).astype(jnp.int32)
-    copy = pltpu.make_async_copy(ints.at[pl.ds(0, tiles * rows), :], scalars, sem)
-    copy.start()
+    values = tables.astype(F32).astype(jnp.int32)
+    lists = pl.ds(0, tiles * tiles)
+    others = pl.ds(tiles * tiles, tiles * 2 * taps)
+    start = tiles * (tiles + 2 * taps)
+    for band in range(tiles):
+        ints[band * tiles : (band + 1) * tiles, :] = values[band * rows + 2 * taps : band * rows + 2 * taps + tiles]
+    lists_copy = pltpu.make_async_copy(ints.at[lists, :], scalars.at[lists, :], sems.at[0])
+    lists_copy.start()
+    for band in range(tiles):
+        at = tiles * tiles + band * 2 * taps
+        ints[at : at + 2 * taps, :] = values[band * rows : band * rows + 2 * taps]
+    others_copy = pltpu.make_async_copy(ints.at[others, :], scalars.at[others, :], sems.at[1])
+    others_copy.start()
+    ints[start : start + tiles * rows, :] = values
     row = lax.broadcasted_iota(jnp.int32, (side, side), 0)
     flip = (lax.broadcasted_iota(jnp.int32, (side, side), 1) + row == side - 1).astype(BF16)
-    ints[tiles * rows :, :] = dot(tables, flip).astype(jnp.int32)
+    ints[start + tiles * rows :, :] = dot(tables, flip).astype(jnp.int32)
     lane = lax.broadcasted_iota(jnp.int32, (side, side), 1)
     total = jnp.zeros((side, side), F32)
     for kind in range(kinds):
         moved = pltpu.roll(table_ref[kind].astype(F32), per_group * kind + 1, 1)
         total = jnp.where(lane // per_group == kind, moved, total)
     columns[...] = total
-    copy.wait()
-    own_row = me * rows + 2 * taps
+    lists_copy.wait()
+    own_row = me * tiles
     neigh = [scalars[own_row, cap + s] for s in range(4)]
     codes = [scalars[own_row, cap + 4 + s] for s in range(4)]
 
     def block_of(owner, slot):
         band = slot // cap
-        local = scalars[band * rows + 2 * taps + owner, slot % cap]
+        local = scalars[band * tiles + owner, slot % cap]
         return gathered_ref[pl.ds(pl.multiple_of(local * chans, chans), chans), pl.ds(pl.multiple_of(band * side, side), side)]
 
     for slot in range(count):
@@ -110,20 +121,6 @@
         owner = neigh[s]
         edge = codes[s] % 4
         dest = pl.ds((count + s) * chans, chans)
-
-        @pl.when(edge < 2)
-        def _():
-            at = jnp.where(edge == 0, 0, side - 1)
-            acc = jnp.zeros((chans, side), F32)
-            for k in range(taps):
-                slot = scalars[owner * rows + k, at]
-                kind = scalars[owner * rows + taps + k, at]
-                acc = acc + dot(block_of(owner, slot), table_ref[kind])
-            out_ref[dest, :] = acc.astype(BF16)
-
-            @pl.when(codes[s] >= 4)
-            def _():
-                out_ref[dest, :] = dot(acc.astype(BF16), flip).astype(BF16)
 
         @pl.when(edge >= 2)
         def _():
@@ -139,7 +136,7 @@
             z = dot(picked[...], spread)
             z_hi = z.astype(BF16)
             z_lo = (z - z_hi.astype(F32)).astype(BF16)
-            first = owner * rows + jnp.where(codes[s] >= 4, tiles * rows, 0)
+            first = start + owner * rows + jnp.where(codes[s] >= 4, tiles * rows, 0)
             slots = ints[pl.ds(first, taps), :]
             inside = slots % per_group + ints[pl.ds(first + taps, taps), :] * per_group
             spots = [jnp.where(row == inside[k : k + 1], 1.0, 0.0).astype(BF16) for k in range(taps)]
@@ -150,6 +147,26 @@
                 at = slice(group * chans, (group + 1) * chans)
                 acc = acc + dot(jnp.concatenate([z_hi[at], z_lo[at]], axis=0), hits)
             out_ref[dest, :] = (acc[:chans] + acc[chans:]).astype(BF16)
+
+    others_copy.wait()
+    for s in range(4):
+        owner = neigh[s]
+        edge = codes[s] % 4
+        dest = pl.ds((count + s) * chans, chans)
+
+        @pl.when(edge < 2)
+        def _():
+            at = jnp.where(edge == 0, 0, side - 1)
+            acc = jnp.zeros((chans, side), F32)
+            for k in range(taps):
+                slot = scalars[tiles * tiles + owner * 2 * taps + k, at]
+                kind = scalars[tiles * tiles + owner * 2 * taps + taps + k, at]
+                acc = acc + dot(block_of(owner, slot), table_ref[kind])
+            out_ref[dest, :] = acc.astype(BF16)
+
+            @pl.when(codes[s] >= 4)
+            def _():
+                out_ref[dest, :] = dot(acc.astype(BF16), flip).astype(BF16)
 
 
 def filter_kernel(chans, last, filters, out_ref):
@@ -313,11 +330,11 @@
         in_specs=[VMEM, VMEM],
         out_specs=VMEM,
         scratch_shapes=[
-            pltpu.VMEM((2 * tiles * rows, side), jnp.int32),
-            pltpu.SMEM((tiles * rows, side), jnp.int32),
+            pltpu.VMEM((tiles * (tiles + 2 * taps + 2 * rows), side), jnp.int32),
+            pltpu.SMEM((tiles * (tiles + 2 * taps), side), jnp.int32),
             pltpu.VMEM((count * kinds // side * chans, side * side // kinds), BF16),
             pltpu.VMEM((side, side), F32),
-            pltpu.SemaphoreType.DMA,
+            pltpu.SemaphoreType.DMA((2,)),
         ],
         compiler_params=params,
         name="edges",
@@ -348,7 +365,6 @@
         )(filters)
 
     near_filters = matrix(False, filters)
-    mine, near_filters = lax.optimization_barrier((mine, near_filters))
     across = swap(mine, many)
     dims = (side, chans, cap, tiles, all_chans, outs)
     scratch = [

time: 42.8 us -> 42.4 us (level)
  transfers between devices with their start and end apart: 3 -> 3, of which waited for: 2 -> 1; matrix products, arithmetic and copies ran while one was open for 0% -> 0% of each run, Pallas kernels for 19% -> 19%
where the time goes in v10:
time: 42.4 us; the launch traced here: 42.3 us
  Pallas kernels  21.8 us (51%)
  blocking collectives  17 us (40%)
  starting transfers between devices  1.86 us (4%)
  waiting for transfers between devices  1.42 us (3%)
    all_gather x1, blocking collectives, body(): gathered = lax.all_gather(packed, 'tile', axis=1, tiled=True)  17 us
    pallas_call x1, Pallas kernels, body(): pl.pallas_call(functools.partial(tile_kernel, dims, True, many), out_shap...  9.2 us
    pallas_call x1, Pallas kernels, body(): pl.pallas_call(functools.partial(tile_kernel, dims, False, many), out_sha...  7.34 us
    pallas_call x1, Pallas kernels, body(): pl.pallas_call(functools.partial(edge_kernel, (side, chans, blocks, tiles...  2.95 us
    ppermute x3, starting transfers between devices, swap(): return lax.ppermute(value, 'chan', [(i, i ^ flip) for i in range(parts)])  1.86 us
    pallas_call x1, Pallas kernels, body(): pl.pallas_call(pack_kernel, out_shape=[jax.ShapeDtypeStruct((blocks * cha...  1.62 us
    ppermute x3, waiting for transfers between devices, swap(): return lax.ppermute(value, 'chan', [(i, i ^ flip) for i in range(parts)])  1.42 us
  transfers between devices with their start and end apart: 3, of which 1 were waited for; matrix products, arithmetic and copies ran while one was open for 0% of the time, Pallas kernels for 19%

profile of v10, /device:TPU:0, one launch (start us, length us, event | category | flops | bytes accessed | tf_op | source)
XLA Modules:
  0.0 42.3 jit_solution(14881702537318850796)
XLA Ops:
  0.0 1.6 %pack.1 = (bf16[528,128]{1,0:T(8,128)(2,1)S(1)}, s32[6,128]{1,0:T(8,128)S(1)}, s32[6,128]{1,0:T(8,128)S(1)}, bf16[32,128,128]{2,1,0:T(8,128)(2,1)S(1)}, bf16[3,3,64,128]{3,2,1,0:T(8,128)(2,1)S(1)}) custom-call(s32[6,128]{1,0:T(8,128)} %bitcast.12, s32[6,128]{1,0:T(8,128)} %bitcast.13, s32[1,4,8]{2,1,0:T(4,128)} %lists_hbm.1, s32[1,4]{1,0:T(1,128)} %neigh_hbm.1, ...), custom_call_target="tpu_custom_call" | custom-call | tf_op jit(solution)/shard_map/pack/pallas_call | solution.py:303
  1.6 17.0 %all_gather.3.gathered_ref = bf16[528,512]{1,0:T(8,128)(2,1)S(1)} all-gather(bf16[528,128]{1,0:T(8,128)(2,1)S(1)} %get-tuple-element.17), channel_id=1, replica_groups=mesh['group'=2,'tile'=4,'chan'=4] {'tile'}, dimensions={1}, use_global_device_ids=true | all-gather | bytes 675840 | tf_op jit(solution)/shard_map/all_gather | solution.py:326
  18.6 2.9 %edges.1 = bf16[1152,128]{1,0:T(8,128)(2,1)S(1)} custom-call(bf16[528,512]{1,0:T(8,128)(2,1)S(1)} %all_gather.3.gathered_ref, bf16[32,128,128]{2,1,0:T(8,128)(2,1)S(1)} %get-tuple-element.18.table_ref.refs_4_.refs_5_), custom_call_target="tpu_custom_call" | custom-call | tf_op jit(solution)/shard_map/edges/pallas_call | solution.py:327
  21.6 0.1 collective-permute-start.1
  21.7 1.6 %collective-permute-start = (bf16[1152,128]{1,0:T(8,128)(2,1)S(1)}, bf16[1152,128]{1,0:T(8,128)(2,1)S(1)}, u32[]{:S(2)}, u32[]{:S(2)}) collective-permute-start(bf16[1152,128]{1,0:T(8,128)(2,1)S(1)} %edges.1), channel_id=1, source_target_pairs={{0,2},{1,3},{2,0},{3,1},{4,6},{5,7},{6,4},{7,5},{8,10},{9,11},{10,... | collective-permute-start | bytes 884744 | tf_op jit(solution)/shard_map/ppermute | solution.py:344
  23.2 0.4 filters.2.refs_5_
  23.6 0.0 collective-permute-done.1
  23.6 7.3 %near.1.refs_2_ = f32[130,64,128]{2,1,0:T(8,128)S(1)} custom-call(bf16[36,32,128]{2,1,0:T(8,128)(2,1)S(1)} %bitcast.7, bf16[36,32,128]{2,1,0:T(8,128)(2,1)S(1)} %bitcast.9, s32[6,128]{1,0:T(8,128)S(1)} %get-tuple-element.22.refs_2_.refs_3_, s32[6,128]{1,0:T(8,128)S(1)} %get-tuple-element.23.refs_3_.refs_4_, ...), custom_call_target="tpu_custom_call" | custom-call | flops 2818572288 | bytes 4259840 | tf_op jit(solution)/shard_map/near/pallas_call | solution.py:377
  30.9 0.3 filters.3.refs_6_
  31.3 0.0 collective-permute-done
  31.3 0.2 collective-permute-start.2
  31.5 1.4 %collective-permute-done.2 = bf16[1152,128]{1,0:T(8,128)(2,1)S(1)} collective-permute-done((bf16[1152,128]{1,0:T(8,128)(2,1)S(1)}, bf16[1152,128]{1,0:T(8,128)(2,1)S(1)}, u32[]{:S(2)}, u32[]{:S(2)}) %collective-permute-start.2) | collective-permute-done | bytes 294944 | tf_op jit(solution)/shard_map/ppermute | solution.py:344
  33.0 9.2 %far.1 = bf16[64,128,128]{2,1,0:T(8,128)(2,1)} custom-call(bf16[36,32,128]{2,1,0:T(8,128)(2,1)S(1)} %bitcast.8, bf16[36,32,128]{2,1,0:T(8,128)(2,1)S(1)} %bitcast.10, f32[130,64,128]{2,1,0:T(8,128)S(1)} %near.1.refs_2_, s32[6,128]{1,0:T(8,128)S(1)} %get-tuple-element.22.refs_2_.refs_3_, s32[6,128]{1,0:T(8,128)S(1)} %get-tuple-element.23.refs_3_.refs_4_, ...), custom_call_target="tpu_custom_call" | custom-call | flops 2818572288 | bytes 4259840 | tf_op jit(solution)/shard_map/far/pallas_call | solution.py:391
Async XLA Ops:
  21.6 2.0 %collective-permute-start.1 = (bf16[1152,128]{1,0:T(8,128)(2,1)S(1)}, bf16[1152,128]{1,0:T(8,128)(2,1)S(1)}, u32[]{:S(2)}, u32[]{:S(2)}) collective-permute-start(bf16[1152,128]{1,0:T(8,128)(2,1)S(1)} %edges.1), channel_id=1, source_target_pairs={{0,1},{1,0},{2,3},{3,2},{4,5},{5,4},{6,7},{7,6},{8,9},{9,8},{10,11... | collective-permute-start | bytes 884744 | tf_op jit(solution)/shard_map/ppermute | solution.py:344
  21.7 9.6 %collective-permute-start = (bf16[1152,128]{1,0:T(8,128)(2,1)S(1)}, bf16[1152,128]{1,0:T(8,128)(2,1)S(1)}, u32[]{:S(2)}, u32[]{:S(2)}) collective-permute-start(bf16[1152,128]{1,0:T(8,128)(2,1)S(1)} %edges.1), channel_id=1, source_target_pairs={{0,2},{1,3},{2,0},{3,1},{4,6},{5,7},{6,4},{7,5},{8,10},{9,11},{10,... | collective-permute-start | bytes 884744 | tf_op jit(solution)/shard_map/ppermute | solution.py:344
  31.3 1.6 %collective-permute-start.2 = (bf16[1152,128]{1,0:T(8,128)(2,1)S(1)}, bf16[1152,128]{1,0:T(8,128)(2,1)S(1)}, u32[]{:S(2)}, u32[]{:S(2)}) collective-permute-start(bf16[1152,128]{1,0:T(8,128)(2,1)S(1)} %collective-permute-done), channel_id=1, source_target_pairs={{0,1},{1,0},{2,3},{3,2},{4,5},{5,4},{6,7},{7,6},{8,9},{9,8},{10,11... | collective-permute-start | bytes 884744 | tf_op jit(solution)/shard_map/ppermute | solution.py:344

commit v11 on v10

--- a/solution.py
+++ b/solution.py
@@ -14,6 +14,7 @@
 LIMIT = 32 * 2**20
 SEND = 16
 AHEAD = 8
+PIECES = 4
 
 
 def round_up(value, step):
@@ -269,20 +270,22 @@
             combine(i + h, y[:, h * side : (h + 1) * side])
         if last and (i + 2) % SEND == 0:
             rows = pl.ds(i + 2 - SEND, SEND)
-            for o in range(outs):
-                staged[o, rows, :] = spread[pl.ds(o, SEND, stride=outs + 1), :].astype(BF16)
-            sent.append(
-                pltpu.make_async_copy(staged.at[:, rows, :], out_ref.at[:, rows, :], out_sems.at[(i + 2) // SEND - 1])
-            )
-            sent[-1].start()
+            step = outs // PIECES if i + 2 == side else outs
+            for begin in range(0, outs, step):
+                for o in range(begin, begin + step):
+                    staged[o, rows, :] = spread[pl.ds(o, SEND, stride=outs + 1), :].astype(BF16)
+                some = pl.ds(begin, step)
+                sent.append(
+                    pltpu.make_async_copy(staged.at[some, rows, :], out_ref.at[some, rows, :], out_sems.at[len(sent)])
+                )
+                sent[-1].start()
 
     for r in range(AHEAD + 1):
         place(r)
     for i in range(0, side, 2):
-        y = multiply(i)
         for r in range(i + AHEAD + 1, min(i + AHEAD + 3, side)):
             place(r)
-        finish(i, y)
+        finish(i, multiply(i))
     for copy in sent:
         copy.wait()
 
@@ -397,7 +400,7 @@
         + [
             pltpu.VMEM((round_up(SEND * (outs + 1), 8), side), F32),
             pltpu.VMEM((outs, side, side), BF16),
-            pltpu.SemaphoreType.DMA((side // SEND,)),
+            pltpu.SemaphoreType.DMA((side // SEND + PIECES - 1,)),
             pltpu.SemaphoreType.DMA((2,)),
         ],
         compiler_params=params,

time: 42.4 us -> 42.2 us (level)
  Pallas kernels: 21.8 us -> 21.3 us
where the time goes in v11:
time: 42.2 us; the launch traced here: 41.8 us
  Pallas kernels  21.3 us (50%)
  blocking collectives  17 us (40%)
  starting transfers between devices  1.86 us (4%)
  waiting for transfers between devices  1.42 us (3%)
    all_gather x1, blocking collectives, body(): gathered = lax.all_gather(packed, 'tile', axis=1, tiled=True)  17 us
    pallas_call x1, Pallas kernels, body(): pl.pallas_call(functools.partial(tile_kernel, dims, True, many), out_shap...  9.08 us
    pallas_call x1, Pallas kernels, body(): pl.pallas_call(functools.partial(tile_kernel, dims, False, many), out_sha...  7.13 us
    pallas_call x1, Pallas kernels, body(): pl.pallas_call(functools.partial(edge_kernel, (side, chans, blocks, tiles...  2.76 us
    ppermute x3, starting transfers between devices, swap(): return lax.ppermute(value, 'chan', [(i, i ^ flip) for i in range(parts)])  1.86 us
    pallas_call x1, Pallas kernels, body(): pl.pallas_call(pack_kernel, out_shape=[jax.ShapeDtypeStruct((blocks * cha...  1.62 us
    ppermute x3, waiting for transfers between devices, swap(): return lax.ppermute(value, 'chan', [(i, i ^ flip) for i in range(parts)])  1.42 us
  transfers between devices with their start and end apart: 3, of which 1 were waited for; matrix products, arithmetic and copies ran while one was open for 0% of the time, Pallas kernels for 19%

profile of v11, /device:TPU:0, one launch (start us, length us, event | category | flops | bytes accessed | tf_op | source)
XLA Modules:
  0.0 41.8 jit_solution(5926800196660765008)
XLA Ops:
  0.0 1.6 %pack.1 = (bf16[528,128]{1,0:T(8,128)(2,1)S(1)}, s32[6,128]{1,0:T(8,128)S(1)}, s32[6,128]{1,0:T(8,128)S(1)}, bf16[32,128,128]{2,1,0:T(8,128)(2,1)S(1)}, bf16[3,3,64,128]{3,2,1,0:T(8,128)(2,1)S(1)}) custom-call(s32[6,128]{1,0:T(8,128)} %bitcast.12, s32[6,128]{1,0:T(8,128)} %bitcast.13, s32[1,4,8]{2,1,0:T(4,128)} %lists_hbm.1, s32[1,4]{1,0:T(1,128)} %neigh_hbm.1, ...), custom_call_target="tpu_custom_call" | custom-call | tf_op jit(solution)/shard_map/pack/pallas_call | solution.py:306
  1.6 17.0 %all_gather.3.gathered_ref = bf16[528,512]{1,0:T(8,128)(2,1)S(1)} all-gather(bf16[528,128]{1,0:T(8,128)(2,1)S(1)} %get-tuple-element.17), channel_id=1, replica_groups=mesh['group'=2,'tile'=4,'chan'=4] {'tile'}, dimensions={1}, use_global_device_ids=true | all-gather | bytes 675840 | tf_op jit(solution)/shard_map/all_gather | solution.py:329
  18.6 2.8 %edges.1 = bf16[1152,128]{1,0:T(8,128)(2,1)S(1)} custom-call(bf16[528,512]{1,0:T(8,128)(2,1)S(1)} %all_gather.3.gathered_ref, bf16[32,128,128]{2,1,0:T(8,128)(2,1)S(1)} %get-tuple-element.18.table_ref.refs_4_.refs_5_), custom_call_target="tpu_custom_call" | custom-call | tf_op jit(solution)/shard_map/edges/pallas_call | solution.py:330
  21.4 0.1 collective-permute-start.1
  21.5 1.6 %collective-permute-start = (bf16[1152,128]{1,0:T(8,128)(2,1)S(1)}, bf16[1152,128]{1,0:T(8,128)(2,1)S(1)}, u32[]{:S(2)}, u32[]{:S(2)}) collective-permute-start(bf16[1152,128]{1,0:T(8,128)(2,1)S(1)} %edges.1), channel_id=1, source_target_pairs={{0,2},{1,3},{2,0},{3,1},{4,6},{5,7},{6,4},{7,5},{8,10},{9,11},{10,... | collective-permute-start | bytes 884744 | tf_op jit(solution)/shard_map/ppermute | solution.py:347
  23.0 0.4 filters.2.refs_5_
  23.4 0.0 collective-permute-done.1
  23.4 7.1 %near.1.refs_2_ = f32[130,64,128]{2,1,0:T(8,128)S(1)} custom-call(bf16[36,32,128]{2,1,0:T(8,128)(2,1)S(1)} %bitcast.7, bf16[36,32,128]{2,1,0:T(8,128)(2,1)S(1)} %bitcast.9, s32[6,128]{1,0:T(8,128)S(1)} %get-tuple-element.22.refs_2_.refs_3_, s32[6,128]{1,0:T(8,128)S(1)} %get-tuple-element.23.refs_3_.refs_4_, ...), custom_call_target="tpu_custom_call" | custom-call | flops 2818572288 | bytes 4259840 | tf_op jit(solution)/shard_map/near/pallas_call | solution.py:380
  30.5 0.3 filters.3.refs_6_
  30.9 0.0 collective-permute-done
  30.9 0.2 collective-permute-start.2
  31.1 1.4 %collective-permute-done.2 = bf16[1152,128]{1,0:T(8,128)(2,1)S(1)} collective-permute-done((bf16[1152,128]{1,0:T(8,128)(2,1)S(1)}, bf16[1152,128]{1,0:T(8,128)(2,1)S(1)}, u32[]{:S(2)}, u32[]{:S(2)}) %collective-permute-start.2) | collective-permute-done | bytes 294944 | tf_op jit(solution)/shard_map/ppermute | solution.py:347
  32.6 9.1 %far.1 = bf16[64,128,128]{2,1,0:T(8,128)(2,1)} custom-call(bf16[36,32,128]{2,1,0:T(8,128)(2,1)S(1)} %bitcast.8, bf16[36,32,128]{2,1,0:T(8,128)(2,1)S(1)} %bitcast.10, f32[130,64,128]{2,1,0:T(8,128)S(1)} %near.1.refs_2_, s32[6,128]{1,0:T(8,128)S(1)} %get-tuple-element.22.refs_2_.refs_3_, s32[6,128]{1,0:T(8,128)S(1)} %get-tuple-element.23.refs_3_.refs_4_, ...), custom_call_target="tpu_custom_call" | custom-call | flops 2818572288 | bytes 4259840 | tf_op jit(solution)/shard_map/far/pallas_call | solution.py:394
Async XLA Ops:
  21.4 2.0 %collective-permute-start.1 = (bf16[1152,128]{1,0:T(8,128)(2,1)S(1)}, bf16[1152,128]{1,0:T(8,128)(2,1)S(1)}, u32[]{:S(2)}, u32[]{:S(2)}) collective-permute-start(bf16[1152,128]{1,0:T(8,128)(2,1)S(1)} %edges.1), channel_id=1, source_target_pairs={{0,1},{1,0},{2,3},{3,2},{4,5},{5,4},{6,7},{7,6},{8,9},{9,8},{10,11... | collective-permute-start | bytes 884744 | tf_op jit(solution)/shard_map/ppermute | solution.py:347
  21.5 9.4 %collective-permute-start = (bf16[1152,128]{1,0:T(8,128)(2,1)S(1)}, bf16[1152,128]{1,0:T(8,128)(2,1)S(1)}, u32[]{:S(2)}, u32[]{:S(2)}) collective-permute-start(bf16[1152,128]{1,0:T(8,128)(2,1)S(1)} %edges.1), channel_id=1, source_target_pairs={{0,2},{1,3},{2,0},{3,1},{4,6},{5,7},{6,4},{7,5},{8,10},{9,11},{10,... | collective-permute-start | bytes 884744 | tf_op jit(solution)/shard_map/ppermute | solution.py:347
  30.9 1.6 %collective-permute-start.2 = (bf16[1152,128]{1,0:T(8,128)(2,1)S(1)}, bf16[1152,128]{1,0:T(8,128)(2,1)S(1)}, u32[]{:S(2)}, u32[]{:S(2)}) collective-permute-start(bf16[1152,128]{1,0:T(8,128)(2,1)S(1)} %collective-permute-done), channel_id=1, source_target_pairs={{0,1},{1,0},{2,3},{3,2},{4,5},{5,4},{6,7},{7,6},{8,9},{9,8},{10,11... | collective-permute-start | bytes 884744 | tf_op jit(solution)/shard_map/ppermute | solution.py:347

commit v12 on v11

--- a/solution.py
+++ b/solution.py
@@ -387,10 +387,9 @@
         cost_estimate=cost,
         name="near",
     )(*near, slots, weights, table, near_filters)
-    filters, so_far = lax.optimization_barrier((filters, so_far))
+    across, filters, so_far = lax.optimization_barrier((across, filters, so_far))
+    far = spread({many: across}, many // 2)
     far_filters = matrix(True, filters)
-    across, so_far, far_filters = lax.optimization_barrier((across, so_far, far_filters))
-    far = spread({many: across}, many // 2)
     return pl.pallas_call(
         functools.partial(tile_kernel, dims, True, many),
         out_shape=jax.ShapeDtypeStruct((outs, side, side), BF16),

time: 42.2 us -> 42.1 us (level)
  transfers between devices with their start and end apart: 3 -> 3, of which waited for: 1 -> 2; matrix products, arithmetic and copies ran while one was open for 0% -> 0% of each run, Pallas kernels for 19% -> 19%
where the time goes in v12:
time: 42.1 us; the launch traced here: 41.7 us
  Pallas kernels  21.2 us (50%)
  blocking collectives  17 us (40%)
  starting transfers between devices  1.63 us (4%)
  waiting for transfers between devices  1.6 us (4%)
    all_gather x1, blocking collectives, body(): gathered = lax.all_gather(packed, 'tile', axis=1, tiled=True)  17 us
    pallas_call x1, Pallas kernels, body(): pl.pallas_call(functools.partial(tile_kernel, dims, True, many), out_shap...  9.05 us
    pallas_call x1, Pallas kernels, body(): pl.pallas_call(functools.partial(tile_kernel, dims, False, many), out_sha...  7.11 us
    pallas_call x1, Pallas kernels, body(): pl.pallas_call(functools.partial(edge_kernel, (side, chans, blocks, tiles...  2.76 us
    ppermute x3, starting transfers between devices, swap(): return lax.ppermute(value, 'chan', [(i, i ^ flip) for i in range(parts)])  1.63 us
    pallas_call x1, Pallas kernels, body(): pl.pallas_call(pack_kernel, out_shape=[jax.ShapeDtypeStruct((blocks * cha...  1.62 us
    ppermute x3, waiting for transfers between devices, swap(): return lax.ppermute(value, 'chan', [(i, i ^ flip) for i in range(parts)])  1.6 us
  transfers between devices with their start and end apart: 3, of which 2 were waited for; matrix products, arithmetic and copies ran while one was open for 0% of the time, Pallas kernels for 19%

profile of v12, /device:TPU:0, one launch (start us, length us, event | category | flops | bytes accessed | tf_op | source)
XLA Modules:
  0.0 41.7 jit_solution(10314087511007715960)
XLA Ops:
  0.0 1.6 %pack.1 = (bf16[528,128]{1,0:T(8,128)(2,1)S(1)}, s32[6,128]{1,0:T(8,128)S(1)}, s32[6,128]{1,0:T(8,128)S(1)}, bf16[32,128,128]{2,1,0:T(8,128)(2,1)S(1)}, bf16[3,3,64,128]{3,2,1,0:T(8,128)(2,1)S(1)}) custom-call(s32[6,128]{1,0:T(8,128)} %bitcast.12, s32[6,128]{1,0:T(8,128)} %bitcast.13, s32[1,4,8]{2,1,0:T(4,128)} %lists_hbm.1, s32[1,4]{1,0:T(1,128)} %neigh_hbm.1, ...), custom_call_target="tpu_custom_call" | custom-call | tf_op jit(solution)/shard_map/pack/pallas_call | solution.py:306
  1.6 17.0 %all_gather.3.gathered_ref = bf16[528,512]{1,0:T(8,128)(2,1)S(1)} all-gather(bf16[528,128]{1,0:T(8,128)(2,1)S(1)} %get-tuple-element.15), channel_id=1, replica_groups=mesh['group'=2,'tile'=4,'chan'=4] {'tile'}, dimensions={1}, use_global_device_ids=true | all-gather | bytes 675840 | tf_op jit(solution)/shard_map/all_gather | solution.py:329
  18.6 2.8 %edges.1 = bf16[1152,128]{1,0:T(8,128)(2,1)S(1)} custom-call(bf16[528,512]{1,0:T(8,128)(2,1)S(1)} %all_gather.3.gathered_ref, bf16[32,128,128]{2,1,0:T(8,128)(2,1)S(1)} %get-tuple-element.16.table_ref.refs_4_.refs_5_), custom_call_target="tpu_custom_call" | custom-call | tf_op jit(solution)/shard_map/edges/pallas_call | solution.py:330
  21.4 0.1 collective-permute-start.1
  21.5 1.6 %collective-permute-start = (bf16[1152,128]{1,0:T(8,128)(2,1)S(1)}, bf16[1152,128]{1,0:T(8,128)(2,1)S(1)}, u32[]{:S(2)}, u32[]{:S(2)}) collective-permute-start(bf16[1152,128]{1,0:T(8,128)(2,1)S(1)} %edges.1), channel_id=1, source_target_pairs={{0,2},{1,3},{2,0},{3,1},{4,6},{5,7},{6,4},{7,5},{8,10},{9,11},{10,... | collective-permute-start | bytes 884744 | tf_op jit(solution)/shard_map/ppermute | solution.py:347
  23.0 0.4 filters.2.refs_5_
  23.4 0.0 collective-permute-done.1
  23.4 7.1 %near.1.refs_2_ = f32[130,64,128]{2,1,0:T(8,128)S(1)} custom-call(bf16[36,32,128]{2,1,0:T(8,128)(2,1)S(1)} %bitcast.7, bf16[36,32,128]{2,1,0:T(8,128)(2,1)S(1)} %bitcast.10, s32[6,128]{1,0:T(8,128)S(1)} %get-tuple-element.20.refs_2_.refs_3_, s32[6,128]{1,0:T(8,128)S(1)} %get-tuple-element.21.refs_3_.refs_4_, ...), custom_call_target="tpu_custom_call" | custom-call | flops 2818572288 | bytes 4259840 | tf_op jit(solution)/shard_map/near/pallas_call | solution.py:380
  30.5 0.4 collective-permute-done
  30.9 0.0 collective-permute-start.2
  30.9 0.3 filters.3.refs_6_
  31.3 1.2 %collective-permute-done.2 = bf16[1152,128]{1,0:T(8,128)(2,1)S(1)} collective-permute-done((bf16[1152,128]{1,0:T(8,128)(2,1)S(1)}, bf16[1152,128]{1,0:T(8,128)(2,1)S(1)}, u32[]{:S(2)}, u32[]{:S(2)}) %collective-permute-start.2) | collective-permute-done | bytes 294944 | tf_op jit(solution)/shard_map/ppermute | solution.py:347
  32.5 9.1 %far.1 = bf16[64,128,128]{2,1,0:T(8,128)(2,1)} custom-call(bf16[36,32,128]{2,1,0:T(8,128)(2,1)S(1)} %bitcast.8, bf16[36,32,128]{2,1,0:T(8,128)(2,1)S(1)} %bitcast.9, f32[130,64,128]{2,1,0:T(8,128)S(1)} %near.1.refs_2_, s32[6,128]{1,0:T(8,128)S(1)} %get-tuple-element.20.refs_2_.refs_3_, s32[6,128]{1,0:T(8,128)S(1)} %get-tuple-element.21.refs_3_.refs_4_, ...), custom_call_target="tpu_custom_call" | custom-call | flops 2818572288 | bytes 4259840 | tf_op jit(solution)/shard_map/far/pallas_call | solution.py:393
Async XLA Ops:
  21.4 2.0 %collective-permute-start.1 = (bf16[1152,128]{1,0:T(8,128)(2,1)S(1)}, bf16[1152,128]{1,0:T(8,128)(2,1)S(1)}, u32[]{:S(2)}, u32[]{:S(2)}) collective-permute-start(bf16[1152,128]{1,0:T(8,128)(2,1)S(1)} %edges.1), channel_id=1, source_target_pairs={{0,1},{1,0},{2,3},{3,2},{4,5},{5,4},{6,7},{7,6},{8,9},{9,8},{10,11... | collective-permute-start | bytes 884744 | tf_op jit(solution)/shard_map/ppermute | solution.py:347
  21.5 9.4 %collective-permute-start = (bf16[1152,128]{1,0:T(8,128)(2,1)S(1)}, bf16[1152,128]{1,0:T(8,128)(2,1)S(1)}, u32[]{:S(2)}, u32[]{:S(2)}) collective-permute-start(bf16[1152,128]{1,0:T(8,128)(2,1)S(1)} %edges.1), channel_id=1, source_target_pairs={{0,2},{1,3},{2,0},{3,1},{4,6},{5,7},{6,4},{7,5},{8,10},{9,11},{10,... | collective-permute-start | bytes 884744 | tf_op jit(solution)/shard_map/ppermute | solution.py:347
  30.9 1.6 %collective-permute-start.2 = (bf16[1152,128]{1,0:T(8,128)(2,1)S(1)}, bf16[1152,128]{1,0:T(8,128)(2,1)S(1)}, u32[]{:S(2)}, u32[]{:S(2)}) collective-permute-start(bf16[1152,128]{1,0:T(8,128)(2,1)S(1)} %collective-permute-done), channel_id=1, source_target_pairs={{0,1},{1,0},{2,3},{3,2},{4,5},{5,4},{6,7},{7,6},{8,9},{9,8},{10,11... | collective-permute-start | bytes 884744 | tf_op jit(solution)/shard_map/ppermute | solution.py:347

commit v13 on v12

--- a/solution.py
+++ b/solution.py
@@ -105,7 +105,10 @@
     for kind in range(kinds):
         moved = pltpu.roll(table_ref[kind].astype(F32), per_group * kind + 1, 1)
         total = jnp.where(lane // per_group == kind, moved, total)
-    columns[...] = total
+    for n, moved in enumerate([pltpu.roll(total, side - 1, 1), total]):
+        moved = jnp.where(lane % per_group == 0, moved, 0.0)
+        for m in range(per_group):
+            columns[n, m * side : (m + 1) * side, :] = (moved if m == 0 else pltpu.roll(moved, m, 1)).astype(BF16)
     lists_copy.wait()
     own_row = me * tiles
     neigh = [scalars[own_row, cap + s] for s in range(4)]
@@ -128,13 +131,7 @@
             for slot in range(count):
                 group, member = slot // per_group, slot % per_group
                 picked[group * chans : (group + 1) * chans, member * side : (member + 1) * side] = block_of(owner, slot)
-            col = columns[...]
-            col = jnp.where(edge == 2, pltpu.roll(col, side - 1, 1), col)
-            col = jnp.where(lane % per_group == 0, col, 0.0)
-            spread = jnp.concatenate(
-                [col if m == 0 else pltpu.roll(col, m, 1) for m in range(per_group)], axis=0
-            ).astype(BF16)
-            z = dot(picked[...], spread)
+            z = dot(picked[...], columns[edge - 2])
             z_hi = z.astype(BF16)
             z_lo = (z - z_hi.astype(F32)).astype(BF16)
             first = start + owner * rows + jnp.where(codes[s] >= 4, tiles * rows, 0)
@@ -336,7 +333,7 @@
             pltpu.VMEM((tiles * (tiles + 2 * taps + 2 * rows), side), jnp.int32),
             pltpu.SMEM((tiles * (tiles + 2 * taps), side), jnp.int32),
             pltpu.VMEM((count * kinds // side * chans, side * side // kinds), BF16),
-            pltpu.VMEM((side, side), F32),
+            pltpu.VMEM((2, side // kinds * side, side), BF16),
             pltpu.SemaphoreType.DMA((2,)),
         ],
         compiler_params=params,

time: 42.1 us -> 41.9 us (level)
  no operation moved by 1% of the time
where the time goes in v13:
time: 41.9 us; the launch traced here: 41.5 us
  Pallas kernels  21.1 us (50%)
  blocking collectives  17 us (41%)
  starting transfers between devices  1.63 us (4%)
  waiting for transfers between devices  1.59 us (4%)
    all_gather x1, blocking collectives, body(): gathered = lax.all_gather(packed, 'tile', axis=1, tiled=True)  17 us
    pallas_call x1, Pallas kernels, body(): pl.pallas_call(functools.partial(tile_kernel, dims, True, many), out_shap...  9.08 us
    pallas_call x1, Pallas kernels, body(): pl.pallas_call(functools.partial(tile_kernel, dims, False, many), out_sha...  7.11 us
    pallas_call x1, Pallas kernels, body(): pl.pallas_call(functools.partial(edge_kernel, (side, chans, blocks, tiles...  2.56 us
    ppermute x3, starting transfers between devices, swap(): return lax.ppermute(value, 'chan', [(i, i ^ flip) for i in range(parts)])  1.63 us
    pallas_call x1, Pallas kernels, body(): pl.pallas_call(pack_kernel, out_shape=[jax.ShapeDtypeStruct((blocks * cha...  1.62 us
    ppermute x3, waiting for transfers between devices, swap(): return lax.ppermute(value, 'chan', [(i, i ^ flip) for i in range(parts)])  1.59 us
  transfers between devices with their start and end apart: 3, of which 2 were waited for; matrix products, arithmetic and copies ran while one was open for 0% of the time, Pallas kernels for 19%

profile of v13, /device:TPU:0, one launch (start us, length us, event | category | flops | bytes accessed | tf_op | source)
XLA Modules:
  0.0 41.5 jit_solution(7034157879279376321)
XLA Ops:
  0.0 1.6 %pack.1 = (bf16[528,128]{1,0:T(8,128)(2,1)S(1)}, s32[6,128]{1,0:T(8,128)S(1)}, s32[6,128]{1,0:T(8,128)S(1)}, bf16[32,128,128]{2,1,0:T(8,128)(2,1)S(1)}, bf16[3,3,64,128]{3,2,1,0:T(8,128)(2,1)S(1)}) custom-call(s32[6,128]{1,0:T(8,128)} %bitcast.12, s32[6,128]{1,0:T(8,128)} %bitcast.13, s32[1,4,8]{2,1,0:T(4,128)} %lists_hbm.1, s32[1,4]{1,0:T(1,128)} %neigh_hbm.1, ...), custom_call_target="tpu_custom_call" | custom-call | tf_op jit(solution)/shard_map/pack/pallas_call | solution.py:303
  1.6 17.0 %all_gather.3.gathered_ref = bf16[528,512]{1,0:T(8,128)(2,1)S(1)} all-gather(bf16[528,128]{1,0:T(8,128)(2,1)S(1)} %get-tuple-element.15), channel_id=1, replica_groups=mesh['group'=2,'tile'=4,'chan'=4] {'tile'}, dimensions={1}, use_global_device_ids=true | all-gather | bytes 675840 | tf_op jit(solution)/shard_map/all_gather | solution.py:326
  18.6 2.6 %edges.1 = bf16[1152,128]{1,0:T(8,128)(2,1)S(1)} custom-call(bf16[528,512]{1,0:T(8,128)(2,1)S(1)} %all_gather.3.gathered_ref, bf16[32,128,128]{2,1,0:T(8,128)(2,1)S(1)} %get-tuple-element.16.table_ref.refs_4_.refs_5_), custom_call_target="tpu_custom_call" | custom-call | tf_op jit(solution)/shard_map/edges/pallas_call | solution.py:327
  21.2 0.1 collective-permute-start.1
  21.3 1.6 %collective-permute-start = (bf16[1152,128]{1,0:T(8,128)(2,1)S(1)}, bf16[1152,128]{1,0:T(8,128)(2,1)S(1)}, u32[]{:S(2)}, u32[]{:S(2)}) collective-permute-start(bf16[1152,128]{1,0:T(8,128)(2,1)S(1)} %edges.1), channel_id=1, source_target_pairs={{0,2},{1,3},{2,0},{3,1},{4,6},{5,7},{6,4},{7,5},{8,10},{9,11},{10,... | collective-permute-start | bytes 884744 | tf_op jit(solution)/shard_map/ppermute | solution.py:344
  22.8 0.4 filters.2.refs_5_
  23.2 0.0 collective-permute-done.1
  23.2 7.1 %near.1.refs_2_ = f32[130,64,128]{2,1,0:T(8,128)S(1)} custom-call(bf16[36,32,128]{2,1,0:T(8,128)(2,1)S(1)} %bitcast.7, bf16[36,32,128]{2,1,0:T(8,128)(2,1)S(1)} %bitcast.10, s32[6,128]{1,0:T(8,128)S(1)} %get-tuple-element.20.refs_2_.refs_3_, s32[6,128]{1,0:T(8,128)S(1)} %get-tuple-element.21.refs_3_.refs_4_, ...), custom_call_target="tpu_custom_call" | custom-call | flops 2818572288 | bytes 4259840 | tf_op jit(solution)/shard_map/near/pallas_call | solution.py:377
  30.3 0.4 collective-permute-done
  30.7 0.0 collective-permute-start.2
  30.7 0.3 filters.3.refs_6_
  31.1 1.2 %collective-permute-done.2 = bf16[1152,128]{1,0:T(8,128)(2,1)S(1)} collective-permute-done((bf16[1152,128]{1,0:T(8,128)(2,1)S(1)}, bf16[1152,128]{1,0:T(8,128)(2,1)S(1)}, u32[]{:S(2)}, u32[]{:S(2)}) %collective-permute-start.2) | collective-permute-done | bytes 294944 | tf_op jit(solution)/shard_map/ppermute | solution.py:344
  32.3 9.1 %far.1 = bf16[64,128,128]{2,1,0:T(8,128)(2,1)} custom-call(bf16[36,32,128]{2,1,0:T(8,128)(2,1)S(1)} %bitcast.8, bf16[36,32,128]{2,1,0:T(8,128)(2,1)S(1)} %bitcast.9, f32[130,64,128]{2,1,0:T(8,128)S(1)} %near.1.refs_2_, s32[6,128]{1,0:T(8,128)S(1)} %get-tuple-element.20.refs_2_.refs_3_, s32[6,128]{1,0:T(8,128)S(1)} %get-tuple-element.21.refs_3_.refs_4_, ...), custom_call_target="tpu_custom_call" | custom-call | flops 2818572288 | bytes 4259840 | tf_op jit(solution)/shard_map/far/pallas_call | solution.py:390
Async XLA Ops:
  21.2 2.0 %collective-permute-start.1 = (bf16[1152,128]{1,0:T(8,128)(2,1)S(1)}, bf16[1152,128]{1,0:T(8,128)(2,1)S(1)}, u32[]{:S(2)}, u32[]{:S(2)}) collective-permute-start(bf16[1152,128]{1,0:T(8,128)(2,1)S(1)} %edges.1), channel_id=1, source_target_pairs={{0,1},{1,0},{2,3},{3,2},{4,5},{5,4},{6,7},{7,6},{8,9},{9,8},{10,11... | collective-permute-start | bytes 884744 | tf_op jit(solution)/shard_map/ppermute | solution.py:344
  21.3 9.4 %collective-permute-start = (bf16[1152,128]{1,0:T(8,128)(2,1)S(1)}, bf16[1152,128]{1,0:T(8,128)(2,1)S(1)}, u32[]{:S(2)}, u32[]{:S(2)}) collective-permute-start(bf16[1152,128]{1,0:T(8,128)(2,1)S(1)} %edges.1), channel_id=1, source_target_pairs={{0,2},{1,3},{2,0},{3,1},{4,6},{5,7},{6,4},{7,5},{8,10},{9,11},{10,... | collective-permute-start | bytes 884744 | tf_op jit(solution)/shard_map/ppermute | solution.py:344
  30.7 1.6 %collective-permute-start.2 = (bf16[1152,128]{1,0:T(8,128)(2,1)S(1)}, bf16[1152,128]{1,0:T(8,128)(2,1)S(1)}, u32[]{:S(2)}, u32[]{:S(2)}) collective-permute-start(bf16[1152,128]{1,0:T(8,128)(2,1)S(1)} %collective-permute-done), channel_id=1, source_target_pairs={{0,1},{1,0},{2,3},{3,2},{4,5},{5,4},{6,7},{7,6},{8,9},{9,8},{10,11... | collective-permute-start | bytes 884744 | tf_op jit(solution)/shard_map/ppermute | solution.py:344

commit v14 on v13

--- a/solution.py
+++ b/solution.py
@@ -203,11 +203,14 @@
     if last:
         spread, staged, out_sems, sems = refs
     else:
-        (sems,) = refs
+        filters = matrix
+        matrix, sems = refs
     taps = slots.shape[0]
     count = tiles * cap
     half = chans * many
     copies = start_all(sems, [(slots_ref, slots), (weights_ref, weights)])
+    if not last:
+        filter_kernel(chans, False, filters, matrix)
 
     def channels(index):
         return jnp.concatenate([part[index] for part in parts], axis=0)
@@ -364,7 +367,6 @@
             name="filters",
         )(filters)
 
-    near_filters = matrix(False, filters)
     across = swap(mine, many)
     dims = (side, chans, cap, tiles, all_chans, outs)
     scratch = [
@@ -379,11 +381,11 @@
         out_shape=jax.ShapeDtypeStruct((side + 2, outs, side), F32),
         in_specs=[VMEM] * (many + 4),
         out_specs=VMEM,
-        scratch_shapes=scratch + [pltpu.SemaphoreType.DMA((2,))],
+        scratch_shapes=scratch + [pltpu.VMEM((3 * outs, 3 * half), BF16), pltpu.SemaphoreType.DMA((2,))],
         compiler_params=params,
         cost_estimate=cost,
         name="near",
-    )(*near, slots, weights, table, near_filters)
+    )(*near, slots, weights, table, filters)
     across, filters, so_far = lax.optimization_barrier((across, filters, so_far))
     far = spread({many: across}, many // 2)
     far_filters = matrix(True, filters)

time: 41.9 us -> 42 us (level)
  no operation moved by 1% of the time
where the time goes in v14:
time: 42 us; the launch traced here: 41.8 us
  Pallas kernels  21.3 us (51%)
  blocking collectives  17 us (40%)
  waiting for transfers between devices  1.66 us (4%)
  starting transfers between devices  1.63 us (4%)
    all_gather x1, blocking collectives, body(): gathered = lax.all_gather(packed, 'tile', axis=1, tiled=True)  17 us
    pallas_call x1, Pallas kernels, body(): pl.pallas_call(functools.partial(tile_kernel, dims, True, many), out_shap...  9.07 us
    pallas_call x1, Pallas kernels, body(): pl.pallas_call(functools.partial(tile_kernel, dims, False, many), out_sha...  7.43 us
    pallas_call x1, Pallas kernels, body(): pl.pallas_call(functools.partial(edge_kernel, (side, chans, blocks, tiles...  2.86 us
    ppermute x3, waiting for transfers between devices, swap(): return lax.ppermute(value, 'chan', [(i, i ^ flip) for i in range(parts)])  1.66 us
    ppermute x3, starting transfers between devices, swap(): return lax.ppermute(value, 'chan', [(i, i ^ flip) for i in range(parts)])  1.63 us
    pallas_call x1, Pallas kernels, body(): pl.pallas_call(pack_kernel, out_shape=[jax.ShapeDtypeStruct((blocks * cha...  1.62 us
  transfers between devices with their start and end apart: 3, of which 2 were waited for; matrix products, arithmetic and copies ran while one was open for 0% of the time, Pallas kernels for 19%

profile of v14, /device:TPU:0, one launch (start us, length us, event | category | flops | bytes accessed | tf_op | source)
XLA Modules:
  0.0 41.8 jit_solution(9867166474897514803)
XLA Ops:
  0.0 1.6 %pack.1 = (bf16[528,128]{1,0:T(8,128)(2,1)S(1)}, s32[6,128]{1,0:T(8,128)S(1)}, s32[6,128]{1,0:T(8,128)S(1)}, bf16[32,128,128]{2,1,0:T(8,128)(2,1)S(1)}, bf16[3,3,64,128]{3,2,1,0:T(8,128)(2,1)S(1)}) custom-call(s32[6,128]{1,0:T(8,128)} %bitcast.12, s32[6,128]{1,0:T(8,128)} %bitcast.13, s32[1,4,8]{2,1,0:T(4,128)} %lists_hbm.1, s32[1,4]{1,0:T(1,128)} %neigh_hbm.1, ...), custom_call_target="tpu_custom_call" | custom-call | tf_op jit(solution)/shard_map/pack/pallas_call | solution.py:306
  1.6 17.0 %all_gather.3.gathered_ref = bf16[528,512]{1,0:T(8,128)(2,1)S(1)} all-gather(bf16[528,128]{1,0:T(8,128)(2,1)S(1)} %get-tuple-element.15), channel_id=1, replica_groups=mesh['group'=2,'tile'=4,'chan'=4] {'tile'}, dimensions={1}, use_global_device_ids=true | all-gather | bytes 675840 | tf_op jit(solution)/shard_map/all_gather | solution.py:329
  18.6 2.9 %edges.1 = bf16[1152,128]{1,0:T(8,128)(2,1)S(1)} custom-call(bf16[528,512]{1,0:T(8,128)(2,1)S(1)} %all_gather.3.gathered_ref, bf16[32,128,128]{2,1,0:T(8,128)(2,1)S(1)} %get-tuple-element.16.table_ref.refs_4_.refs_5_), custom_call_target="tpu_custom_call" | custom-call | tf_op jit(solution)/shard_map/edges/pallas_call | solution.py:330
  21.5 0.1 collective-permute-start.1
  21.6 1.6 %collective-permute-start = (bf16[1152,128]{1,0:T(8,128)(2,1)S(1)}, bf16[1152,128]{1,0:T(8,128)(2,1)S(1)}, u32[]{:S(2)}, u32[]{:S(2)}) collective-permute-start(bf16[1152,128]{1,0:T(8,128)(2,1)S(1)} %edges.1), channel_id=1, source_target_pairs={{0,2},{1,3},{2,0},{3,1},{4,6},{5,7},{6,4},{7,5},{8,10},{9,11},{10,... | collective-permute-start | bytes 884744 | tf_op jit(solution)/shard_map/ppermute | solution.py:347
  23.1 0.0 collective-permute-done.1
  23.1 7.4 %near.1.refs_2_ = f32[130,64,128]{2,1,0:T(8,128)S(1)} custom-call(bf16[36,32,128]{2,1,0:T(8,128)(2,1)S(1)} %bitcast.7, bf16[36,32,128]{2,1,0:T(8,128)(2,1)S(1)} %bitcast.10, s32[6,128]{1,0:T(8,128)S(1)} %get-tuple-element.20.refs_2_.refs_3_, s32[6,128]{1,0:T(8,128)S(1)} %get-tuple-element.21.refs_3_.refs_4_, ...), custom_call_target="tpu_custom_call" | custom-call | flops 2818572288 | bytes 4259840 | tf_op jit(solution)/shard_map/near/pallas_call | solution.py:379
  30.6 0.4 %collective-permute-done = bf16[1152,128]{1,0:T(8,128)(2,1)S(1)} collective-permute-done((bf16[1152,128]{1,0:T(8,128)(2,1)S(1)}, bf16[1152,128]{1,0:T(8,128)(2,1)S(1)}, u32[]{:S(2)}, u32[]{:S(2)}) %collective-permute-start) | collective-permute-done | bytes 294944 | tf_op jit(solution)/shard_map/ppermute | solution.py:347
  31.0 0.0 collective-permute-start.2
  31.0 0.3 filters.1.refs_6_
  31.4 1.2 %collective-permute-done.2 = bf16[1152,128]{1,0:T(8,128)(2,1)S(1)} collective-permute-done((bf16[1152,128]{1,0:T(8,128)(2,1)S(1)}, bf16[1152,128]{1,0:T(8,128)(2,1)S(1)}, u32[]{:S(2)}, u32[]{:S(2)}) %collective-permute-start.2) | collective-permute-done | bytes 294944 | tf_op jit(solution)/shard_map/ppermute | solution.py:347
  32.6 9.1 %far.1 = bf16[64,128,128]{2,1,0:T(8,128)(2,1)} custom-call(bf16[36,32,128]{2,1,0:T(8,128)(2,1)S(1)} %bitcast.8, bf16[36,32,128]{2,1,0:T(8,128)(2,1)S(1)} %bitcast.9, f32[130,64,128]{2,1,0:T(8,128)S(1)} %near.1.refs_2_, s32[6,128]{1,0:T(8,128)S(1)} %get-tuple-element.20.refs_2_.refs_3_, s32[6,128]{1,0:T(8,128)S(1)} %get-tuple-element.21.refs_3_.refs_4_, ...), custom_call_target="tpu_custom_call" | custom-call | flops 2818572288 | bytes 4259840 | tf_op jit(solution)/shard_map/far/pallas_call | solution.py:392
Async XLA Ops:
  21.5 1.6 %collective-permute-start.1 = (bf16[1152,128]{1,0:T(8,128)(2,1)S(1)}, bf16[1152,128]{1,0:T(8,128)(2,1)S(1)}, u32[]{:S(2)}, u32[]{:S(2)}) collective-permute-start(bf16[1152,128]{1,0:T(8,128)(2,1)S(1)} %edges.1), channel_id=1, source_target_pairs={{0,1},{1,0},{2,3},{3,2},{4,5},{5,4},{6,7},{7,6},{8,9},{9,8},{10,11... | collective-permute-start | bytes 884744 | tf_op jit(solution)/shard_map/ppermute | solution.py:347
  21.6 9.4 %collective-permute-start = (bf16[1152,128]{1,0:T(8,128)(2,1)S(1)}, bf16[1152,128]{1,0:T(8,128)(2,1)S(1)}, u32[]{:S(2)}, u32[]{:S(2)}) collective-permute-start(bf16[1152,128]{1,0:T(8,128)(2,1)S(1)} %edges.1), channel_id=1, source_target_pairs={{0,2},{1,3},{2,0},{3,1},{4,6},{5,7},{6,4},{7,5},{8,10},{9,11},{10,... | collective-permute-start | bytes 884744 | tf_op jit(solution)/shard_map/ppermute | solution.py:347
  31.0 1.6 %collective-permute-start.2 = (bf16[1152,128]{1,0:T(8,128)(2,1)S(1)}, bf16[1152,128]{1,0:T(8,128)(2,1)S(1)}, u32[]{:S(2)}, u32[]{:S(2)}) collective-permute-start(bf16[1152,128]{1,0:T(8,128)(2,1)S(1)} %collective-permute-done), channel_id=1, source_target_pairs={{0,1},{1,0},{2,3},{3,2},{4,5},{5,4},{6,7},{7,6},{8,9},{9,8},{10,11... | collective-permute-start | bytes 884744 | tf_op jit(solution)/shard_map/ppermute | solution.py:347
